TPU v7x, 32 devices: a whole 2x2x4 slice. The times are simulated.
32 devices in a mesh: fsdp: 16 (over z, y, core), tp: 2 (over x).
Axes of the slice: x: 2, y: 2, z: 4, core: 2. Of those that a mesh axis runs over, the one named last changes fastest.
Arguments:
- hidden: bfloat16 [16384, 2048], P(('fsdp', 'tp')), may hold values from -6 to 6
- cotangent: bfloat16 [16384, 2048], P(('fsdp', 'tp')), may hold values from -6 to 6
- prefix: int32 [16], P('fsdp'), may hold values from 102 to 512, as said below
- input_norm_gain: bfloat16 [2048], P('fsdp'), may hold values from 0.5 to 1.5
- z_weight: bfloat16 [2048, 4096], P('fsdp', 'tp'), may hold values from -0.125 to 0.125
- x_weight: bfloat16 [2048, 4096], P('fsdp', 'tp'), may hold values from -0.125 to 0.125
- bc_weight: bfloat16 [2048, 256], P('fsdp'), may hold values from -0.125 to 0.125
- dt_weight: bfloat16 [2048, 64], P('fsdp', 'tp'), may hold values from -0.125 to 0.125
- x_conv: bfloat16 [64, 4, 64], P('tp', None, 'fsdp'), may hold values from -3 to 3
- bc_conv: bfloat16 [4, 256], P(None, 'fsdp'), may hold values from -3 to 3
- log_decay: float32 [64], P('tp'), may hold values from 0 to 2.77
- dt_bias: float32 [64], P('tp'), may hold values from -4 to -1
- skip_gain: float32 [64], P('tp'), may hold values from 0.5 to 1.5
- gate_gain: bfloat16 [64, 64], P('tp', 'fsdp'), may hold values from 0.5 to 1.5
- out_weight: bfloat16 [4096, 2048], P('tp', 'fsdp'), may hold values from -0.09375 to 0.09375
Outputs:
- mixed: float32 [16384, 2048], P(('fsdp', 'tp'))
- grad_hidden: float32 [16384, 2048], P(('fsdp', 'tp'))
- grad_input_norm_gain: float32 [2048], P('fsdp')
- grad_z_weight: float32 [2048, 4096], P('fsdp', 'tp')
- grad_x_weight: float32 [2048, 4096], P('fsdp', 'tp')
- grad_bc_weight: float32 [2048, 256], P('fsdp')
- grad_dt_weight: float32 [2048, 64], P('fsdp', 'tp')
- grad_x_conv: float32 [64, 4, 64], P('tp', None, 'fsdp')
- grad_bc_conv: float32 [4, 256], P(None, 'fsdp')
- grad_log_decay: float32 [64], P('tp')
- grad_dt_bias: float32 [64], P('tp')
- grad_skip_gain: float32 [64], P('tp')
- grad_gate_gain: float32 [64, 64], P('tp', 'fsdp')
- grad_out_weight: float32 [4096, 2048], P('tp', 'fsdp')
Inputs may be any that keep to these rules, and one draw needn't show every extreme that they name: `prefix`: prefix length of each sequence; some sequence has the least and some the most.
All inputs are finite; a program needn't handle non-finite values.
Results may differ from a plain program's by a relative error of at most 0.0082.
Values may be sent and summed in bfloat16 or wider, within the bound.
No kernel may reach another device: no remote copies, remote signals or barrier semaphores. Data moves between devices by JAX's collectives and lax.ppermute only.
A program may use at most 384 MiB of HBM per device.

v0:
```python
import functools

import jax
import jax.numpy as jnp
from jax import lax
from jax.experimental import pallas as pl
from jax.experimental.pallas import tpu as pltpu
from jax.sharding import PartitionSpec as P

P_SIZE = 64
N = 128
Q = 128
HG = 8
CG = HG * P_SIZE
MAX_PREFIX = 512
EPSILON = 1e-05
F32 = jnp.float32
BF16 = jnp.bfloat16
NEG = -1e30
NN = ((1,), (0,))
NT = ((1,), (1,))
TN = ((0,), (0,))
MIB = 1024 * 1024
NO_COST = pl.CostEstimate(flops=0, bytes_accessed=0, transcendentals=0)


def dot(a, b, dims=NN):
    return lax.dot_general(a, b, (dims, ((), ())), preferred_element_type=F32)


def low(v):
    return v.astype(BF16)


def split_dot(v, e):
    hi = low(v)
    rest = low(v - hi.astype(F32))
    return dot(jnp.concatenate([hi, rest], axis=1), e)


def low_pair_dot(v, e):
    hi = low(v)
    return dot(hi, e) + dot(low(v - hi.astype(F32)), e)


def three_dot(e, v):
    hi = low(v)
    rest = v - hi.astype(F32)
    mid = low(rest)
    return dot(e, hi) + (dot(e, mid) + dot(e, low(rest - mid.astype(F32))))


def iota(shape, dim):
    return lax.broadcasted_iota(jnp.int32, shape, dim)


def sig(v):
    return 0.5 + 0.5 * jnp.tanh(0.5 * v)


def rows_of(c):
    return pl.ds(pl.multiple_of(c * Q, Q), Q)


def shifted_rows(x_ref, c, width=None):
    lanes = slice(0, width)
    cur = x_ref[rows_of(c), lanes].astype(F32)
    start = pl.multiple_of(jnp.maximum(c * Q - 16, 0), 16)
    before = x_ref[pl.ds(start, 16), lanes].astype(F32)[8:]
    before = jnp.where(c > 0, before, 0.0)
    both = jnp.concatenate([before, cur], axis=0)
    return [cur] + [pltpu.roll(both, j, 0)[8:] for j in (1, 2, 3)]


def conv_of(shifted, taps):
    total = taps[3:4] * shifted[0]
    for j in (1, 2, 3):
        total = total + taps[3 - j : 4 - j] * shifted[j]
    return total


def spread_matrix(start, width):
    return jnp.where(
        iota((256, width), 1) // P_SIZE + start == iota((256, width), 0) % 128, 1.0, 0.0
    ).astype(BF16)


def gather_matrix(start, width):
    return jnp.where(
        iota((width, 128), 0) // P_SIZE + start == iota((width, 128), 1), 1.0, 0.0
    ).astype(BF16)


def prep_kernel(rest_ref, taps_ref, decay_ref, bias_ref, act_ref, cols_ref, rows_ref):
    heads = decay_ref.shape[1]
    length = rest_ref.shape[0]
    taps = taps_ref[...]
    tri = jnp.where(iota((Q, Q), 0) >= iota((Q, Q), 1), 1.0, 0.0).astype(BF16)
    lane = iota((1, 128), 1)
    filler = jnp.zeros((1, 128 - 3 * heads), F32)
    decay = jnp.concatenate([decay_ref[...]] * 3 + [filler], axis=1)
    bias = jnp.concatenate([bias_ref[...]] * 3 + [filler], axis=1)
    growth = -jnp.exp(decay)

    def body(c, _):
        conv = conv_of(shifted_rows(rest_ref, c, 2 * N), taps)
        act_ref[rows_of(c), :] = low(conv * sig(conv))
        raw = rest_ref[rows_of(c), 2 * N :] + bias
        raw = jnp.where(lane < 3 * heads, raw, 0.0)
        step = jnp.maximum(raw, 0.0) + jnp.log(1.0 + jnp.exp(-jnp.abs(raw)))
        rate = growth * step
        cum = three_dot(tri, rate)
        packed = jnp.where(lane < heads, cum, jnp.where(lane < 2 * heads, cum - rate, step))
        packed = jnp.where(lane < 3 * heads, packed, 0.0)
        cols_ref[rows_of(c), :] = packed
        rows_ref[:, rows_of(c)] = packed.T
        return 0

    lax.fori_loop(0, length // Q, body, 0, unroll=4)


def prep(rest_pre, bc_taps, log_decay, dt_bias):
    length = rest_pre.shape[0]
    return pl.pallas_call(
        prep_kernel,
        out_shape=(
            jax.ShapeDtypeStruct((length, 2 * N), BF16),
            jax.ShapeDtypeStruct((length, 128), F32),
            jax.ShapeDtypeStruct((128, length), F32),
        ),
        compiler_params=pltpu.CompilerParams(vmem_limit_bytes=32 * MIB),
        cost_estimate=NO_COST,
        name="prep",
    )(rest_pre, bc_taps, log_decay[None], dt_bias[None])


def prefix_column(prefix, c):
    return jnp.where(iota((Q, 1), 0) + c * Q < prefix, 1.0, 0.0).astype(F32)


def growths(part, heads):
    lane = iota((1, 128), 1)
    used = lane < 2 * heads
    tail = part[Q - 8 :]
    last = jnp.where(lane < heads, tail, pltpu.roll(tail, heads, 1))[7:8]
    within = jnp.where(used, jnp.exp(jnp.where(used, part, 0.0)), 0.0)
    beyond = jnp.where(used, jnp.exp(jnp.where(used, last - part, 0.0)), 0.0)
    return within, beyond


def forward_kernel(
    heads, first, prefix_ref, x_ref, taps_ref, skip_ref, cols_ref, rows_ref, act_ref, *refs
):
    out_ref, xd_ref, kept_ref, back_ref, state_ref = refs[-5:]
    length, width = x_ref.shape
    chunks = length // Q
    anti = min(MAX_PREFIX // Q, chunks)
    prefix = prefix_ref[0]
    taps = taps_ref[...].astype(F32)
    skip = skip_ref[...]
    by_cum = spread_matrix(first, width)
    by_ecum = spread_matrix(heads + first, width)
    by_step = spread_matrix(2 * heads + first, width)
    lane_low = iota((1, 128), 1) < P_SIZE

    def stage_a(c, _):
        conv = conv_of(shifted_rows(x_ref, c), taps)
        x = conv * sig(conv)
        xd_ref[rows_of(c), :] = low(x * split_dot(cols_ref[rows_of(c), :], by_step))
        kept_ref[rows_of(c), :] = x * skip
        return 0

    lax.fori_loop(0, chunks, stage_a, 0, unroll=4)

    state_ref[...] = jnp.zeros_like(state_ref)
    back_ref[anti - 1] = jnp.zeros_like(back_ref[anti - 1])
    for c in range(anti - 1, 0, -1):
        within, _ = growths(cols_ref[rows_of(c), :], heads)
        weight = split_dot(within * prefix_column(prefix, c), by_ecum)
        grow = split_dot(within[Q - 8 :], by_cum)[7:8]
        b_mat = act_ref[rows_of(c), 0:N]
        xw = low(xd_ref[rows_of(c), :].astype(F32) * weight)
        state_ref[...] = state_ref[...] * grow + dot(b_mat, xw, TN)
        back_ref[c - 1] = low(state_ref[...])

    state_ref[...] = jnp.zeros_like(state_ref)
    causal_bias = jnp.where(iota((Q, Q), 1) <= iota((Q, Q), 0), 0.0, NEG).astype(F32)

    def chunk_body(c, two_way):
        b_mat = act_ref[rows_of(c), 0:N]
        c_mat = act_ref[rows_of(c), N : 2 * N]
        products = dot(c_mat, b_mat, NT)
        part = cols_ref[rows_of(c), :]
        within, beyond = growths(part, heads)
        entering = split_dot(within, by_cum)
        total = kept_ref[rows_of(c), :] + dot(c_mat, low(state_ref[...])) * entering
        if two_way:
            leaving = split_dot(beyond, by_ecum)
            total = total + dot(c_mat, back_ref[c]) * leaving
            anti_bias = jnp.where(
                (iota((Q, Q), 1) > iota((Q, Q), 0)) & (iota((Q, Q), 1) + c * Q < prefix), 0.0, NEG
            ).astype(F32)
        xd = xd_ref[rows_of(c), :]
        rows = rows_ref[first : first + HG, rows_of(c)]
        erows = rows_ref[heads + first : heads + first + HG, rows_of(c)]
        parts = []
        for pair in range(HG // 2):
            mixes = []
            for h in (2 * pair, 2 * pair + 1):
                e = part[:, first + h : first + h + 1] - rows[h : h + 1] + causal_bias
                if two_way:
                    at = heads + first + h
                    back = erows[h : h + 1] - part[:, at : at + 1] + anti_bias
                    e = jnp.maximum(e, back)
                mixes.append(low(jnp.exp(e) * products))
            x_pair = xd[:, pair * 128 : pair * 128 + 128]
            zero = jnp.zeros_like(x_pair)
            blocks = jnp.concatenate(
                [jnp.where(lane_low, x_pair, zero), jnp.where(lane_low, zero, x_pair)], axis=0
            )
            parts.append(dot(jnp.concatenate(mixes, axis=1), blocks))
        out_ref[rows_of(c), :] = (total + jnp.concatenate(parts, axis=1)).astype(out_ref.dtype)
        weight = split_dot(beyond, by_cum)
        xw = low(xd.astype(F32) * weight)
        state_ref[...] = state_ref[...] * entering[Q - 1 : Q] + dot(b_mat, xw, TN)
        return 0

    lax.fori_loop(0, anti, lambda c, _: chunk_body(c, True), 0, unroll=4)
    if chunks > anti:
        lax.fori_loop(anti, chunks, lambda c, _: chunk_body(c, False), 0, unroll=4)


def scan_forward(prefix, x_pre, taps, skip, cols, rows, act, group, out):
    length, channels = x_pre.shape
    anti = min(MAX_PREFIX // Q, length // Q)
    given = [prefix, x_pre, taps, skip, cols, rows, act]
    in_specs = [
        pl.BlockSpec(memory_space=pltpu.SMEM),
        pl.BlockSpec((length, CG), lambda g: (0, group)),
        pl.BlockSpec((4, CG), lambda g: (0, group)),
        pl.BlockSpec((1, CG), lambda g: (0, group)),
        pl.BlockSpec((length, 128), lambda g: (0, 0)),
        pl.BlockSpec((128, length), lambda g: (0, 0)),
        pl.BlockSpec((length, 2 * N), lambda g: (0, 0)),
    ]
    aliases = {}
    if out is not None:
        aliases = {len(given): 0}
        given.append(out)
        in_specs.append(pl.BlockSpec(memory_space=pl.ANY))
    return pl.pallas_call(
        functools.partial(forward_kernel, channels // P_SIZE, group * HG),
        grid=(1,),
        in_specs=in_specs,
        out_specs=pl.BlockSpec((length, CG), lambda g: (0, group)),
        out_shape=jax.ShapeDtypeStruct((length, channels), BF16),
        input_output_aliases=aliases,
        scratch_shapes=[
            pltpu.VMEM((length, CG), BF16),
            pltpu.VMEM((length, CG), F32),
            pltpu.VMEM((anti, N, CG), BF16),
            pltpu.VMEM((N, CG), F32),
        ],
        compiler_params=pltpu.CompilerParams(vmem_limit_bytes=40 * MIB),
        cost_estimate=NO_COST,
        name="scan_forward",
    )(*given)


def backward_kernel(
    heads,
    first,
    more,
    prefix_ref,
    x_ref,
    dy_scr,
    taps_ref,
    skip_ref,
    cols_ref,
    rows_ref,
    act_ref,
    *refs,
):
    (
        gx_ref,
        gact_ref,
        gcols_ref,
        grows_ref,
        gsum_ref,
        x_scr,
        slope_scr,
        states_scr,
        dback_scr,
        state_ref,
        dstate_ref,
        next_scr,
    ) = refs[-12:]
    length, width = x_ref.shape
    chunks = length // Q
    anti = min(MAX_PREFIX // Q, chunks)
    prefix = prefix_ref[0]
    taps = taps_ref[...].astype(F32)
    skip = skip_ref[...]
    by_cum = spread_matrix(first, width)
    by_ecum = spread_matrix(heads + first, width)
    by_step = spread_matrix(2 * heads + first, width)
    collect = gather_matrix(first, width)
    lane_low = iota((1, 128), 1) < P_SIZE

    gsum_ref[...] = jnp.zeros_like(gsum_ref)
    state_ref[...] = jnp.zeros_like(state_ref)

    def stage_a(c, two_way):
        conv = conv_of(shifted_rows(x_ref, c), taps)
        s = sig(conv)
        x = conv * s
        x_scr[rows_of(c), :] = x
        slope_scr[rows_of(c), :] = s + x * (1.0 - s)
        dy = dy_scr[rows_of(c), :].astype(F32)
        gsum_ref[4:5, :] += jnp.sum(dy * x, axis=0, keepdims=True)
        part = cols_ref[rows_of(c), :]
        within, beyond = growths(part, heads)
        states_scr[c] = low(state_ref[...])
        entering = split_dot(within[Q - 8 :], by_cum)
        x_low = low(x * split_dot(part, by_step) * split_dot(beyond, by_cum))
        b_mat = act_ref[rows_of(c), 0:N]
        c_mat = act_ref[rows_of(c), N : 2 * N]
        state_ref[...] = state_ref[...] * entering[7:8] + dot(b_mat, x_low, TN)
        if two_way:
            leaving = split_dot(beyond, by_ecum)
            dback_scr[c + 1] = low(
                dback_scr[c].astype(F32) * entering[7:8] + dot(c_mat, low(dy * leaving), TN)
            )
        return 0

    dback_scr[0] = jnp.zeros_like(dback_scr[0])
    lax.fori_loop(0, anti, lambda c, _: stage_a(c, True), 0, unroll=4)
    if chunks > anti:
        lax.fori_loop(anti, chunks, lambda c, _: stage_a(c, False), 0, unroll=4)

    state_ref[...] = jnp.zeros_like(state_ref)
    dstate_ref[...] = jnp.zeros_like(dstate_ref)
    next_scr[...] = jnp.zeros_like(next_scr)
    s_idx, t_idx = iota((Q, Q), 0), iota((Q, Q), 1)
    causal_bias = jnp.where(s_idx <= t_idx, 0.0, NEG).astype(F32)
    from_r = jnp.where(s_idx >= t_idx, 1.0, 0.0)
    upto_r = jnp.where(s_idx <= t_idx, 1.0, 0.0)
    zero_q = jnp.zeros((Q, Q), F32)

    def twice(m):
        return low(
            jnp.concatenate(
                [jnp.concatenate([m, zero_q], axis=1), jnp.concatenate([zero_q, m], axis=1)], axis=0
            )
        )

    from_pair, upto_pair = twice(from_r), twice(upto_r)
    pair_s, pair_r = iota((Q, 2 * Q), 0), iota((Q, 2 * Q), 1) % Q
    before_pair = pair_s < pair_r
    after_pair = pair_s > pair_r
    sum_from = jnp.where(t_idx >= s_idx, 1.0, 0.0).astype(BF16)
    sum_before = jnp.where(t_idx < s_idx, 1.0, 0.0).astype(BF16)
    sum_upto = jnp.where(t_idx <= s_idx, 1.0, 0.0).astype(BF16)
    sum_after = jnp.where(t_idx > s_idx, 1.0, 0.0).astype(BF16)
    sum_all = jnp.concatenate([sum_from, sum_before, sum_upto, sum_after], axis=1)

    def chunk_body(c, two_way):
        b_mat = act_ref[rows_of(c), 0:N]
        c_mat = act_ref[rows_of(c), N : 2 * N]
        products = dot(b_mat, c_mat, NT)
        part = cols_ref[rows_of(c), :]
        within, beyond = growths(part, heads)
        rows = rows_ref[first : first + HG, rows_of(c)]
        erows = rows_ref[heads + first : heads + first + HG, rows_of(c)]
        x = x_scr[rows_of(c), :]
        dy_low = dy_scr[rows_of(c), :]
        dy = dy_low.astype(F32)
        step_wide = split_dot(part, by_step)
        xd = x * step_wide
        xd_low = low(xd)
        if two_way:
            anti_bias = jnp.where((s_idx > t_idx) & (s_idx + c * Q < prefix), 0.0, NEG).astype(F32)
        dprod = jnp.zeros((Q, Q), F32)
        parts, inner = [], []
        for pair in range(HG // 2):
            lanes = slice(pair * 128, pair * 128 + 128)
            dy_pair = dy_low[:, lanes]
            zero = jnp.zeros_like(dy_pair)
            blocks = jnp.concatenate(
                [jnp.where(lane_low, dy_pair, zero), jnp.where(lane_low, zero, dy_pair)], axis=0
            )
            dmix = dot(xd_low[:, lanes], blocks, NT)
            mixes, moved = [], []
            for k in (0, 1):
                h = 2 * pair + k
                e = rows[h : h + 1] - part[:, first + h : first + h + 1] + causal_bias
                if two_way:
                    at = heads + first + h
                    back = part[:, at : at + 1] - erows[h : h + 1] + anti_bias
                    e = jnp.maximum(e, back)
                decay = jnp.exp(e)
                slab = dmix[:, k * Q : k * Q + Q] * decay
                dprod = dprod + slab
                mixes.append(low(decay * products))
                moved.append(low(slab * products))
            parts.append(dot(jnp.concatenate(mixes, axis=1), blocks))
            both = jnp.concatenate(moved, axis=1)
            crossing = jnp.where(before_pair, dot(both, from_pair), 0.0)
            if two_way:
                crossing = jnp.where(after_pair, dot(both, upto_pair), crossing)
            inner.append(jnp.sum(crossing, axis=0, keepdims=True))
        for pair in range(HG // 2):
            for k in (0, 1):
                h = 2 * pair + k
                grows_ref[0, h : h + 1, rows_of(c)] = inner[pair][:, k * Q : k * Q + Q]

        entering = split_dot(within, by_cum)
        to_last = split_dot(beyond, by_cum)
        grow = entering[Q - 1 : Q]
        dstate_low = low(dstate_ref[...])
        state_in = states_scr[c]
        du_carry = dot(b_mat, dstate_low) * to_last
        du = jnp.concatenate(parts, axis=1) + du_carry
        y_in = dot(c_mat, state_in) * entering
        dy_in = low(dy * entering)
        x_out = low(xd * to_last)
        d_c = dot(low(dprod), b_mat, TN) + dot(dy_in, state_in, NT)
        d_b = dot(low(dprod), c_mat) + dot(x_out, dstate_low, NT)
        moved_by = [low(dy * y_in), low(xd * du_carry)]
        across = jnp.sum(dstate_ref[...] * state_in.astype(F32), axis=0, keepdims=True) * grow
        if two_way:
            back_state = state_ref[...]
            back_low = low(back_state)
            dback_low = dback_scr[c]
            leaving = split_dot(beyond, by_ecum)
            from_first = split_dot(within * prefix_column(prefix, c), by_ecum)
            du_back = dot(b_mat, dback_low) * from_first
            du = du + du_back
            y_back = dot(c_mat, back_low) * leaving
            x_back = low(xd * from_first)
            d_c = d_c + dot(low(dy * leaving), back_low, NT)
            d_b = d_b + dot(x_back, dback_low, NT)
            moved_by = moved_by + [low(dy * y_back), low(xd * du_back)]
            across = across + grow * jnp.sum(
                dback_low.astype(F32) * back_state, axis=0, keepdims=True
            )
            state_ref[...] = back_state * grow + dot(b_mat, x_back, TN)
        dstate_ref[...] = dstate_ref[...] * grow + dot(c_mat, dy_in, TN)
        d_bc = jnp.concatenate([d_b, d_c], axis=1)
        summed = dot(sum_all if two_way else sum_all[:, : 2 * Q], jnp.concatenate(moved_by, axis=0))
        qk = dot(low(summed), collect)
        direct = dot(low(x * du), collect)
        across8 = low_pair_dot(jnp.broadcast_to(across, (8, width)), collect)
        d_cols = jnp.concatenate([direct, qk + across8[0:1]], axis=1)
        if more:
            d_bc = d_bc + refs[0][rows_of(c), :]
            d_cols = d_cols + refs[1][rows_of(c), :]
        gact_ref[rows_of(c), :] = d_bc
        gcols_ref[rows_of(c), :] = d_cols

        dconv = (du * step_wide + skip * dy) * slope_scr[rows_of(c), :]
        shifted = shifted_rows(x_ref, c)
        both = jnp.concatenate([dconv, next_scr[...]], axis=0)
        gx = taps[3:4] * dconv
        gsum_ref[3:4, :] += jnp.sum(dconv * shifted[0], axis=0, keepdims=True)
        for j in (1, 2, 3):
            gx = gx + taps[3 - j : 4 - j] * pltpu.roll(both, Q + 8 - j, 0)[:Q]
            gsum_ref[3 - j : 4 - j, :] += jnp.sum(dconv * shifted[j], axis=0, keepdims=True)
        gx_ref[rows_of(c), :] = low(gx)
        next_scr[...] = dconv[0:8]
        return 0

    if chunks > anti:
        lax.fori_loop(0, chunks - anti, lambda i, _: chunk_body(chunks - 1 - i, False), 0, unroll=4)
    lax.fori_loop(0, anti, lambda i, _: chunk_body(anti - 1 - i, True), 0, unroll=4)


def scan_backward(prefix, x_pre, grad_ssd, taps, skip, cols, rows, act, group, place, places, gx, before):
    length, channels = x_pre.shape
    chunks = length // Q
    anti = min(MAX_PREFIX // Q, chunks)
    wide = pl.BlockSpec((length, CG), lambda i: (0, group))
    given = [prefix, x_pre, grad_ssd, taps, skip, cols, rows, act]
    in_specs = [
        pl.BlockSpec(memory_space=pltpu.SMEM),
        wide,
        wide,
        pl.BlockSpec((4, CG), lambda i: (0, group)),
        pl.BlockSpec((1, CG), lambda i: (0, group)),
        pl.BlockSpec((length, 128), lambda i: (0, 0)),
        pl.BlockSpec((128, length), lambda i: (0, 0)),
        pl.BlockSpec((length, 2 * N), lambda i: (0, 0)),
    ]
    aliases = {}
    if before is not None:
        given += list(before)
        in_specs += [
            pl.BlockSpec((length, 2 * N), lambda i: (0, 0)),
            pl.BlockSpec((length, 256), lambda i: (0, 0)),
        ]
        aliases = {len(given) - 2: 1, len(given) - 1: 2}
    if gx is not None:
        aliases[len(given)] = 0
        given.append(gx)
        in_specs.append(pl.BlockSpec(memory_space=pl.ANY))
    return pl.pallas_call(
        functools.partial(backward_kernel, channels // P_SIZE, group * HG, before is not None),
        grid=(1,),
        in_specs=in_specs,
        out_specs=[
            pl.BlockSpec((length, CG), lambda i: (0, place)),
            pl.BlockSpec((length, 2 * N), lambda i: (0, 0)),
            pl.BlockSpec((length, 256), lambda i: (0, 0)),
            pl.BlockSpec((1, HG, length), lambda i: (0, 0, 0)),
            pl.BlockSpec((8, CG), lambda i: (0, 0)),
        ],
        out_shape=(
            jax.ShapeDtypeStruct((length, places * CG), BF16),
            jax.ShapeDtypeStruct((length, 2 * N), F32),
            jax.ShapeDtypeStruct((length, 256), F32),
            jax.ShapeDtypeStruct((1, HG, length), F32),
            jax.ShapeDtypeStruct((8, CG), F32),
        ),
        input_output_aliases=aliases,
        scratch_shapes=[
            pltpu.VMEM((length, CG), F32),
            pltpu.VMEM((length, CG), F32),
            pltpu.VMEM((chunks, N, CG), BF16),
            pltpu.VMEM((anti + 1, N, CG), BF16),
            pltpu.VMEM((N, CG), F32),
            pltpu.VMEM((N, CG), F32),
            pltpu.VMEM((8, CG), F32),
        ],
        compiler_params=pltpu.CompilerParams(vmem_limit_bytes=40 * MIB),
        cost_estimate=NO_COST,
        name="scan_backward",
    )(*given)


TILE = 128


def block_of(lanes_ref, j):
    return pl.ds(pl.multiple_of(lanes_ref[j] * 128, 128), 128)


def place_kernel(normalize, count, tiles, lanes_ref, slots_ref, *refs):
    sources, by_ref, out_ref = refs[:count], refs[count], refs[count + 1]
    width = out_ref.shape[1]
    for k in range(count):

        @pl.when(pl.program_id(0) // tiles == k)
        def _(ref=sources[k]):
            if normalize:
                wide = ref[...].astype(F32)
                inv = lax.rsqrt(jnp.sum(wide * wide, axis=-1, keepdims=True) / width + EPSILON)
            else:
                inv = by_ref[...]
            for j in range(width // 128):
                there = block_of(lanes_ref, j)
                v = ref[:, there].astype(F32) * inv
                if normalize:
                    v = v * by_ref[:, there]
                out_ref[:, j * 128 : j * 128 + 128] = low(v)


def place_tokens(lanes, slots, sources, by, normalize):
    tokens, width = sources[0].shape
    count, tiles = len(sources), tokens // TILE

    def source(k):
        return pl.BlockSpec((TILE, width), lambda i, a, s: (jnp.clip(i - k * tiles, 0, tiles - 1), 0))

    def placed(i, a, s):
        return (s[i // tiles] * tiles + i % tiles, 0)

    by_spec = pl.BlockSpec((1, width), lambda i, a, s: (0, 0)) if normalize else pl.BlockSpec((TILE, 1), placed)
    return pl.pallas_call(
        functools.partial(place_kernel, normalize, count, tiles),
        grid_spec=pltpu.PrefetchScalarGridSpec(
            num_scalar_prefetch=2,
            grid=(count * tiles,),
            in_specs=[source(k) for k in range(count)] + [by_spec],
            out_specs=pl.BlockSpec((TILE, width), placed),
        ),
        out_shape=jax.ShapeDtypeStruct((tokens * count, width), BF16),
        compiler_params=pltpu.CompilerParams(vmem_limit_bytes=32 * MIB),
        cost_estimate=NO_COST,
        name="place_tokens",
    )(lanes, slots, *sources, by)


def half_sum(refs, j, per_half):
    here = slice((j % per_half) * 128, (j % per_half) * 128 + 128)
    side = refs[: len(refs) // 2] if j < per_half else refs[len(refs) // 2 :]
    total = side[0][:, here].astype(F32)
    for ref in side[1:]:
        total = total + ref[:, here].astype(F32)
    return total


def mixed_kernel(lanes_ref, slots_ref, hidden_ref, *refs):
    out_ref = refs[-1]
    blocks = hidden_ref.shape[1] // 128
    for j in range(blocks):
        there = block_of(lanes_ref, j)
        out_ref[:, there] = hidden_ref[:, there].astype(F32) + half_sum(refs[:-1], j, blocks // 2)


def finish_kernel(lanes_ref, slots_ref, hidden_ref, cot_ref, gain_ref, *refs):
    out_ref = refs[-1]
    width = hidden_ref.shape[1]
    blocks = width // 128
    wide = hidden_ref[...].astype(F32)
    inv = lax.rsqrt(jnp.sum(wide * wide, axis=-1, keepdims=True) / width + EPSILON)
    total = jnp.zeros((TILE, 128), F32)
    for j in range(blocks):
        there = block_of(lanes_ref, j)
        scaled = half_sum(refs[:-1], j, blocks // 2) * gain_ref[:, there]
        total = total + scaled * hidden_ref[:, there].astype(F32)
        out_ref[:, there] = scaled
    coef = inv * inv * inv * (jnp.sum(total, axis=-1, keepdims=True) / width)
    out_ref[...] = inv * out_ref[...] - wide * coef + cot_ref[...].astype(F32)


def own_rows(kernel, name, lanes, slots, hidden, more, gain, halves):
    tokens, width = hidden.shape
    tiles = tokens // TILE
    tile = pl.BlockSpec((TILE, width), lambda i, a, s: (i, 0))
    given, specs = [hidden, *more], [tile] * (1 + len(more))
    if gain is not None:
        given.append(gain)
        specs.append(pl.BlockSpec((1, width), lambda i, a, s: (0, 0)))
    for half in halves:
        for array, whole in half:
            given.append(array)
            if whole:
                specs.append(pl.BlockSpec((TILE, width // 2), lambda i, a, s: (s[0] * tiles + i, 0)))
            else:
                specs.append(pl.BlockSpec((TILE, width // 2), lambda i, a, s: (i, 0)))
    return pl.pallas_call(
        kernel,
        grid_spec=pltpu.PrefetchScalarGridSpec(
            num_scalar_prefetch=2, grid=(tiles,), in_specs=specs, out_specs=tile
        ),
        out_shape=jax.ShapeDtypeStruct((tokens, width), F32),
        compiler_params=pltpu.CompilerParams(vmem_limit_bytes=40 * MIB),
        cost_estimate=NO_COST,
        name=name,
    )(lanes, slots, *given)


def post_kernel(rest_ref, taps_ref, decay_ref, bias_ref, *refs):
    gbc_ref, gtaps_ref, ghead_ref, next_scr = refs[-4:]
    gact_ref, gcols_ref, grows = refs[0], refs[1], refs[2:-4]
    length, heads = rest_ref.shape[0], decay_ref.shape[1]
    chunks = length // Q
    taps = taps_ref[...]
    gtaps_ref[...] = jnp.zeros_like(gtaps_ref)
    ghead_ref[...] = jnp.zeros_like(ghead_ref)
    next_scr[...] = jnp.zeros_like(next_scr)
    filler = jnp.zeros((1, 128 - heads), F32)
    growth = -jnp.exp(jnp.concatenate([decay_ref[...], filler], axis=1))
    bias = jnp.concatenate([bias_ref[...], filler], axis=1)

    def body(i, _):
        c = chunks - 1 - i
        shifted = shifted_rows(rest_ref, c, 2 * N)
        conv = conv_of(shifted, taps)
        s = sig(conv)
        dconv = gact_ref[rows_of(c), :] * (s + conv * s * (1.0 - s))
        both = jnp.concatenate([dconv, next_scr[...]], axis=0)
        g = taps[3:4] * dconv
        gtaps_ref[3:4, :] += jnp.sum(dconv * shifted[0], axis=0, keepdims=True)
        for j in (1, 2, 3):
            g = g + taps[3 - j : 4 - j] * pltpu.roll(both, Q + 8 - j, 0)[:Q]
            gtaps_ref[3 - j : 4 - j, :] += jnp.sum(dconv * shifted[j], axis=0, keepdims=True)
        gbc_ref[rows_of(c), 0 : 2 * N] = low(g)
        next_scr[...] = dconv[0:8]

        direct, moved = gcols_ref[rows_of(c), 0:128], gcols_ref[rows_of(c), 128:256]
        inner = [ref[0, :, rows_of(c)] for ref in grows]
        inner.append(jnp.zeros((128 - heads, Q), F32))
        moved = moved + jnp.concatenate(inner, axis=0).T
        raw = rest_ref[rows_of(c), 2 * N :] + bias
        step = jnp.maximum(raw, 0.0) + jnp.log(1.0 + jnp.exp(-jnp.abs(raw)))
        gdt = (direct + moved * growth) * sig(raw)
        gbc_ref[rows_of(c), 2 * N :] = low(gdt[:, 0:heads])
        ghead_ref[0:1, :] += jnp.sum(moved * growth * step, axis=0, keepdims=True)
        ghead_ref[1:2, :] += jnp.sum(gdt, axis=0, keepdims=True)
        return 0

    lax.fori_loop(0, chunks, body, 0, unroll=4)


def post(rest_pre, bc_taps, log_decay, dt_bias, grad_act, gcols, grows):
    length, heads = rest_pre.shape[0], log_decay.shape[0]
    return pl.pallas_call(
        post_kernel,
        out_shape=(
            jax.ShapeDtypeStruct((length, 2 * N + heads), BF16),
            jax.ShapeDtypeStruct((8, 2 * N), F32),
            jax.ShapeDtypeStruct((8, 128), F32),
        ),
        scratch_shapes=[pltpu.VMEM((8, 2 * N), F32)],
        compiler_params=pltpu.CompilerParams(vmem_limit_bytes=40 * MIB),
        cost_estimate=NO_COST,
        name="post",
    )(rest_pre, bc_taps, log_decay[None], dt_bias[None], grad_act, gcols, *grows)


def snake(devices):
    half = devices // 4
    return [z * 2 for z in range(half)] + [z * 2 + 1 for z in reversed(range(half))]


def chip_groups(devices):
    return [[chip * 2 + core for chip in snake(devices)] for core in (0, 1)]


def other_core(v, devices):
    return lax.ppermute(v, "fsdp", [(i, i ^ 1) for i in range(devices)])


def other_half(v):
    return lax.ppermute(v, "tp", [(0, 1), (1, 0)])


def tie(first, second):
    return lax.optimization_barrier((first, second))


def gather(v, devices):
    return lax.all_gather(v, "fsdp", axis=0, tiled=True, axis_index_groups=chip_groups(devices))


def doubling_gather(v, devices):
    me = lax.axis_index("fsdp")
    bit = 1
    while bit < devices:
        came = lax.ppermute(v, "fsdp", [(i, i ^ bit) for i in range(devices)])
        mine_first = me & bit == 0
        v = jnp.concatenate([jnp.where(mine_first, v, came), jnp.where(mine_first, came, v)], axis=0)
        bit *= 2
    return v


def scatter(v, devices):
    return lax.psum_scatter(
        v, "fsdp", scatter_dimension=0, tiled=True, axis_index_groups=chip_groups(devices)
    )


def on_device(
    hidden,
    cotangent,
    prefix,
    input_norm_gain,
    z_weight,
    x_weight,
    bc_weight,
    dt_weight,
    x_conv,
    bc_conv,
    log_decay,
    dt_bias,
    skip_gain,
    gate_gain,
    out_weight,
):
    fsdp = lax.axis_size("fsdp")
    tp = lax.axis_size("tp")
    own_tokens, width = hidden.shape
    heads = log_decay.shape[0]
    channels = heads * P_SIZE
    all_channels = channels * tp
    groups = channels // CG
    taps_own = x_conv.shape[2]
    rows = width // fsdp
    ring = fsdp // 2
    half_width = width // 2

    order = snake(fsdp)
    core = lax.axis_index("fsdp") % 2
    line = jnp.array(order, jnp.int32)
    blocks = jnp.concatenate([line * 2 + core, line * 2 + 1 - core])
    direct = rows % 128 == 0
    per = max(rows // 128, 1)
    if direct:
        lanes = (blocks[:, None] * per + jnp.arange(per)[None]).reshape(-1)
    else:
        lanes = jnp.arange(width // 128)
    lanes = lanes.astype(jnp.int32)

    def to_cores(v):
        zero = jnp.stack([v[2 * chip] for chip in order])
        one = jnp.stack([v[2 * chip + 1] for chip in order])
        return jnp.where(core == 0, zero, one), jnp.where(core == 0, one, zero)

    def to_ring(v):
        return v if direct else v.reshape(-1, fsdp, rows)[:, blocks].reshape(v.shape)

    def from_ring(v):
        if direct:
            return v
        return v.reshape(-1, fsdp, rows)[:, jnp.argsort(blocks)].reshape(v.shape)

    small = jnp.concatenate(
        [input_norm_gain.reshape(-1), x_conv.reshape(-1), bc_conv.reshape(-1), gate_gain.reshape(-1)]
    )
    sizes = [input_norm_gain.size, x_conv.size, bc_conv.size, gate_gain.size]
    cuts = [0]
    for size in sizes:
        cuts.append(cuts[-1] + size)
    small_all = doubling_gather(jnp.pad(small, (0, -small.size % 128))[None], fsdp)
    payload = jnp.concatenate([x_weight, bc_weight, dt_weight, dt_weight, dt_weight], axis=1)
    payload = jnp.pad(payload, ((0, 0), (0, 128 - 3 * heads)))

    if tp == 2:
        mine = lax.axis_index("tp").astype(jnp.int32)
        slots = jnp.stack([mine, 1 - mine])
        hidden_other = other_half(hidden)
        cot_given, hidden_other = tie(cotangent, hidden_other)
        hidden_parts = [hidden, hidden_other]
        cot_parts = [cotangent, other_half(cot_given)]
    else:
        slots = jnp.zeros((2,), jnp.int32)
        hidden_parts = [lax.all_gather(hidden, "tp", axis=0, tiled=True)]
        cot_parts = [lax.all_gather(cotangent, "tp", axis=0, tiled=True)]
    hidden_parts = [to_ring(v) for v in hidden_parts]
    cot_parts = [to_ring(v) for v in cot_parts]

    norm_gain = small_all[:, cuts[0] : cuts[1]].reshape(1, -1).astype(F32)
    x_taps = small_all[:, cuts[1] : cuts[2]].reshape(fsdp, heads, 4, taps_own)
    x_taps = jnp.transpose(x_taps, (2, 1, 0, 3)).reshape(4, channels).astype(F32)
    bc_taps = small_all[:, cuts[2] : cuts[3]].reshape(fsdp, 4, -1)
    bc_taps = jnp.transpose(bc_taps, (1, 0, 2)).reshape(4, 2 * N).astype(F32)
    gain = small_all[:, cuts[3] : cuts[4]].reshape(fsdp, heads, -1)
    gain = jnp.transpose(gain, (1, 0, 2)).reshape(1, channels).astype(F32)
    skip = jnp.repeat(skip_gain, P_SIZE)[None]
    hidden_parts[-1], (norm_gain, x_taps, bc_taps, gain, skip) = tie(
        hidden_parts[-1], (norm_gain, x_taps, bc_taps, gain, skip)
    )

    x_own = gather(payload, fsdp)
    z_own = gather(z_weight, fsdp)
    out_own = gather(out_weight.T, fsdp)
    x_own, hidden_parts[-1] = tie(x_own, hidden_parts[-1])
    x_other = other_core(x_own, fsdp)

    norm_gain = to_ring(norm_gain)
    normed = place_tokens(lanes, slots, hidden_parts, norm_gain, True)
    na, nb = normed[:, :half_width], normed[:, half_width:]
    few = slice(channels, channels + 2 * N + 128)
    rest_pre = dot(na, x_own[:, few]) + dot(nb, x_other[:, few])
    rest = slice(channels, channels + 2 * N + heads)
    rest_own, rest_other = x_own[:, rest], x_other[:, rest]
    act, cols, head_rows = prep(rest_pre, bc_taps, log_decay, dt_bias)
    x_pre = low(dot(na, x_own[:, :channels]) + dot(nb, x_other[:, :channels]))
    ssd_out = None
    for g in range(groups):
        ssd_out = scan_forward(prefix, x_pre, x_taps, skip, cols, head_rows, act, g, ssd_out)
    (z_own, cot_parts[-1]), ssd_out = tie((z_own, cot_parts[-1]), ssd_out)
    z_other = other_core(z_own, fsdp)

    gate_pre = dot(na, z_own) + dot(nb, z_other)
    gated = ssd_out.astype(F32) * (gate_pre * sig(gate_pre))
    square_sum = lax.psum(jnp.sum(gated * gated, axis=-1), "tp")
    gate_low = low(gate_pre)
    scaled_out = low(gated * gain)
    out_own, scaled_out = tie(out_own, scaled_out)
    out_other = other_core(out_own, fsdp)

    inv_gate = lax.rsqrt(square_sum / all_channels + EPSILON)[:, None]
    cot_rel = place_tokens(lanes, slots, cot_parts, inv_gate, False)
    ca, cb = cot_rel[:, :half_width], cot_rel[:, half_width:]
    gout_came = other_core(low(dot(cb, scaled_out, TN)), fsdp)

    branch, along = [], 0.0
    for cot_half, out_half in ((ca, out_own), (cb, out_other)):
        v = dot(scaled_out, out_half, NT)
        along = along + jnp.sum(v * cot_half.astype(F32), axis=-1)
        branch.append(low(v * inv_gate))
    along = lax.psum(along, "tp")
    coef = inv_gate * inv_gate * (along / all_channels)[:, None]
    scaled_out, coef = tie(scaled_out, coef)
    gout_sum = low(dot(ca, scaled_out, TN) + gout_came.astype(F32))
    (coef, branch), gout_sum = tie((coef, branch), gout_sum)
    grad_out = scatter(gout_sum, fsdp)

    def to_own_tokens(v):
        if tp == 2:
            leaving = lax.dynamic_slice_in_dim(v, (1 - mine) * own_tokens, own_tokens, 0)
            return [(v, True), (other_half(leaving), False)]
        return [(lax.psum_scatter(v, "tp", scatter_dimension=0, tiled=True), False)]

    branch_parts = [to_own_tokens(v) for v in branch]
    kinds = [[whole for _, whole in half] for half in branch_parts]
    branch_parts = [[v for v, _ in half] for half in branch_parts]

    scaled = dot(ca, out_own) + dot(cb, out_other)
    z = gate_low.astype(F32)
    s = sig(z)
    gate_act = z * s
    y = ssd_out.astype(F32)
    gated = y * gate_act
    ggain = jnp.sum(scaled * gated, axis=0)
    grad_gated = gain * scaled - gated * coef
    ggate = low(grad_gated * y * (s + gate_act * (1.0 - s)))
    dy = low(grad_gated * gate_act)
    gz_came = other_core(low(dot(nb, ggate, TN)), fsdp)
    z_parts = [dot(ggate, z_own, NT), dot(ggate, z_other, NT)]
    na, z_parts = tie(na, z_parts)
    gz_sum = low(dot(na, ggate, TN) + gz_came.astype(F32))
    dy, gz_sum = tie(dy, gz_sum)
    grad_z = scatter(gz_sum, fsdp)

    grows, gsums = [], []
    first = groups // 2
    before = None

    def back_through(start, stop, dy, before):
        gx = None
        for g in range(start, stop):
            if g == 1:
                dy, branch_parts[0] = tie(dy, branch_parts[0])
            gx, gact, gcol, grow, gsum = scan_backward(
                prefix, x_pre, dy, x_taps, skip, cols, head_rows, act, g, g - start, stop - start, gx, before
            )
            before = (gact, gcol)
            grows.append(grow)
            gsums.append(gsum)
        return gx, before

    grad_x = []
    if first:
        gx, before = back_through(0, first, dy, before)
        gx, branch_parts[1] = tie(gx, branch_parts[1])
        came = other_core(low(dot(nb, gx, TN)), fsdp)
        z_parts = [
            v + dot(gx, half[:, : first * CG], NT) for v, half in zip(z_parts, (x_own, x_other))
        ]
        na, z_parts = tie(na, z_parts)
        total = low(dot(na, gx, TN) + came.astype(F32))
        dy, (total, grad_out) = tie(dy, (total, grad_out))
        grad_x.append(scatter(total, fsdp))
    gx, before = back_through(first, groups, dy, before)
    gx, (grad_z, *grad_x) = tie(gx, (grad_z, *grad_x))
    gx_other = low(dot(nb, gx, TN))
    came = other_core(gx_other, fsdp)
    before, gx_other = tie(before, gx_other)
    grest, gbc_taps, ghead = post(rest_pre, bc_taps, log_decay, dt_bias, before[0], before[1], grows)
    na, grest = tie(na, grest)
    gx_sum = low(dot(na, gx, TN) + came.astype(F32))
    (gx, grest, ghead), gx_sum = tie((gx, grest, ghead), gx_sum)
    grad_x = list(grad_x)
    grad_x.append(scatter(gx_sum, fsdp))

    gsum = jnp.concatenate(gsums, axis=1)
    gx_taps = jnp.transpose(gsum[0:4].reshape(4, heads, fsdp, taps_own), (2, 1, 0, 3))
    g_taps = jnp.transpose(gbc_taps[0:4].reshape(4, fsdp, -1), (1, 0, 2))
    g_gain = jnp.transpose(ggain.reshape(heads, fsdp, -1), (1, 0, 2))
    g_skip = jnp.sum(gsum[4].reshape(heads, P_SIZE), axis=-1)
    per_head = jnp.concatenate([ghead[0, :heads], ghead[1, :heads], g_skip])
    slices = jnp.concatenate(
        [
            g_taps.reshape(fsdp, -1),
            gx_taps.reshape(fsdp, -1),
            g_gain.reshape(fsdp, -1),
            jnp.broadcast_to(per_head[None], (fsdp, per_head.size)),
        ],
        axis=1,
    )
    size = slices.shape[1]
    lone = -(-size // rows)
    lines_own, lines_other = [
        jnp.pad(v, ((0, 0), (0, lone * rows - size))).reshape(half_width, lone) for v in to_cores(slices)
    ]
    rest_came = other_core(jnp.concatenate([dot(nb, grest, TN), lines_other], axis=1), fsdp)

    def part_of(v, x_half, r_half):
        return low(v + dot(gx, x_half[:, first * CG : channels], NT) + dot(grest, r_half, NT))

    part_sums = [to_own_tokens(part_of(z_parts[0], x_own, rest_own))]
    kinds_part = [whole for _, whole in part_sums[0]]
    gx, first_part = tie(gx, part_sums[0][0][0])
    arrived = [first_part] + [v for v, _ in part_sums[0][1:]]
    second = part_of(z_parts[1], x_other, rest_other)
    part_sums.append(to_own_tokens(second))
    rest_sum = jnp.concatenate([dot(na, grest, TN), lines_own], axis=1) + rest_came
    rest_sum, arrived, second, grad_x[-1] = lax.optimization_barrier(
        (rest_sum, arrived, second, grad_x[-1])
    )
    part_sums[0] = list(zip(arrived, kinds_part))
    mine_rest = scatter(rest_sum, fsdp)

    mixed = from_ring(
        own_rows(
            mixed_kernel, "add_branch", lanes, slots, to_ring(hidden), [], None,
            [list(zip(half, kind)) for half, kind in zip(branch_parts, kinds)],
        )
    )
    grad_hidden = from_ring(
        own_rows(finish_kernel, "finish", lanes, slots, to_ring(hidden), [to_ring(cotangent)], norm_gain, part_sums)
    )

    grad_z, grad_out = grad_z.astype(F32), grad_out.astype(F32).T
    grad_x = jnp.concatenate(grad_x, axis=1).astype(F32)
    grad_bc, grad_dt = mine_rest[:, : 2 * N], mine_rest[:, 2 * N : 2 * N + heads]
    lines = mine_rest[:, 2 * N + heads :].reshape(-1)
    grad_gain = sum(
        jnp.sum(w.astype(F32) * g, axis=1)
        for w, g in ((z_weight, grad_z), (x_weight, grad_x), (bc_weight, grad_bc), (dt_weight, grad_dt))
    ) / input_norm_gain.astype(F32)
    n_taps = bc_conv.size
    together = jnp.concatenate([grad_bc.reshape(-1), grad_gain, lines[:n_taps]])
    together = together + other_half(together) if tp == 2 else lax.psum(together, "tp")
    bc_size = rows * 2 * N
    at = [n_taps]
    for size in (x_conv.size, gate_gain.size, heads, heads, heads):
        at.append(at[-1] + size)
    return (
        mixed,
        grad_hidden,
        together[bc_size : bc_size + rows],
        grad_z,
        grad_x,
        together[:bc_size].reshape(rows, 2 * N),
        grad_dt,
        lines[at[0] : at[1]].reshape(x_conv.shape),
        together[bc_size + rows :].reshape(bc_conv.shape),
        lines[at[2] : at[3]],
        lines[at[3] : at[4]],
        lines[at[4] : at[5]],
        lines[at[1] : at[2]].reshape(gate_gain.shape),
        grad_out,
    )


def solution(mesh):
    both = P(("fsdp", "tp"), None)
    split = P("fsdp", "tp")
    ins = (
        both, both, P("fsdp"), P("fsdp"), split, split, P("fsdp", None), split, P("tp", None, "fsdp"),
        P(None, "fsdp"), P("tp"), P("tp"), P("tp"), P("tp", "fsdp"), P("tp", "fsdp"),
    )
    outs = (
        both, both, P("fsdp"), split, split, P("fsdp", None), split, P("tp", None, "fsdp"),
        P(None, "fsdp"), P("tp"), P("tp"), P("tp"), P("tp", "fsdp"), P("tp", "fsdp"),
    )
    return jax.shard_map(on_device, mesh=mesh, in_specs=ins, out_specs=outs, check_vma=False)
```

profile of v0, /device:TPU:0, one launch (start us, length us, event | category | flops | bytes accessed | tf_op | source)
XLA Modules:
  0.0 505.6 jit_solution(1104151603532173567)
XLA Ops:
  35.8 24.2 %collective-permute-done.refs_1_ = bf16[512,2048]{1,0:T(8,128)(2,1)} collective-permute-done((bf16[512,2048]{1,0:T(8,128)(2,1)}, bf16[512,2048]{1,0:T(8,128)(2,1)}, u32[]{:S(2)}, u32[]{:S(2)}) %collective-permute-start) | collective-permute-done | bytes 2097184 | tf_op jit(solution)/shard_map/ppermute | solution.py:726
  60.0 8.8 %all-gather.6.cloned.1.call-done = bf16[1024,2432]{1,0:T(8,128)(2,1)} async-done(((bf16[128,2432]{1,0:T(8,128)(2,1)}), bf16[1024,2432]{1,0:T(8,128)(2,1)}) %all-gather.6.cloned.1.call-update) | async-done | bytes 4980752 | tf_op jit(solution)/shard_map/all_gather | solution.py:734
  76.9 6.8 %fusion.10 = f32[1024,2048]{1,0:T(8,128)} fusion(bf16[1024,2432]{1,0:T(8,128)(2,1)S(1)} %copy-done.57, bf16[1024,2048]{1,0:T(8,128)(2,1)S(1)} %place_tokens.2), kind=kOutput, calls=%fused_computation.31 | convolution fusion | flops 4294967296 | bytes 14680064 | tf_op jit(solution)/shard_map/dot_general | solution.py:28
  85.0 8.3 %add_convert_fusion.2.x_ref = bf16[1024,2048]{1,0:T(8,128)(2,1)S(1)} fusion(f32[1024,2048]{1,0:T(8,128)} %fusion.10, bf16[1024,2432]{1,0:T(8,128)(2,1)} %collective-permute-done.6, bf16[1024,2048]{1,0:T(8,128)(2,1)S(1)} %place_tokens.2), kind=kOutput, calls=%fused_computation.20 | convolution fusion | flops 4299161600 | bytes 18874368 | tf_op jit(solution)/shard_map/dot_general | solution.py:28
  98.3 6.8 %scan_forward.4.refs_0_ = bf16[1024,2048]{1,0:T(8,128)(2,1)S(1)} custom-call(s32[1]{0:T(128)S(6)} %copy.165.prefix_ref, bf16[1024,2048]{1,0:T(8,128)(2,1)S(1)} %add_convert_fusion.2.x_ref, f32[4,2048]{1,0:T(4,128)S(1)} %reshape.149.taps_ref, f32[1,2048]{1,0:T(1,128)S(1)} %broadcast_in_dim_reshape.3.skip_ref, f32[1024,128]{1,0:T(8,128)S(1)} %get-tuple-element.105.cols_ref, ...), custom_call_target="tpu_custom_call" | custom-call | tf_op jit(solution)/shard_map/scan_forward/pallas_call | solution.py:251
  105.2 6.6 %scan_forward.5.refs_0_ = bf16[1024,2048]{1,0:T(8,128)(2,1)S(1)} custom-call(s32[1]{0:T(128)S(6)} %copy.165.prefix_ref, bf16[1024,2048]{1,0:T(8,128)(2,1)S(1)} %add_convert_fusion.2.x_ref, f32[4,2048]{1,0:T(4,128)S(1)} %reshape.149.taps_ref, f32[1,2048]{1,0:T(1,128)S(1)} %broadcast_in_dim_reshape.3.skip_ref, ...), custom_call_target="tpu_custom_call", output_to_operand_aliasing={{}: (7, {})} | custom-call | tf_op jit(solution)/shard_map/scan_forward/pallas_call | solution.py:251
  111.8 7.2 %scan_forward.6.refs_0_ = bf16[1024,2048]{1,0:T(8,128)(2,1)S(1)} custom-call(s32[1]{0:T(128)S(6)} %copy.165.prefix_ref, bf16[1024,2048]{1,0:T(8,128)(2,1)S(1)} %add_convert_fusion.2.x_ref, f32[4,2048]{1,0:T(4,128)S(1)} %reshape.149.taps_ref, f32[1,2048]{1,0:T(1,128)S(1)} %broadcast_in_dim_reshape.3.skip_ref, ...), custom_call_target="tpu_custom_call", output_to_operand_aliasing={{}: (7, {})} | custom-call | tf_op jit(solution)/shard_map/scan_forward/pallas_call | solution.py:251
  118.9 6.7 %scan_forward.7 = bf16[1024,2048]{1,0:T(8,128)(2,1)S(1)} custom-call(s32[1]{0:T(128)S(6)} %copy.165.prefix_ref, bf16[1024,2048]{1,0:T(8,128)(2,1)S(1)} %add_convert_fusion.2.x_ref, f32[4,2048]{1,0:T(4,128)S(1)} %reshape.149.taps_ref, f32[1,2048]{1,0:T(1,128)S(1)} %broadcast_in_dim_reshape.3.skip_ref, ...), custom_call_target="tpu_custom_call", output_to_operand_aliasing={{}: (7, {})} | custom-call | tf_op jit(solution)/shard_map/scan_forward/pallas_call | solution.py:251
  129.3 7.1 %collective-permute-done.7 = bf16[1024,2048]{1,0:T(8,128)(2,1)S(1)} collective-permute-done((bf16[1024,2048]{1,0:T(8,128)(2,1)}, bf16[1024,2048]{1,0:T(8,128)(2,1)S(1)}, u32[]{:S(2)}, u32[]{:S(2)}) %collective-permute-start.7) | collective-permute-done | bytes 4194336 | tf_op jit(solution)/shard_map/ppermute | solution.py:722
  136.4 9.9 %fusion.49 = f32[1024,2048]{1,0:T(8,128)} fusion(bf16[1024,2048]{1,0:T(8,128)(2,1)S(1)} %collective-permute-done.7, bf16[1024,2048]{1,0:T(8,128)(2,1)} %copy-done.16), kind=kOutput, calls=%fused_computation.72 | convolution fusion | flops 4294967296 | bytes 14680064 | tf_op jit(solution)/shard_map/dot_general | solution.py:28
  146.4 11.5 %multiply_reduce_fusion.1 = (f32[1024]{0:T(1024)S(1)}, bf16[1024,2048]{1,0:T(8,128)(2,1)}, bf16[1024,2048]{1,0:T(8,128)(2,1)}) fusion(bf16[1024,2048]{1,0:T(8,128)(2,1)S(1)} %copy-done.6, f32[2048]{0:T(1024)S(1)} %bitcast.87, f32[1024,2048]{1,0:T(8,128)} %fusion.49, bf16[1024,2048]{1,0:T(8,128)(2,1)S(1)} %copy-done.62, bf16[1024,2048]{1,0:T(8,128)(2,1)S(1)} %copy-done.17), kind=kOutput, calls=%fused_computation.19 | convolution fusion | flops 4320132096 | bytes 27275264 | tf_op jit(solution)/shard_map/dot_general | solution.py:28
  157.9 17.5 %all-gather.8.cloned.1.call-done = bf16[1024,2048]{0,1:T(8,128)(2,1)} async-done(((bf16[128,2048]{0,1:T(8,128)(2,1)}), bf16[1024,2048]{0,1:T(8,128)(2,1)}) %all-gather.8.cloned.1.call-update) | async-done | bytes 4194320 | tf_op jit(solution)/shard_map/all_gather | solution.py:734
  186.6 6.3 %convolution_convert_fusion.1 = bf16[1024,2048]{1,0:T(8,128)(2,1)} fusion(bf16[1024,2048]{1,0:T(8,128)(2,1)S(1)} %copy-done.69, bf16[1024,2048]{1,0:T(8,128)(2,1)S(1)} %place_tokens.3), kind=kOutput, calls=%fused_computation.36 | convolution fusion | flops 4297064448 | bytes 10485760 | tf_op jit(solution)/shard_map/dot_general | solution.py:28
  192.9 6.9 %fusion.32 = f32[1024,2048]{1,0:T(8,128)} fusion(bf16[1024,2048]{0,1:T(8,128)(2,1)S(1)} %copy-done.64, bf16[1024,2048]{1,0:T(8,128)(2,1)S(1)} %place_tokens.3), kind=kOutput, calls=%fused_computation.53 | convolution fusion | flops 4294967296 | bytes 14680064 | tf_op jit(solution)/shard_map/dot_general | solution.py:28
  204.3 9.0 %multiply_reduce_fusion.2 = (f32[1024]{0:T(1024)S(1)}, f32[1024]{0:T(1024)S(1)}, bf16[1024,1024]{1,0:T(8,128)(2,1)}, bf16[1024,1024]{1,0:T(8,128)(2,1)}) fusion(bf16[1024,2048]{1,0:T(8,128)(2,1)S(1)} %place_tokens.3, f32[1024,1024]{1,0:T(8,128)S(1)} %fusion.72, f32[1024]{0:T(1024)S(1)} %add_rsqrt_fusion, bf16[1024,2048]{1,0:T(8,128)(2,1)S(1)} %copy-done.69, ...), kind=kOutput, calls=%fused_computation.29 | convolution fusion | flops 4305451008 | bytes 20983808 | tf_op jit(solution)/shard_map/dot_general | solution.py:28
  218.2 10.6 %add_convert_fusion.1 = bf16[1024,2048]{1,0:T(8,128)(2,1)} fusion(bf16[1024,2048]{1,0:T(8,128)(2,1)} %collective-permute-done.9, bf16[1024,2048]{1,0:T(8,128)(2,1)} %get-tuple-element.114, bf16[1024,2048]{1,0:T(8,128)(2,1)} %copy-done.26), kind=kOutput, calls=%fused_computation.17 | convolution fusion | flops 4301258752 | bytes 14680064 | tf_op jit(solution)/shard_map/dot_general | solution.py:28
  229.3 18.7 %fusion.7 = (bf16[1024,2048]{1,0:T(8,128)(2,1)}, bf16[1024,2048]{1,0:T(8,128)(2,1)}, f32[2048]{0:T(1024)S(1)}) fusion(bf16[1024,2048]{1,0:T(8,128)(2,1)} %copy-done.5, f32[1024]{0:T(1024)S(1)} %multiply_multiply_fusion, f32[2048]{0:T(1024)S(1)} %bitcast.88, bf16[1024,2048]{1,0:T(8,128)(2,1)} %get-tuple-element.282, f32[1024,2048]{1,0:T(8,128)} %fusion.32, ...), kind=kOutput, calls=%fused_computation.12 | convolution fusion | flops 4339005440 | bytes 31477760 | tf_op jit(solution)/shard_map/dot_general | solution.py:28
  248.0 7.3 %convolution_convert_fusion = bf16[1024,2048]{1,0:T(8,128)(2,1)S(1)} fusion(bf16[1024,2048]{1,0:T(8,128)(2,1)} %get-tuple-element.240, bf16[1024,2048]{1,0:T(8,128)(2,1)S(1)} %copy-done.18), kind=kOutput, calls=%fused_computation.35 | convolution fusion | flops 4297064448 | bytes 10485760 | tf_op jit(solution)/shard_map/dot_general | solution.py:28
  257.5 6.1 %fusion.73 = f32[1024,1024]{1,0:T(8,128)} fusion(bf16[1024,2048]{1,0:T(8,128)(2,1)S(1)} %copy-done.70, bf16[1024,2048]{1,0:T(8,128)(2,1)S(1)} %copy-done.63), kind=kOutput, calls=%fused_computation.143 | convolution fusion | flops 4294967296 | bytes 12582912 | tf_op jit(solution)/shard_map/dot_general | solution.py:28
  263.5 6.1 %fusion.74 = f32[1024,1024]{1,0:T(8,128)} fusion(bf16[1024,2048]{1,0:T(8,128)(2,1)S(1)} %copy-done.70, bf16[1024,2048]{1,0:T(8,128)(2,1)S(1)} %copy-done.66), kind=kOutput, calls=%fused_computation.144 | convolution fusion | flops 4294967296 | bytes 12582912 | tf_op jit(solution)/shard_map/dot_general | solution.py:28
  269.6 6.3 %add_convert_fusion = bf16[1024,2048]{1,0:T(8,128)(2,1)} fusion(bf16[1024,2048]{1,0:T(8,128)(2,1)S(1)} %collective-permute-done.10, bf16[1024,1024]{1,0:T(8,128)(2,1)S(1)} %slice.227, bf16[1024,2048]{1,0:T(8,128)(2,1)S(1)} %copy-done.70), kind=kOutput, calls=%fused_computation.14 | convolution fusion | flops 4301258752 | bytes 14680064 | tf_op jit(solution)/shard_map/dot_general | solution.py:28
  283.3 17.3 %scan_backward.4 = (bf16[1024,1024]{1,0:T(8,128)(2,1)S(1)}, f32[1024,256]{1,0:T(8,128)S(1)}, f32[1024,256]{1,0:T(8,128)S(1)}, f32[1,8,1024]{2,1,0:T(8,128)S(1)}, f32[8,512]{1,0:T(8,128)S(1)}) custom-call(s32[1]{0:T(128)S(6)} %copy.165.prefix_ref, bf16[1024,2048]{1,0:T(8,128)(2,1)S(1)} %copy-done.1, bf16[1024,2048]{1,0:T(8,128)(2,1)S(1)} %copy-done.3, ...), custom_call_target="tpu_custom_call" | custom-call | tf_op jit(solution)/shard_map/scan_backward/pallas_call | solution.py:506
  304.8 17.7 %scan_backward.5 = (bf16[1024,1024]{1,0:T(8,128)(2,1)S(1)}, f32[1024,256]{1,0:T(8,128)S(1)}, f32[1024,256]{1,0:T(8,128)S(1)}, f32[1,8,1024]{2,1,0:T(8,128)S(1)}, f32[8,512]{1,0:T(8,128)S(1)}) custom-call(s32[1]{0:T(128)S(6)} %copy.165.prefix_ref, bf16[1024,2048]{1,0:T(8,128)(2,1)S(1)} %copy-done.1, ...), custom_call_target="tpu_custom_call", output_to_operand_aliasing={{1}: (8, {}), {2}: (9, {}), {0}: (10, {})} | custom-call | tf_op jit(solution)/shard_map/scan_backward/pallas_call | solution.py:506
  327.4 6.1 %fusion.22 = f32[1024,1024]{1,0:T(8,128)} fusion(f32[1024,1024]{1,0:T(8,128)S(1)} %copy-done.67, bf16[1024,1024]{1,0:T(8,128)(2,1)S(1)} %get-tuple-element.130, bf16[1024,2432]{1,0:T(8,128)(2,1)} %all-gather.6.cloned.1.call-done), kind=kOutput, calls=%fused_computation.45 | convolution fusion | flops 2148532224 | bytes 12582912 | tf_op jit(solution)/shard_map/dot_general | solution.py:28
  333.6 6.3 %fusion.25 = f32[1024,1024]{1,0:T(8,128)} fusion(f32[1024,1024]{1,0:T(8,128)S(1)} %copy-done.68, bf16[1024,1024]{1,0:T(8,128)(2,1)S(1)} %get-tuple-element.130, bf16[1024,2432]{1,0:T(8,128)(2,1)} %collective-permute-done.6), kind=kOutput, calls=%fused_computation.46 | convolution fusion | flops 2148532224 | bytes 12582912 | tf_op jit(solution)/shard_map/dot_general | solution.py:28
  349.4 17.8 %scan_backward.6 = (bf16[1024,1024]{1,0:T(8,128)(2,1)S(1)}, f32[1024,256]{1,0:T(8,128)S(1)}, f32[1024,256]{1,0:T(8,128)S(1)}, f32[1,8,1024]{2,1,0:T(8,128)S(1)}, f32[8,512]{1,0:T(8,128)S(1)}) custom-call(s32[1]{0:T(128)S(6)} %copy.165.prefix_ref, bf16[1024,2048]{1,0:T(8,128)(2,1)S(1)} %copy-done.2, ...), custom_call_target="tpu_custom_call", output_to_operand_aliasing={{1}: (8, {}), {2}: (9, {})} | custom-call | tf_op jit(solution)/shard_map/scan_backward/pallas_call | solution.py:506
  367.1 17.5 %scan_backward.7 = (bf16[1024,1024]{1,0:T(8,128)(2,1)S(1)}, f32[1024,256]{1,0:T(8,128)S(1)}, f32[1024,256]{1,0:T(8,128)S(1)}, f32[1,8,1024]{2,1,0:T(8,128)S(1)}, f32[8,512]{1,0:T(8,128)S(1)}) custom-call(s32[1]{0:T(128)S(6)} %copy.165.prefix_ref, bf16[1024,2048]{1,0:T(8,128)(2,1)S(1)} %copy-done.2, ...), custom_call_target="tpu_custom_call", output_to_operand_aliasing={{1}: (8, {}), {2}: (9, {}), {0}: (10, {})} | custom-call | tf_op jit(solution)/shard_map/scan_backward/pallas_call | solution.py:506
  387.0 6.0 %convolution_convert_fusion.2 = bf16[1024,1024]{1,0:T(8,128)(2,1)} fusion(bf16[1024,1024]{1,0:T(8,128)(2,1)} %copy-done.29, bf16[1024,2048]{1,0:T(8,128)(2,1)} %copy-done.16), kind=kOutput, calls=%fused_computation.47 | convolution fusion | flops 2148532224 | bytes 6291456 | tf_op jit(solution)/shard_map/dot_general | solution.py:28
  402.6 6.6 %add_convert_fusion.5 = bf16[1024,1024]{1,0:T(8,128)(2,1)} fusion(bf16[1024,1024]{1,0:T(8,128)(2,1)} %collective-permute-done.14, bf16[1024,1024]{1,0:T(8,128)(2,1)} %copy-done.50, bf16[1024,1024]{1,0:T(8,128)(2,1)} %copy-done.29), kind=kOutput, calls=%fused_computation.25 | convolution fusion | flops 2150629376 | bytes 8388608 | tf_op jit(solution)/shard_map/dot_general | solution.py:28
  437.2 11.0 %collective-permute-done.16.refs_1_ = bf16[512,1024]{1,0:T(8,128)(2,1)} collective-permute-done((bf16[512,1024]{1,0:T(8,128)(2,1)}, bf16[512,1024]{1,0:T(8,128)(2,1)}, u32[]{:S(2)}, u32[]{:S(2)}) %collective-permute-start.16) | collective-permute-done | bytes 1048608 | tf_op jit(solution)/shard_map/ppermute | solution.py:726
  466.7 8.6 %collective-permute-done.17.refs_3_ = bf16[512,1024]{1,0:T(8,128)(2,1)} collective-permute-done((bf16[512,1024]{1,0:T(8,128)(2,1)}, bf16[512,1024]{1,0:T(8,128)(2,1)}, u32[]{:S(2)}, u32[]{:S(2)}) %collective-permute-start.17) | collective-permute-done | bytes 1048608 | tf_op jit(solution)/shard_map/ppermute | solution.py:726
  480.1 6.4 %finish.1 = f32[512,2048]{1,0:T(8,128)} custom-call(s32[16]{0:T(128)S(1)} %copy-done.40, s32[2]{0:T(128)S(1)} %copy-done.42, bf16[512,2048]{1,0:T(8,128)(2,1)S(1)} %copy-done.8, bf16[512,2048]{1,0:T(8,128)(2,1)S(1)} %copy-done.21, f32[1,2048]{1,0:T(1,128)S(1)} %bitcast.69, bf16[1024,1024]{1,0:T(8,128)(2,1)S(1)} %copy-done.14, ...), custom_call_target="tpu_custom_call" | custom-call | tf_op jit(solution)/shard_map/finish/pallas_call | solution.py:641
  (320 shorter events, 169.2 us)
Async XLA Ops:
  7.2 62.4 %copy-start.60 = (s32[8]{0:T(128)S(1)}, s32[8]{0:T(128)}, u32[]{:S(2)}) copy-start(s32[8]{0:T(128)} %constant.63) | copy-start | bytes 100
  7.2 62.4 %copy-start.61 = (s32[8]{0:T(128)S(1)}, s32[8]{0:T(128)}, u32[]{:S(2)}) copy-start(s32[8]{0:T(128)} %constant.62) | copy-start | bytes 100
  7.2 64.1 %copy-start.7 = (bf16[512,2048]{1,0:T(8,128)(2,1)S(1)}, bf16[512,2048]{1,0:T(8,128)(2,1)}, u32[]{:S(2)}) copy-start(bf16[512,2048]{1,0:T(8,128)(2,1)} %hidden_ref.3) | copy-start | bytes 6291460
  7.2 61.7 %all-gather.6.cloned.1.call-start = ((), (), s32[]{:S(2)}) async-start(), calls=%async_computation.6 | async-start | bytes 5603328 | tf_op jit(solution)/shard_map/all_gather | solution.py:734
  10.3 118.7 %all-gather.4.cloned.1.call-start = ((), (), s32[]{:S(2)}) async-start(), calls=%async_computation.5 | async-start | bytes 4718592 | tf_op jit(solution)/shard_map/all_gather | solution.py:734
  11.0 164.4 %all-gather.8.cloned.1.call-start = ((), (), s32[]{:S(2)}) async-start(), calls=%async_computation.7 | async-start | bytes 4718592 | tf_op jit(solution)/shard_map/all_gather | solution.py:734
  11.1 49.0 %collective-permute-start = (bf16[512,2048]{1,0:T(8,128)(2,1)}, bf16[512,2048]{1,0:T(8,128)(2,1)}, u32[]{:S(2)}, u32[]{:S(2)}) collective-permute-start(bf16[512,2048]{1,0:T(8,128)(2,1)} %hidden_ref.3), channel_id=1, source_target_pairs={{0,1},{1,0},{2,3},{3,2},{4,5},{5,4},{6,7},{7,6},{8,9},{9,8},{10,11... | collective-permute-start | bytes 6291464 | tf_op jit(solution)/shard_map/ppermute | solution.py:726
  17.4 1.2 collective-permute-start.1
  18.7 3.7 collective-permute-start.2
  22.4 3.8 collective-permute-start.3
  26.2 5.0 collective-permute-start.4
  68.9 16.1 %collective-permute-start.6 = (bf16[1024,2432]{1,0:T(8,128)(2,1)}, bf16[1024,2432]{1,0:T(8,128)(2,1)}, u32[]{:S(2)}, u32[]{:S(2)}) collective-permute-start(bf16[1024,2432]{1,0:T(8,128)(2,1)} %all-gather.6.cloned.1.call-done), channel_id=1, source_target_pairs={{0,2},{2,0},{4,6},{6,4},{8,10},{10,8},{12,14},{14,12},{16,18},{18,... | collective-permute-start | bytes 14942216 | tf_op jit(solution)/shard_map/ppermute | solution.py:722
  68.9 274.8 %reduce-scatter.6.cloned.1.call-start = ((), (), s32[]{:S(2)}) async-start(), calls=%async_computation.8 | async-start | bytes 4718592 | tf_op jit(solution)/shard_map/reduce_scatter | solution.py:749
  69.7 110.9 %copy-start.39 = (s32[16]{0:T(128)}, s32[16]{0:T(128)S(1)}, u32[]{:S(2)}) copy-start(s32[16]{0:T(128)S(1)} %pad_add_fusion.lanes_ref) | copy-start | bytes 196
  69.8 110.8 %copy-start.41 = (s32[2]{0:T(128)}, s32[2]{0:T(128)S(1)}, u32[]{:S(2)}) copy-start(s32[2]{0:T(128)S(1)} %pad_add_fusion.1.slots_ref) | copy-start | bytes 28
  69.8 57.9 %collective-permute-start.5 = (bf16[512,2048]{1,0:T(8,128)(2,1)}, bf16[512,2048]{1,0:T(8,128)(2,1)S(1)}, u32[]{:S(2)}, u32[]{:S(2)}) collective-permute-start(bf16[512,2048]{1,0:T(8,128)(2,1)} %cot_ref.1), channel_id=1, source_target_pairs={{0,1},{1,0},{2,3},{3,2},{4,5},{5,4},{6,7},{7,6},{8,9},{9,8},{10,11... | collective-permute-start | bytes 6291464 | tf_op jit(solution)/shard_map/ppermute | solution.py:726
  129.0 7.4 %collective-permute-start.7 = (bf16[1024,2048]{1,0:T(8,128)(2,1)}, bf16[1024,2048]{1,0:T(8,128)(2,1)S(1)}, u32[]{:S(2)}, u32[]{:S(2)}) collective-permute-start(bf16[1024,2048]{1,0:T(8,128)(2,1)} %all-gather.4.cloned.1.call-done), channel_id=1, source_target_pairs={{0,2},{2,0},{4,6},{6,4},{8,10},{10,8},{12,14},{14,12},{16,18},{18,... | collective-permute-start | bytes 12582920 | tf_op jit(solution)/shard_map/ppermute | solution.py:722
  175.4 28.8 %collective-permute-start.8 = (bf16[1024,2048]{0,1:T(8,128)(2,1)}, bf16[1024,2048]{0,1:T(8,128)(2,1)}, u32[]{:S(2)}, u32[]{:S(2)}) collective-permute-start(bf16[1024,2048]{0,1:T(8,128)(2,1)} %all-gather.8.cloned.1.call-done), channel_id=1, source_target_pairs={{0,2},{2,0},{4,6},{6,4},{8,10},{10,8},{12,14},{14,12},{16,18},{18,... | collective-permute-start | bytes 12582920 | tf_op jit(solution)/shard_map/ppermute | solution.py:722
  192.9 25.3 %collective-permute-start.9 = (bf16[1024,2048]{1,0:T(8,128)(2,1)}, bf16[1024,2048]{1,0:T(8,128)(2,1)}, u32[]{:S(2)}, u32[]{:S(2)}) collective-permute-start(bf16[1024,2048]{1,0:T(8,128)(2,1)} %convolution_convert_fusion.1), channel_id=1, source_target_pairs={{0,2},{2,0},{4,6},{6,4},{8,10},{10,8},{12,14},{14,12},{16,18},{18,... | collective-permute-start | bytes 12582920 | tf_op jit(solution)/shard_map/ppermute | solution.py:722
  228.8 158.2 %reduce-scatter.8.cloned.1.call-start = ((), (), s32[]{:S(2)}) async-start(), calls=%async_computation.9 | async-start | bytes 4718592 | tf_op jit(solution)/shard_map/reduce_scatter | solution.py:749
  255.2 14.4 %collective-permute-start.10 = (bf16[1024,2048]{1,0:T(8,128)(2,1)S(1)}, bf16[1024,2048]{1,0:T(8,128)(2,1)S(1)}, u32[]{:S(2)}, u32[]{:S(2)}) collective-permute-start(bf16[1024,2048]{1,0:T(8,128)(2,1)S(1)} %convolution_convert_fusion), channel_id=1, source_target_pairs={{0,2},{2,0},{4,6},{6,4},{8,10},{10,8},{12,14},{14,12},{16,18},{18,... | collective-permute-start | bytes 12582920 | tf_op jit(solution)/shard_map/ppermute | solution.py:722
  276.0 111.0 %reduce-scatter.10.cloned.1.call-start = ((), (), s32[]{:S(2)}) async-start(), calls=%async_computation.10 | async-start | bytes 2359296 | tf_op jit(solution)/shard_map/reduce_scatter | solution.py:749
  277.7 26.2 %collective-permute-start.11 = (bf16[512,1024]{1,0:T(8,128)(2,1)S(1)}, bf16[512,1024]{1,0:T(8,128)(2,1)S(1)}, u32[]{:S(2)}, u32[]{:S(2)}) collective-permute-start(bf16[512,1024]{1,0:T(8,128)(2,1)S(1)} %constant_dynamic-slice_fusion.3), channel_id=1, source_target_pairs={{0,1},{1,0},{2,3},{3,2},{4,5},{5,4},{6,7},{7,6},{8,9},{9,8},{10,11... | collective-permute-start | bytes 3145736 | tf_op jit(solution)/shard_map/ppermute | solution.py:726
  280.9 43.9 %collective-permute-start.12 = (bf16[512,1024]{1,0:T(8,128)(2,1)S(1)}, bf16[512,1024]{1,0:T(8,128)(2,1)S(1)}, u32[]{:S(2)}, u32[]{:S(2)}) collective-permute-start(bf16[512,1024]{1,0:T(8,128)(2,1)S(1)} %constant_dynamic-slice_fusion.2), channel_id=1, source_target_pairs={{0,1},{1,0},{2,3},{3,2},{4,5},{5,4},{6,7},{7,6},{8,9},{9,8},{10,11... | collective-permute-start | bytes 3145736 | tf_op jit(solution)/shard_map/ppermute | solution.py:726
  327.2 12.7 %collective-permute-start.13 = (bf16[1024,1024]{1,0:T(8,128)(2,1)S(1)}, bf16[1024,1024]{1,0:T(8,128)(2,1)S(1)}, u32[]{:S(2)}, u32[]{:S(2)}) collective-permute-start(bf16[1024,1024]{1,0:T(8,128)(2,1)S(1)} %convolution_convert_fusion.3), channel_id=1, source_target_pairs={{0,2},{2,0},{4,6},{6,4},{8,10},{10,8},{12,14},{14,12},{16,18},{18,... | collective-permute-start | bytes 6291464 | tf_op jit(solution)/shard_map/ppermute | solution.py:722
  343.7 104.5 %reduce-scatter.12.cloned.1.call-start = ((), (), s32[]{:S(2)}) async-start(), calls=%async_computation.11 | async-start | bytes 2359296 | tf_op jit(solution)/shard_map/reduce_scatter | solution.py:749
  393.0 9.5 %collective-permute-start.14 = (bf16[1024,1024]{1,0:T(8,128)(2,1)}, bf16[1024,1024]{1,0:T(8,128)(2,1)}, u32[]{:S(2)}, u32[]{:S(2)}) collective-permute-start(bf16[1024,1024]{1,0:T(8,128)(2,1)} %convolution_convert_fusion.2), channel_id=1, source_target_pairs={{0,2},{2,0},{4,6},{6,4},{8,10},{10,8},{12,14},{14,12},{16,18},{18,... | collective-permute-start | bytes 6291464 | tf_op jit(solution)/shard_map/ppermute | solution.py:722
  409.2 78.4 %reduce-scatter.14.cloned.1.call-start = ((), (), s32[]{:S(2)}) async-start(), calls=%async_computation.12 | async-start | bytes 1363968 | tf_op jit(solution)/shard_map/reduce_scatter | solution.py:749
  413.9 20.5 %collective-permute-start.15 = (f32[1024,295]{0,1:T(8,128)}, f32[1024,295]{0,1:T(8,128)}, u32[]{:S(2)}, u32[]{:S(2)}) collective-permute-start(f32[1024,295]{0,1:T(8,128)} %pad_maximum_fusion), channel_id=1, source_target_pairs={{0,2},{2,0},{4,6},{6,4},{8,10},{10,8},{12,14},{14,12},{16,18},{18,... | collective-permute-start | bytes 3624968 | tf_op jit(solution)/shard_map/ppermute | solution.py:722
  422.5 25.6 %collective-permute-start.16 = (bf16[512,1024]{1,0:T(8,128)(2,1)}, bf16[512,1024]{1,0:T(8,128)(2,1)}, u32[]{:S(2)}, u32[]{:S(2)}) collective-permute-start(bf16[512,1024]{1,0:T(8,128)(2,1)} %constant_dynamic-slice_fusion.1), channel_id=1, source_target_pairs={{0,1},{1,0},{2,3},{3,2},{4,5},{5,4},{6,7},{7,6},{8,9},{9,8},{10,11... | collective-permute-start | bytes 3145736 | tf_op jit(solution)/shard_map/ppermute | solution.py:726
  450.5 24.8 %collective-permute-start.17 = (bf16[512,1024]{1,0:T(8,128)(2,1)}, bf16[512,1024]{1,0:T(8,128)(2,1)}, u32[]{:S(2)}, u32[]{:S(2)}) collective-permute-start(bf16[512,1024]{1,0:T(8,128)(2,1)} %constant_dynamic-slice_fusion), channel_id=1, source_target_pairs={{0,1},{1,0},{2,3},{3,2},{4,5},{5,4},{6,7},{7,6},{8,9},{9,8},{10,11... | collective-permute-start | bytes 3145736 | tf_op jit(solution)/shard_map/ppermute | solution.py:726
  491.3 5.1 %collective-permute-start.18 = (f32[32960]{0:T(1024)S(1)}, f32[32960]{0:T(1024)S(1)}, u32[]{:S(2)}, u32[]{:S(2)}) collective-permute-start(f32[32960]{0:T(1024)S(1)} %pad_maximum_fusion.1), channel_id=1, source_target_pairs={{0,1},{1,0},{2,3},{3,2},{4,5},{5,4},{6,7},{7,6},{8,9},{9,8},{10,11... | collective-permute-start | bytes 395528 | tf_op jit(solution)/shard_map/ppermute | solution.py:726
  (66 other events, 582.6 us)
Sparse Core Ops, SparseCore 0:
  10.4 58.4 all-gather.5
  70.4 47.9 all-gather.3
  119.8 55.5 all-gather.7
  228.9 47.1 reduce-scatter.5
  278.3 48.4 reduce-scatter.7
  343.8 31.2 reduce-scatter.9
  409.3 31.2 reduce-scatter.11
  448.3 28.1 reduce-scatter.13
where the time goes:
time: 515 us; the launch traced here: 506 us
  matrix products  172 us (33%)
  Pallas kernels  121 us (23%)
  waiting for transfers between devices  91.8 us (18%)
  local copies, waits for them, and re-layouts  63.6 us (12%)
  starting transfers between devices  19.7 us (4%)
  between operations  16.3 us (3%)
  other arithmetic  12.1 us (2%)
  blocking collectives  9.83 us (2%)
    dot_general x28, matrix products, dot(): return lax.dot_general(a, b, (dims, ((), ())), preferred_element_type=F32)  172 us
    pallas_call x4, Pallas kernels, scan_backward(): pl.pallas_call(functools.partial(backward_kernel, channels // P_SIZE, gro...  70.3 us
    ppermute x7, waiting for transfers between devices, other_half(): return lax.ppermute(v, 'tp', [(0, 1), (1, 0)])  50.5 us
    unnamed x153, local copies, waits for them, and re-layouts  38.4 us
    pallas_call x4, Pallas kernels, scan_forward(): pl.pallas_call(functools.partial(forward_kernel, channels // P_SIZE, grou...  27.3 us
    all_gather x3, waiting for transfers between devices, gather(): lax.all_gather(v, 'fsdp', axis=0, tiled=True, axis_index_groups=chip_grou...  26.3 us
    ppermute x7, starting transfers between devices, other_half(): return lax.ppermute(v, 'tp', [(0, 1), (1, 0)])  11.9 us
    pallas_call x2, Pallas kernels, own_rows(): pl.pallas_call(kernel, grid_spec=pltpu.PrefetchScalarGridSpec(num_scalar_...  10.3 us
  transfers between devices with their start and end apart: 27, of which 13 were waited for; matrix products, arithmetic and copies ran while one was open for 36% of the time, Pallas kernels for 24%

commit v1 on v0

--- a/solution.py
+++ b/solution.py
@@ -644,7 +644,7 @@
             num_scalar_prefetch=2, grid=(tiles,), in_specs=specs, out_specs=tile
         ),
         out_shape=jax.ShapeDtypeStruct((tokens, width), F32),
-        compiler_params=pltpu.CompilerParams(vmem_limit_bytes=40 * MIB),
+        compiler_params=pltpu.CompilerParams(vmem_limit_bytes=60 * MIB),
         cost_estimate=NO_COST,
         name=name,
     )(lanes, slots, *given)
@@ -707,6 +707,85 @@
         cost_estimate=NO_COST,
         name="post",
     )(rest_pre, bc_taps, log_decay[None], dt_bias[None], grad_act, gcols, *grows)
+
+
+def gate_kernel(a_ref, own_ref, other_ref, ssd_ref, gain_ref, gate_ref, out_ref, square_ref):
+    depth = own_ref.shape[0]
+    gain = gain_ref[...]
+
+    @pl.when(pl.program_id(0) == 0)
+    def _():
+        square_ref[...] = jnp.zeros_like(square_ref)
+
+    for m in range(0, a_ref.shape[0], 256):
+        here = slice(m, m + 256)
+        z = dot(a_ref[here, :depth], own_ref[...]) + dot(a_ref[here, depth:], other_ref[...])
+        gated = ssd_ref[here, :].astype(F32) * (z * sig(z))
+        gate_ref[here, :] = low(z)
+        out_ref[here, :] = low(gated * gain)
+        square = gated * gated
+        square_ref[here, :] += sum(square[:, k : k + 128] for k in range(0, CG, 128))
+
+
+def gate_product(normed, own, other, ssd_out, gain):
+    tokens, width = normed.shape
+    channels = ssd_out.shape[1]
+    tall = pl.BlockSpec((tokens, CG), lambda j: (0, j))
+    deep = pl.BlockSpec((width // 2, CG), lambda j: (0, j))
+    return pl.pallas_call(
+        gate_kernel,
+        grid=(channels // CG,),
+        in_specs=[
+            pl.BlockSpec((tokens, width), lambda j: (0, 0)), deep, deep, tall, pl.BlockSpec((1, CG), lambda j: (0, j)),
+        ],
+        out_specs=[tall, tall, pl.BlockSpec((tokens, 128), lambda j: (0, 0))],
+        out_shape=(
+            jax.ShapeDtypeStruct((tokens, channels), BF16),
+            jax.ShapeDtypeStruct((tokens, channels), BF16),
+            jax.ShapeDtypeStruct((tokens, 128), F32),
+        ),
+        compiler_params=pltpu.CompilerParams(vmem_limit_bytes=40 * MIB),
+        cost_estimate=NO_COST,
+        name="gate_product",
+    )(normed, own, other, ssd_out, gain)
+
+
+def gating_kernel(a_ref, own_ref, other_ref, gate_ref, ssd_ref, coef_ref, gain_ref, ggate_ref, dy_ref):
+    depth = own_ref.shape[0]
+    gain = gain_ref[...]
+    for m in range(0, a_ref.shape[0], 256):
+        here = slice(m, m + 256)
+        scaled = dot(a_ref[here, :depth], own_ref[...]) + dot(a_ref[here, depth:], other_ref[...])
+        z = gate_ref[here, :].astype(F32)
+        y = ssd_ref[here, :].astype(F32)
+        s = sig(z)
+        act = z * s
+        grad = gain * scaled - y * act * coef_ref[here, :]
+        ggate_ref[here, :] = low(grad * y * (s + act * (1.0 - s)))
+        dy_ref[here, :] = low(grad * act)
+
+
+def gating_product(cot, own, other, gate, ssd_out, coef, gain):
+    tokens, width = cot.shape
+    channels = ssd_out.shape[1]
+    tall = pl.BlockSpec((tokens, CG), lambda j: (0, j))
+    deep = pl.BlockSpec((width // 2, CG), lambda j: (0, j))
+    return pl.pallas_call(
+        gating_kernel,
+        grid=(channels // CG,),
+        in_specs=[
+            pl.BlockSpec((tokens, width), lambda j: (0, 0)), deep, deep, tall, tall,
+            pl.BlockSpec((tokens, 1), lambda j: (0, 0)), pl.BlockSpec((1, CG), lambda j: (0, j)),
+        ],
+        out_specs=[tall, tall],
+        out_shape=(
+            jax.ShapeDtypeStruct((tokens, channels), BF16),
+            jax.ShapeDtypeStruct((tokens, channels), BF16),
+        ),
+        compiler_params=pltpu.CompilerParams(vmem_limit_bytes=40 * MIB),
+        cost_estimate=NO_COST,
+        name="gating_product",
+    )(cot, own, other, gate, ssd_out, coef, gain)
 
 
 def snake(devices):
@@ -863,18 +942,18 @@
     (z_own, cot_parts[-1]), ssd_out = tie((z_own, cot_parts[-1]), ssd_out)
     z_other = other_core(z_own, fsdp)
 
-    gate_pre = dot(na, z_own) + dot(nb, z_other)
-    gated = ssd_out.astype(F32) * (gate_pre * sig(gate_pre))
-    square_sum = lax.psum(jnp.sum(gated * gated, axis=-1), "tp")
-    gate_low = low(gate_pre)
-    scaled_out = low(gated * gain)
-    out_own, scaled_out = tie(out_own, scaled_out)
-    out_other = other_core(out_own, fsdp)
+    gate_low, scaled_out, square = gate_product(normed, z_own, z_other, ssd_out, gain)
+    square_sum = lax.psum(jnp.sum(square, axis=-1), "tp")
 
     inv_gate = lax.rsqrt(square_sum / all_channels + EPSILON)[:, None]
     cot_rel = place_tokens(lanes, slots, cot_parts, inv_gate, False)
     ca, cb = cot_rel[:, :half_width], cot_rel[:, half_width:]
-    gout_came = other_core(low(dot(cb, scaled_out, TN)), fsdp)
+    gout_other = low(dot(cb, scaled_out, TN))
+    gout_came = other_core(gout_other, fsdp)
+    gout_sum = low(dot(ca, scaled_out, TN) + gout_came.astype(F32))
+    (scaled_out, out_own), gout_sum = tie((scaled_out, out_own), gout_sum)
+    grad_out = scatter(gout_sum, fsdp)
+    out_other = other_core(out_own, fsdp)
 
     branch, along = [], 0.0
     for cot_half, out_half in ((ca, out_own), (cb, out_other)):
@@ -883,10 +962,7 @@
         branch.append(low(v * inv_gate))
     along = lax.psum(along, "tp")
     coef = inv_gate * inv_gate * (along / all_channels)[:, None]
-    scaled_out, coef = tie(scaled_out, coef)
-    gout_sum = low(dot(ca, scaled_out, TN) + gout_came.astype(F32))
-    (coef, branch), gout_sum = tie((coef, branch), gout_sum)
-    grad_out = scatter(gout_sum, fsdp)
+    coef, branch = tie(coef, branch)
 
     def to_own_tokens(v):
         if tp == 2:
@@ -898,19 +974,11 @@
     kinds = [[whole for _, whole in half] for half in branch_parts]
     branch_parts = [[v for v, _ in half] for half in branch_parts]
 
-    scaled = dot(ca, out_own) + dot(cb, out_other)
-    z = gate_low.astype(F32)
-    s = sig(z)
-    gate_act = z * s
-    y = ssd_out.astype(F32)
-    gated = y * gate_act
-    ggain = jnp.sum(scaled * gated, axis=0)
-    grad_gated = gain * scaled - gated * coef
-    ggate = low(grad_gated * y * (s + gate_act * (1.0 - s)))
-    dy = low(grad_gated * gate_act)
+    ggate, dy = gating_product(cot_rel, out_own, out_other, gate_low, ssd_out, coef, gain)
     gz_came = other_core(low(dot(nb, ggate, TN)), fsdp)
     z_parts = [dot(ggate, z_own, NT), dot(ggate, z_other, NT)]
-    na, z_parts = tie(na, z_parts)
+    normed, z_parts = tie(normed, z_parts)
+    na, nb = normed[:, :half_width], normed[:, half_width:]
     gz_sum = low(dot(na, ggate, TN) + gz_came.astype(F32))
     dy, gz_sum = tie(dy, gz_sum)
     grad_z = scatter(gz_sum, fsdp)
@@ -922,8 +990,6 @@
     def back_through(start, stop, dy, before):
         gx = None
         for g in range(start, stop):
-            if g == 1:
-                dy, branch_parts[0] = tie(dy, branch_parts[0])
             gx, gact, gcol, grow, gsum = scan_backward(
                 prefix, x_pre, dy, x_taps, skip, cols, head_rows, act, g, g - start, stop - start, gx, before
             )
@@ -935,31 +1001,27 @@
     grad_x = []
     if first:
         gx, before = back_through(0, first, dy, before)
-        gx, branch_parts[1] = tie(gx, branch_parts[1])
+        gx, (branch_parts, grad_out, grad_z) = tie(gx, (branch_parts, grad_out, grad_z))
         came = other_core(low(dot(nb, gx, TN)), fsdp)
         z_parts = [
             v + dot(gx, half[:, : first * CG], NT) for v, half in zip(z_parts, (x_own, x_other))
         ]
-        na, z_parts = tie(na, z_parts)
+        normed, z_parts = tie(normed, z_parts)
+        na, nb = normed[:, :half_width], normed[:, half_width:]
         total = low(dot(na, gx, TN) + came.astype(F32))
-        dy, (total, grad_out) = tie(dy, (total, grad_out))
+        dy, total = tie(dy, total)
         grad_x.append(scatter(total, fsdp))
     gx, before = back_through(first, groups, dy, before)
     gx, (grad_z, *grad_x) = tie(gx, (grad_z, *grad_x))
-    gx_other = low(dot(nb, gx, TN))
-    came = other_core(gx_other, fsdp)
-    before, gx_other = tie(before, gx_other)
+    g_gain = jnp.sum(out_weight.T.astype(F32) * grad_out.astype(F32), axis=0) / gain[0]
+    g_gain = jnp.transpose(g_gain.reshape(heads, fsdp, -1), (1, 0, 2))
+    grad_x = list(grad_x)
+    late = slice(first * CG, channels)
     grest, gbc_taps, ghead = post(rest_pre, bc_taps, log_decay, dt_bias, before[0], before[1], grows)
-    na, grest = tie(na, grest)
-    gx_sum = low(dot(na, gx, TN) + came.astype(F32))
-    (gx, grest, ghead), gx_sum = tie((gx, grest, ghead), gx_sum)
-    grad_x = list(grad_x)
-    grad_x.append(scatter(gx_sum, fsdp))
 
     gsum = jnp.concatenate(gsums, axis=1)
     gx_taps = jnp.transpose(gsum[0:4].reshape(4, heads, fsdp, taps_own), (2, 1, 0, 3))
     g_taps = jnp.transpose(gbc_taps[0:4].reshape(4, fsdp, -1), (1, 0, 2))
-    g_gain = jnp.transpose(ggain.reshape(heads, fsdp, -1), (1, 0, 2))
     g_skip = jnp.sum(gsum[4].reshape(heads, P_SIZE), axis=-1)
     per_head = jnp.concatenate([ghead[0, :heads], ghead[1, :heads], g_skip])
     slices = jnp.concatenate(
@@ -976,64 +1038,72 @@
     lines_own, lines_other = [
         jnp.pad(v, ((0, 0), (0, lone * rows - size))).reshape(half_width, lone) for v in to_cores(slices)
     ]
-    rest_came = other_core(jnp.concatenate([dot(nb, grest, TN), lines_other], axis=1), fsdp)
-
-    def part_of(v, x_half, r_half):
-        return low(v + dot(gx, x_half[:, first * CG : channels], NT) + dot(grest, r_half, NT))
-
-    part_sums = [to_own_tokens(part_of(z_parts[0], x_own, rest_own))]
+    rest_leaves = jnp.concatenate([dot(nb, grest, TN), lines_other], axis=1)
+    rest_came = other_core(rest_leaves, fsdp)
+    gx, rest_leaves = tie(gx, rest_leaves)
+    gx_other = low(dot(nb, gx, TN))
+    came = other_core(gx_other, fsdp)
+    (grest, gx), gx_other = tie((grest, gx), gx_other)
+    rest_sum = jnp.concatenate([dot(na, grest, TN), lines_own], axis=1) + rest_came
+    (grest, gx), rest_sum = tie((grest, gx), rest_sum)
+    mine_rest = scatter(rest_sum, fsdp)
+
+    def first_part(v, x_half):
+        return v + dot(gx, x_half[:, late], NT)
+
+    part = low(first_part(z_parts[0], x_own) + dot(grest, rest_own, NT))
+    part_sums = [to_own_tokens(part)]
     kinds_part = [whole for _, whole in part_sums[0]]
-    gx, first_part = tie(gx, part_sums[0][0][0])
-    arrived = [first_part] + [v for v, _ in part_sums[0][1:]]
-    second = part_of(z_parts[1], x_other, rest_other)
-    part_sums.append(to_own_tokens(second))
-    rest_sum = jnp.concatenate([dot(na, grest, TN), lines_own], axis=1) + rest_came
-    rest_sum, arrived, second, grad_x[-1] = lax.optimization_barrier(
-        (rest_sum, arrived, second, grad_x[-1])
-    )
-    part_sums[0] = list(zip(arrived, kinds_part))
-    mine_rest = scatter(rest_sum, fsdp)
-
+    gx, part = tie(gx, part)
+    gx_sum = low(dot(na, gx, TN) + came.astype(F32))
+    gx, gx_sum = tie(gx, gx_sum)
+    grad_x.append(scatter(gx_sum, fsdp))
+    second = first_part(z_parts[1], x_other)
+    (branch_parts, grad_out, grad_z), part = tie((branch_parts, grad_out, grad_z), part)
     mixed = from_ring(
         own_rows(
             mixed_kernel, "add_branch", lanes, slots, to_ring(hidden), [], None,
             [list(zip(half, kind)) for half, kind in zip(branch_parts, kinds)],
         )
     )
+    grad_z, grad_out = grad_z.astype(F32), grad_out.astype(F32).T
+    arrived = [v for v, _ in part_sums[0]]
+    second, (arrived, mixed, grad_out, grad_z) = tie(second, (arrived, mixed, grad_out, grad_z))
+    part_sums[0] = list(zip(arrived, kinds_part))
+    part_sums.append(to_own_tokens(low(second + dot(grest, rest_other, NT))))
+
+    def over_tp(v):
+        return v + other_half(v) if tp == 2 else lax.psum(v, "tp")
+
+    grad_bc, grad_dt = mine_rest[:, : 2 * N], mine_rest[:, 2 * N : 2 * N + heads]
+    lines = mine_rest[:, 2 * N + heads :].reshape(-1)
+    n_taps, bc_size = bc_conv.size, rows * 2 * N
+    at = [n_taps]
+    for size in (x_conv.size, gate_gain.size, heads, heads, heads):
+        at.append(at[-1] + size)
+    gx_taps = lines[at[0] : at[1]].reshape(x_conv.shape)
+    g_gain = lines[at[1] : at[2]].reshape(gate_gain.shape)
+    g_decay, g_bias, g_skip = [lines[at[k] : at[k + 1]] for k in (2, 3, 4)]
+
+    def weighted(w, g):
+        return jnp.sum(w.astype(F32) * g.astype(F32), axis=1)
+
+    grad_gain = weighted(z_weight, grad_z) + weighted(bc_weight, grad_bc) + weighted(dt_weight, grad_dt)
+    last, whole = part_sums[1][-1]
+    last, (mixed, grad_gain, grad_out, grad_z) = tie(last, (mixed, grad_gain, grad_out, grad_z))
+    part_sums[1][-1] = (last, whole)
     grad_hidden = from_ring(
         own_rows(finish_kernel, "finish", lanes, slots, to_ring(hidden), [to_ring(cotangent)], norm_gain, part_sums)
     )
-
-    grad_z, grad_out = grad_z.astype(F32), grad_out.astype(F32).T
     grad_x = jnp.concatenate(grad_x, axis=1).astype(F32)
-    grad_bc, grad_dt = mine_rest[:, : 2 * N], mine_rest[:, 2 * N : 2 * N + heads]
-    lines = mine_rest[:, 2 * N + heads :].reshape(-1)
-    grad_gain = sum(
-        jnp.sum(w.astype(F32) * g, axis=1)
-        for w, g in ((z_weight, grad_z), (x_weight, grad_x), (bc_weight, grad_bc), (dt_weight, grad_dt))
-    ) / input_norm_gain.astype(F32)
-    n_taps = bc_conv.size
-    together = jnp.concatenate([grad_bc.reshape(-1), grad_gain, lines[:n_taps]])
-    together = together + other_half(together) if tp == 2 else lax.psum(together, "tp")
-    bc_size = rows * 2 * N
-    at = [n_taps]
-    for size in (x_conv.size, gate_gain.size, heads, heads, heads):
-        at.append(at[-1] + size)
+    grad_gain = (grad_gain + weighted(x_weight, grad_x)) / input_norm_gain.astype(F32)
+    together = over_tp(jnp.concatenate([grad_bc.reshape(-1), lines[:n_taps], grad_gain]))
+    grad_bc = together[:bc_size].reshape(rows, 2 * N)
+    g_taps = together[bc_size : bc_size + n_taps].reshape(bc_conv.shape)
+    grad_gain = together[bc_size + n_taps :]
     return (
-        mixed,
-        grad_hidden,
-        together[bc_size : bc_size + rows],
-        grad_z,
-        grad_x,
-        together[:bc_size].reshape(rows, 2 * N),
-        grad_dt,
-        lines[at[0] : at[1]].reshape(x_conv.shape),
-        together[bc_size + rows :].reshape(bc_conv.shape),
-        lines[at[2] : at[3]],
-        lines[at[3] : at[4]],
-        lines[at[4] : at[5]],
-        lines[at[1] : at[2]].reshape(gate_gain.shape),
-        grad_out,
+        mixed, grad_hidden, grad_gain, grad_z, grad_x, grad_bc, grad_dt, gx_taps, g_taps, g_decay, g_bias,
+        g_skip, g_gain, grad_out,
     )
 
 

time: 515 us -> 497 us (0.965)
  matrix products: 172 us -> 119 us
  Pallas kernels: 121 us -> 156 us
  other arithmetic: 12.1 us -> 19.4 us
  waiting for transfers between devices: 91.8 us -> 85.6 us
    dot_general x28 -> x24, matrix products: 172 us -> 119 us  [dot(): return lax.dot_general(a, b, (dims, ((), ())), preferred_element_type=F32)]
    pallas_call x0 -> x2, Pallas kernels: none -> 31 us  [the longest x1 16 us: gating_product(): pl.pallas_call(gating_kernel, grid=(channels // CG,), in_specs=[pl.BlockS...]
    all_gather x3, waiting for transfers between devices: 26.3 us -> 9.57 us  [gather(): lax.all_gather(v, 'fsdp', axis=0, tiled=True, axis_index_groups=chip_grou...]
    ppermute x8, waiting for transfers between devices: 7.16 us -> 13.4 us  [other_core(): return lax.ppermute(v, 'fsdp', [(i, i ^ 1) for i in range(devices)])]
    ppermute x7, waiting for transfers between devices: 50.5 us -> 55.7 us  [other_half(): return lax.ppermute(v, 'tp', [(0, 1), (1, 0)])]
    unnamed x153 -> x128, local copies, waits for them, and re-layouts: 38.4 us -> 34.9 us
  transfers between devices with their start and end apart: 27 -> 27, of which waited for: 13 -> 11; matrix products, arithmetic and copies ran while one was open for 36% -> 32% of each run, Pallas kernels for 24% -> 32%
where the time goes in v1:
time: 497 us; the launch traced here: 487 us
  Pallas kernels  156 us (31%)
  matrix products  119 us (24%)
  waiting for transfers between devices  85.6 us (17%)
  local copies, waits for them, and re-layouts  62.6 us (13%)
  other arithmetic  19.4 us (4%)
  starting transfers between devices  17.9 us (4%)
  between operations  16.4 us (3%)
  blocking collectives  9.88 us (2%)
    dot_general x24, matrix products, dot(): return lax.dot_general(a, b, (dims, ((), ())), preferred_element_type=F32)  119 us
    pallas_call x4, Pallas kernels, scan_backward(): pl.pallas_call(functools.partial(backward_kernel, channels // P_SIZE, gro...  70.5 us
    ppermute x7, waiting for transfers between devices, other_half(): return lax.ppermute(v, 'tp', [(0, 1), (1, 0)])  55.7 us
    unnamed x128, local copies, waits for them, and re-layouts  34.9 us
    pallas_call x4, Pallas kernels, scan_forward(): pl.pallas_call(functools.partial(forward_kernel, channels // P_SIZE, grou...  27.2 us
    pallas_call x1, Pallas kernels, gating_product(): pl.pallas_call(gating_kernel, grid=(channels // CG,), in_specs=[pl.BlockS...  16 us
    pallas_call x1, Pallas kernels, gate_product(): pl.pallas_call(gate_kernel, grid=(channels // CG,), in_specs=[pl.BlockSpe...  15 us
    pallas_call x2, Pallas kernels, own_rows(): pl.pallas_call(kernel, grid_spec=pltpu.PrefetchScalarGridSpec(num_scalar_...  14.7 us
  transfers between devices with their start and end apart: 27, of which 11 were waited for; matrix products, arithmetic and copies ran while one was open for 32% of the time, Pallas kernels for 32%

profile of v1, /device:TPU:0, one launch (start us, length us, event | category | flops | bytes accessed | tf_op | source)
XLA Modules:
  0.0 486.9 jit_solution(9559126980476793435)
XLA Ops:
  32.9 26.4 %collective-permute-done.refs_1_ = bf16[512,2048]{1,0:T(8,128)(2,1)} collective-permute-done((bf16[512,2048]{1,0:T(8,128)(2,1)}, bf16[512,2048]{1,0:T(8,128)(2,1)}, u32[]{:S(2)}, u32[]{:S(2)}) %collective-permute-start) | collective-permute-done | bytes 2097184 | tf_op jit(solution)/shard_map/ppermute | solution.py:805
  59.3 9.6 %all-gather.4.cloned.1.call-done = bf16[1024,2432]{1,0:T(8,128)(2,1)} async-done(((bf16[128,2432]{1,0:T(8,128)(2,1)}), bf16[1024,2432]{1,0:T(8,128)(2,1)}) %all-gather.4.cloned.1.call-update) | async-done | bytes 4980752 | tf_op jit(solution)/shard_map/all_gather | solution.py:813
  71.2 5.6 %place_tokens.2.a_ref = bf16[1024,2048]{1,0:T(8,128)(2,1)S(1)} custom-call(s32[16]{0:T(128)S(1)} %pad_add_fusion.lanes_ref, s32[2]{0:T(128)S(1)} %pad_add_fusion.1.slots_ref, bf16[512,2048]{1,0:T(8,128)(2,1)S(1)} %copy-done.7, bf16[512,2048]{1,0:T(8,128)(2,1)} %collective-permute-done.refs_1_, f32[1,2048]{1,0:T(1,128)S(1)} %bitcast.60), custom_call_target="tpu_custom_call" | custom-call | tf_op jit(solution)/shard_map/place_tokens/pallas_call | solution.py:578
  88.0 7.1 %add_convert_fusion.2.x_ref = bf16[1024,2048]{1,0:T(8,128)(2,1)S(1)} fusion(f32[1024,2048]{1,0:T(8,128)S(1)} %fusion.2, bf16[1024,2432]{1,0:T(8,128)(2,1)} %collective-permute-done.6, bf16[1024,2048]{1,0:T(8,128)(2,1)S(1)} %place_tokens.2.a_ref), kind=kOutput, calls=%fused_computation.2 | convolution fusion | flops 4299161600 | bytes 18874368 | tf_op jit(solution)/shard_map/dot_general | solution.py:28
  95.1 6.8 %scan_forward.4.refs_0_ = bf16[1024,2048]{1,0:T(8,128)(2,1)S(1)} custom-call(s32[1]{0:T(128)S(6)} %copy.173.prefix_ref, bf16[1024,2048]{1,0:T(8,128)(2,1)S(1)} %add_convert_fusion.2.x_ref, f32[4,2048]{1,0:T(4,128)S(1)} %reshape.148.taps_ref, f32[1,2048]{1,0:T(1,128)S(1)} %broadcast_in_dim_reshape.3.skip_ref, f32[1024,128]{1,0:T(8,128)S(1)} %get-tuple-element.119.cols_ref, ...), custom_call_target="tpu_custom_call" | custom-call | tf_op jit(solution)/shard_map/scan_forward/pallas_call | solution.py:251
  101.9 6.6 %scan_forward.5.refs_0_ = bf16[1024,2048]{1,0:T(8,128)(2,1)S(1)} custom-call(s32[1]{0:T(128)S(6)} %copy.173.prefix_ref, bf16[1024,2048]{1,0:T(8,128)(2,1)S(1)} %add_convert_fusion.2.x_ref, f32[4,2048]{1,0:T(4,128)S(1)} %reshape.148.taps_ref, f32[1,2048]{1,0:T(1,128)S(1)} %broadcast_in_dim_reshape.3.skip_ref, ...), custom_call_target="tpu_custom_call", output_to_operand_aliasing={{}: (7, {})} | custom-call | tf_op jit(solution)/shard_map/scan_forward/pallas_call | solution.py:251
  108.5 7.1 %scan_forward.6.refs_0_ = bf16[1024,2048]{1,0:T(8,128)(2,1)S(1)} custom-call(s32[1]{0:T(128)S(6)} %copy.173.prefix_ref, bf16[1024,2048]{1,0:T(8,128)(2,1)S(1)} %add_convert_fusion.2.x_ref, f32[4,2048]{1,0:T(4,128)S(1)} %reshape.148.taps_ref, f32[1,2048]{1,0:T(1,128)S(1)} %broadcast_in_dim_reshape.3.skip_ref, ...), custom_call_target="tpu_custom_call", output_to_operand_aliasing={{}: (7, {})} | custom-call | tf_op jit(solution)/shard_map/scan_forward/pallas_call | solution.py:251
  115.7 6.7 %scan_forward.7.ssd_ref = bf16[1024,2048]{1,0:T(8,128)(2,1)S(1)} custom-call(s32[1]{0:T(128)S(6)} %copy.173.prefix_ref, bf16[1024,2048]{1,0:T(8,128)(2,1)S(1)} %add_convert_fusion.2.x_ref, f32[4,2048]{1,0:T(4,128)S(1)} %reshape.148.taps_ref, f32[1,2048]{1,0:T(1,128)S(1)} %broadcast_in_dim_reshape.3.skip_ref, ...), custom_call_target="tpu_custom_call", output_to_operand_aliasing={{}: (7, {})} | custom-call | tf_op jit(solution)/shard_map/scan_forward/pallas_call | solution.py:251
  127.1 6.2 %collective-permute-done.7.other_ref = bf16[1024,2048]{1,0:T(8,128)(2,1)} collective-permute-done((bf16[1024,2048]{1,0:T(8,128)(2,1)}, bf16[1024,2048]{1,0:T(8,128)(2,1)}, u32[]{:S(2)}, u32[]{:S(2)}) %collective-permute-start.7) | collective-permute-done | bytes 4194336 | tf_op jit(solution)/shard_map/ppermute | solution.py:801
  135.5 15.0 %gate_product.1 = (bf16[1024,2048]{1,0:T(8,128)(2,1)S(1)}, bf16[1024,2048]{1,0:T(8,128)(2,1)S(1)}, f32[1024,128]{1,0:T(8,128)S(1)}) custom-call(bf16[1024,2048]{1,0:T(8,128)(2,1)S(1)} %copy-done.12, bf16[1024,2048]{1,0:T(8,128)(2,1)} %all-gather.6.cloned.1.call-done.own_ref, bf16[1024,2048]{1,0:T(8,128)(2,1)} %collective-permute-done.7.other_ref, ...), custom_call_target="tpu_custom_call" | custom-call | tf_op jit(solution)/shard_map/gate_product/pallas_call | solution.py:735
  165.9 5.0 %convolution_convert_fusion.1 = bf16[1024,2048]{1,0:T(8,128)(2,1)S(1)} fusion(bf16[1024,2048]{1,0:T(8,128)(2,1)S(1)} %copy-done.39, bf16[1024,2048]{1,0:T(8,128)(2,1)S(1)} %place_tokens.3.a_ref), kind=kOutput, calls=%fused_computation.16 | convolution fusion | flops 4297064448 | bytes 10485760 | tf_op jit(solution)/shard_map/dot_general | solution.py:28
  170.9 7.1 %collective-permute-done.8 = bf16[1024,2048]{1,0:T(8,128)(2,1)S(1)} collective-permute-done((bf16[1024,2048]{1,0:T(8,128)(2,1)S(1)}, bf16[1024,2048]{1,0:T(8,128)(2,1)S(1)}, u32[]{:S(2)}, u32[]{:S(2)}) %collective-permute-start.8) | collective-permute-done | bytes 4194336 | tf_op jit(solution)/shard_map/ppermute | solution.py:801
  178.1 6.5 %add_convert_fusion.1 = bf16[1024,2048]{1,0:T(8,128)(2,1)} fusion(bf16[1024,2048]{1,0:T(8,128)(2,1)S(1)} %collective-permute-done.8, bf16[1024,2048]{1,0:T(8,128)(2,1)S(1)} %copy-done.39, bf16[1024,2048]{1,0:T(8,128)(2,1)S(1)} %place_tokens.3.a_ref), kind=kOutput, calls=%fused_computation.1 | convolution fusion | flops 4301258752 | bytes 14680064 | tf_op jit(solution)/shard_map/dot_general | solution.py:28
  184.8 7.7 %fusion.71 = f32[1024,1024]{1,0:T(8,128)S(1)} fusion(bf16[1024,2048]{1,0:T(8,128)(2,1)} %copy-done.38, bf16[1024,2048]{1,0:T(8,128)(2,1)} %all-gather.8.cloned.1.call-done.own_ref), kind=kOutput, calls=%fused_computation.125 | convolution fusion | flops 4294967296 | bytes 12582912 | tf_op jit(solution)/shard_map/dot_general | solution.py:28
  192.5 8.9 %multiply_reduce_fusion = (f32[1024]{0:T(1024)S(1)}, f32[1024]{0:T(1024)S(1)}, bf16[1024,1024]{1,0:T(8,128)(2,1)}, bf16[1024,1024]{1,0:T(8,128)(2,1)}) fusion(bf16[1024,2048]{1,0:T(8,128)(2,1)S(1)} %copy-done.9, f32[1024,1024]{1,0:T(8,128)S(1)} %fusion.71, f32[1024]{0:T(1024)S(1)} %add_rsqrt_fusion, bf16[1024,2048]{1,0:T(8,128)(2,1)S(1)} %copy-done.40, ...), kind=kOutput, calls=%fused_computation.11 | convolution fusion | flops 4305451008 | bytes 20983808 | tf_op jit(solution)/shard_map/dot_general | solution.py:28
  208.9 16.0 %gating_product.1 = (bf16[1024,2048]{1,0:T(8,128)(2,1)S(1)}, bf16[1024,2048]{1,0:T(8,128)(2,1)S(1)}) custom-call(bf16[1024,2048]{1,0:T(8,128)(2,1)S(1)} %copy-done.10, bf16[1024,2048]{1,0:T(8,128)(2,1)} %all-gather.8.cloned.1.call-done.own_ref, bf16[1024,2048]{1,0:T(8,128)(2,1)} %collective-permute-done.9.other_ref, bf16[1024,2048]{1,0:T(8,128)(2,1)} %copy-done.22, ...), custom_call_target="tpu_custom_call" | custom-call | tf_op jit(solution)/shard_map/gating_product/pallas_call | solution.py:773
  229.9 6.1 %fusion.72 = f32[1024,1024]{1,0:T(8,128)} fusion(bf16[1024,2048]{1,0:T(8,128)(2,1)S(1)} %get-tuple-element.132, bf16[1024,2048]{1,0:T(8,128)(2,1)S(1)} %copy-done.46), kind=kOutput, calls=%fused_computation.126 | convolution fusion | flops 4294967296 | bytes 12582912 | tf_op jit(solution)/shard_map/dot_general | solution.py:28
  236.0 8.3 %fusion.73 = f32[1024,1024]{1,0:T(8,128)} fusion(bf16[1024,2048]{1,0:T(8,128)(2,1)S(1)} %get-tuple-element.132, bf16[1024,2048]{1,0:T(8,128)(2,1)} %collective-permute-done.7.other_ref), kind=kOutput, calls=%fused_computation.127 | convolution fusion | flops 4294967296 | bytes 12582912 | tf_op jit(solution)/shard_map/dot_general | solution.py:28
  244.3 6.2 %add_convert_fusion = bf16[1024,2048]{1,0:T(8,128)(2,1)} fusion(bf16[1024,2048]{1,0:T(8,128)(2,1)S(1)} %collective-permute-done.10, bf16[1024,2048]{1,0:T(8,128)(2,1)S(1)} %get-tuple-element.132, bf16[1024,2048]{1,0:T(8,128)(2,1)S(1)} %copy-done.13), kind=kOutput, calls=%fused_computation | convolution fusion | flops 4301258752 | bytes 14680064 | tf_op jit(solution)/shard_map/dot_general | solution.py:28
  258.3 17.3 %scan_backward.4 = (bf16[1024,1024]{1,0:T(8,128)(2,1)S(1)}, f32[1024,256]{1,0:T(8,128)S(1)}, f32[1024,256]{1,0:T(8,128)S(1)}, f32[1,8,1024]{2,1,0:T(8,128)S(1)}, f32[8,512]{1,0:T(8,128)S(1)}) custom-call(s32[1]{0:T(128)S(6)} %copy.173.prefix_ref, bf16[1024,2048]{1,0:T(8,128)(2,1)S(1)} %copy-done.1, bf16[1024,2048]{1,0:T(8,128)(2,1)S(1)} %copy-done.5, ...), custom_call_target="tpu_custom_call" | custom-call | tf_op jit(solution)/shard_map/scan_backward/pallas_call | solution.py:506
  275.6 17.7 %scan_backward.5 = (bf16[1024,1024]{1,0:T(8,128)(2,1)S(1)}, f32[1024,256]{1,0:T(8,128)S(1)}, f32[1024,256]{1,0:T(8,128)S(1)}, f32[1,8,1024]{2,1,0:T(8,128)S(1)}, f32[8,512]{1,0:T(8,128)S(1)}) custom-call(s32[1]{0:T(128)S(6)} %copy.173.prefix_ref, bf16[1024,2048]{1,0:T(8,128)(2,1)S(1)} %copy-done.1, ...), custom_call_target="tpu_custom_call", output_to_operand_aliasing={{1}: (8, {}), {2}: (9, {}), {0}: (10, {})} | custom-call | tf_op jit(solution)/shard_map/scan_backward/pallas_call | solution.py:506
  295.7 6.3 %collective-permute-done.11.refs_1_ = bf16[512,1024]{1,0:T(8,128)(2,1)} collective-permute-done((bf16[512,1024]{1,0:T(8,128)(2,1)S(1)}, bf16[512,1024]{1,0:T(8,128)(2,1)}, u32[]{:S(2)}, u32[]{:S(2)}) %collective-permute-start.11) | collective-permute-done | bytes 1048608 | tf_op jit(solution)/shard_map/ppermute | solution.py:805
  306.9 6.1 %fusion.17 = f32[1024,1024]{1,0:T(8,128)} fusion(f32[1024,1024]{1,0:T(8,128)S(1)} %copy-done.56, bf16[1024,1024]{1,0:T(8,128)(2,1)S(1)} %copy-done.28, bf16[1024,2432]{1,0:T(8,128)(2,1)} %all-gather.4.cloned.1.call-done), kind=kOutput, calls=%fused_computation.28 | convolution fusion | flops 2148532224 | bytes 12582912 | tf_op jit(solution)/shard_map/dot_general | solution.py:28
  313.0 6.3 %fusion.20 = f32[1024,1024]{1,0:T(8,128)} fusion(f32[1024,1024]{1,0:T(8,128)S(1)} %copy-done.57, bf16[1024,1024]{1,0:T(8,128)(2,1)S(1)} %copy-done.28, bf16[1024,2432]{1,0:T(8,128)(2,1)} %collective-permute-done.6), kind=kOutput, calls=%fused_computation.29 | convolution fusion | flops 2148532224 | bytes 12582912 | tf_op jit(solution)/shard_map/dot_general | solution.py:28
  334.6 17.9 %scan_backward.6 = (bf16[1024,1024]{1,0:T(8,128)(2,1)S(1)}, f32[1024,256]{1,0:T(8,128)S(1)}, f32[1024,256]{1,0:T(8,128)S(1)}, f32[1,8,1024]{2,1,0:T(8,128)S(1)}, f32[8,512]{1,0:T(8,128)S(1)}) custom-call(s32[1]{0:T(128)S(6)} %copy.173.prefix_ref, bf16[1024,2048]{1,0:T(8,128)(2,1)S(1)} %copy-done.2, ...), custom_call_target="tpu_custom_call", output_to_operand_aliasing={{1}: (8, {}), {2}: (9, {})} | custom-call | tf_op jit(solution)/shard_map/scan_backward/pallas_call | solution.py:506
  352.5 17.6 %scan_backward.7 = (bf16[1024,1024]{1,0:T(8,128)(2,1)S(1)}, f32[1024,256]{1,0:T(8,128)S(1)}, f32[1024,256]{1,0:T(8,128)S(1)}, f32[1,8,1024]{2,1,0:T(8,128)S(1)}, f32[8,512]{1,0:T(8,128)S(1)}) custom-call(s32[1]{0:T(128)S(6)} %copy.173.prefix_ref, bf16[1024,2048]{1,0:T(8,128)(2,1)S(1)} %copy-done.2, ...), custom_call_target="tpu_custom_call", output_to_operand_aliasing={{1}: (8, {}), {2}: (9, {}), {0}: (10, {})} | custom-call | tf_op jit(solution)/shard_map/scan_backward/pallas_call | solution.py:506
  384.1 5.4 %convolution_convert_fusion.2 = bf16[1024,1024]{1,0:T(8,128)(2,1)} fusion(bf16[1024,1024]{1,0:T(8,128)(2,1)S(1)} %copy-done.26, bf16[1024,2048]{1,0:T(8,128)(2,1)} %copy-done.11), kind=kOutput, calls=%fused_computation.32 | convolution fusion | flops 2148532224 | bytes 6291456 | tf_op jit(solution)/shard_map/dot_general | solution.py:28
  401.5 5.4 %add_convert_fusion.4 = bf16[1024,1024]{1,0:T(8,128)(2,1)} fusion(bf16[1024,1024]{1,0:T(8,128)(2,1)} %collective-permute-done.15, bf16[1024,1024]{1,0:T(8,128)(2,1)S(1)} %copy-done.26, bf16[1024,2048]{1,0:T(8,128)(2,1)S(1)} %copy-done.16), kind=kOutput, calls=%fused_computation.6 | convolution fusion | flops 2150629376 | bytes 8388608 | tf_op jit(solution)/shard_map/dot_general | solution.py:28
  411.3 6.7 %add_branch.1 = f32[512,2048]{1,0:T(8,128)} custom-call(s32[16]{0:T(128)} %copy-done.33, s32[2]{0:T(128)} %copy-done.32, bf16[512,2048]{1,0:T(8,128)(2,1)} %hidden_ref.3, bf16[1024,1024]{1,0:T(8,128)(2,1)} %get-tuple-element.186.refs_0_, bf16[512,1024]{1,0:T(8,128)(2,1)} %collective-permute-done.11.refs_1_, bf16[1024,1024]{1,0:T(8,128)(2,1)} %get-tuple-element.188.refs_2_, ...), custom_call_target="tpu_custom_call" | custom-call | tf_op jit(solution)/shard_map/add_branch/pallas_call | solution.py:641
  426.1 10.0 %collective-permute-done.16.refs_1_ = bf16[512,1024]{1,0:T(8,128)(2,1)} collective-permute-done((bf16[512,1024]{1,0:T(8,128)(2,1)}, bf16[512,1024]{1,0:T(8,128)(2,1)}, u32[]{:S(2)}, u32[]{:S(2)}) %collective-permute-start.16) | collective-permute-done | bytes 1048608 | tf_op jit(solution)/shard_map/ppermute | solution.py:805
  450.6 13.0 %collective-permute-done.17.refs_3_ = bf16[512,1024]{1,0:T(8,128)(2,1)} collective-permute-done((bf16[512,1024]{1,0:T(8,128)(2,1)}, bf16[512,1024]{1,0:T(8,128)(2,1)}, u32[]{:S(2)}, u32[]{:S(2)}) %collective-permute-start.17) | collective-permute-done | bytes 1048608 | tf_op jit(solution)/shard_map/ppermute | solution.py:805
  469.6 8.0 %finish.1 = f32[512,2048]{1,0:T(8,128)} custom-call(s32[16]{0:T(128)} %copy-done.33, s32[2]{0:T(128)} %copy-done.32, bf16[512,2048]{1,0:T(8,128)(2,1)} %hidden_ref.3, bf16[512,2048]{1,0:T(8,128)(2,1)} %cot_ref.1, f32[1,2048]{1,0:T(1,128)} %bitcast.61, bf16[1024,1024]{1,0:T(8,128)(2,1)} %add_convert_fusion.5.refs_0_, ...), custom_call_target="tpu_custom_call" | custom-call | tf_op jit(solution)/shard_map/finish/pallas_call | solution.py:641
  (302 shorter events, 163.8 us)
Async XLA Ops:
  7.2 62.4 %copy-start.53 = (s32[8]{0:T(128)S(1)}, s32[8]{0:T(128)}, u32[]{:S(2)}) copy-start(s32[8]{0:T(128)} %constant.59) | copy-start | bytes 100
  7.2 62.4 %copy-start.54 = (s32[8]{0:T(128)S(1)}, s32[8]{0:T(128)}, u32[]{:S(2)}) copy-start(s32[8]{0:T(128)} %constant.58) | copy-start | bytes 100
  7.2 64.0 %copy-start.7 = (bf16[512,2048]{1,0:T(8,128)(2,1)S(1)}, bf16[512,2048]{1,0:T(8,128)(2,1)}, u32[]{:S(2)}) copy-start(bf16[512,2048]{1,0:T(8,128)(2,1)} %hidden_ref.3) | copy-start | bytes 6291460
  7.2 61.7 %all-gather.4.cloned.1.call-start = ((), (), s32[]{:S(2)}) async-start(), calls=%async_computation.5 | async-start | bytes 5603328 | tf_op jit(solution)/shard_map/all_gather | solution.py:813
  10.3 115.5 %all-gather.6.cloned.1.call-start = ((), (), s32[]{:S(2)}) async-start(), calls=%async_computation.6 | async-start | bytes 4718592 | tf_op jit(solution)/shard_map/all_gather | solution.py:813
  10.3 49.0 %collective-permute-start = (bf16[512,2048]{1,0:T(8,128)(2,1)}, bf16[512,2048]{1,0:T(8,128)(2,1)}, u32[]{:S(2)}, u32[]{:S(2)}) collective-permute-start(bf16[512,2048]{1,0:T(8,128)(2,1)} %hidden_ref.3), channel_id=1, source_target_pairs={{0,1},{1,0},{2,3},{3,2},{4,5},{5,4},{6,7},{7,6},{8,9},{9,8},{10,11... | collective-permute-start | bytes 6291464 | tf_op jit(solution)/shard_map/ppermute | solution.py:805
  16.7 1.2 collective-permute-start.1
  17.9 3.7 collective-permute-start.2
  21.6 3.8 collective-permute-start.3
  23.3 161.2 %all-gather.8.cloned.1.call-start = ((), (), s32[]{:S(2)}) async-start(), calls=%async_computation.7 | async-start | bytes 4718592 | tf_op jit(solution)/shard_map/all_gather | solution.py:813
  25.5 5.0 %collective-permute-start.4 = (bf16[8,896]{1,0:T(8,128)(2,1)S(1)}, bf16[8,896]{1,0:T(8,128)(2,1)S(1)}, u32[]{:S(2)}, u32[]{:S(2)}) collective-permute-start(bf16[8,896]{1,0:T(8,128)(2,1)S(1)} %pad_maximum_fusion.1), channel_id=1, source_target_pairs={{0,16},{2,18},{4,20},{6,22},{8,24},{10,26},{12,28},{14,30},{16,0},... | collective-permute-start | bytes 43016 | tf_op jit(solution)/shard_map/ppermute | solution.py:820
  68.9 13.7 %collective-permute-start.6 = (bf16[1024,2432]{1,0:T(8,128)(2,1)}, bf16[1024,2432]{1,0:T(8,128)(2,1)}, u32[]{:S(2)}, u32[]{:S(2)}) collective-permute-start(bf16[1024,2432]{1,0:T(8,128)(2,1)} %all-gather.4.cloned.1.call-done), channel_id=1, source_target_pairs={{0,2},{2,0},{4,6},{6,4},{8,10},{10,8},{12,14},{14,12},{16,18},{18,... | collective-permute-start | bytes 14942216 | tf_op jit(solution)/shard_map/ppermute | solution.py:801
  69.6 90.3 %copy-start.32 = (s32[2]{0:T(128)}, s32[2]{0:T(128)S(1)}, u32[]{:S(2)}) copy-start(s32[2]{0:T(128)S(1)} %pad_add_fusion.1.slots_ref) | copy-start | bytes 28
  69.7 90.2 %copy-start.33 = (s32[16]{0:T(128)}, s32[16]{0:T(128)S(1)}, u32[]{:S(2)}) copy-start(s32[16]{0:T(128)S(1)} %pad_add_fusion.lanes_ref) | copy-start | bytes 196
  69.7 54.7 %collective-permute-start.5 = (bf16[512,2048]{1,0:T(8,128)(2,1)}, bf16[512,2048]{1,0:T(8,128)(2,1)S(1)}, u32[]{:S(2)}, u32[]{:S(2)}) collective-permute-start(bf16[512,2048]{1,0:T(8,128)(2,1)} %cot_ref.1), channel_id=1, source_target_pairs={{0,1},{1,0},{2,3},{3,2},{4,5},{5,4},{6,7},{7,6},{8,9},{9,8},{10,11... | collective-permute-start | bytes 6291464 | tf_op jit(solution)/shard_map/ppermute | solution.py:805
  125.8 7.5 %collective-permute-start.7 = (bf16[1024,2048]{1,0:T(8,128)(2,1)}, bf16[1024,2048]{1,0:T(8,128)(2,1)}, u32[]{:S(2)}, u32[]{:S(2)}) collective-permute-start(bf16[1024,2048]{1,0:T(8,128)(2,1)} %all-gather.6.cloned.1.call-done.own_ref), channel_id=1, source_target_pairs={{0,2},{2,0},{4,6},{6,4},{8,10},{10,8},{12,14},{14,12},{16,18},{18,... | collective-permute-start | bytes 12582920 | tf_op jit(solution)/shard_map/ppermute | solution.py:801
  127.0 175.0 %reduce-scatter.6.cloned.1.call-start = ((), (), s32[]{:S(2)}) async-start(), calls=%async_computation.8 | async-start | bytes 4718592 | tf_op jit(solution)/shard_map/reduce_scatter | solution.py:828
  170.8 7.2 %collective-permute-start.8 = (bf16[1024,2048]{1,0:T(8,128)(2,1)S(1)}, bf16[1024,2048]{1,0:T(8,128)(2,1)S(1)}, u32[]{:S(2)}, u32[]{:S(2)}) collective-permute-start(bf16[1024,2048]{1,0:T(8,128)(2,1)S(1)} %convolution_convert_fusion.1), channel_id=1, source_target_pairs={{0,2},{2,0},{4,6},{6,4},{8,10},{10,8},{12,14},{14,12},{16,18},{18,... | collective-permute-start | bytes 12582920 | tf_op jit(solution)/shard_map/ppermute | solution.py:801
  184.5 8.0 %collective-permute-start.9 = (bf16[1024,2048]{1,0:T(8,128)(2,1)}, bf16[1024,2048]{1,0:T(8,128)(2,1)}, u32[]{:S(2)}, u32[]{:S(2)}) collective-permute-start(bf16[1024,2048]{1,0:T(8,128)(2,1)} %all-gather.8.cloned.1.call-done.own_ref), channel_id=1, source_target_pairs={{0,2},{2,0},{4,6},{6,4},{8,10},{10,8},{12,14},{14,12},{16,18},{18,... | collective-permute-start | bytes 12582920 | tf_op jit(solution)/shard_map/ppermute | solution.py:801
  184.7 117.3 %reduce-scatter.8.cloned.1.call-start = ((), (), s32[]{:S(2)}) async-start(), calls=%async_computation.9 | async-start | bytes 4718592 | tf_op jit(solution)/shard_map/reduce_scatter | solution.py:828
  229.8 14.5 %collective-permute-start.10 = (bf16[1024,2048]{1,0:T(8,128)(2,1)S(1)}, bf16[1024,2048]{1,0:T(8,128)(2,1)S(1)}, u32[]{:S(2)}, u32[]{:S(2)}) collective-permute-start(bf16[1024,2048]{1,0:T(8,128)(2,1)S(1)} %convolution_convert_fusion), channel_id=1, source_target_pairs={{0,2},{2,0},{4,6},{6,4},{8,10},{10,8},{12,14},{14,12},{16,18},{18,... | collective-permute-start | bytes 12582920 | tf_op jit(solution)/shard_map/ppermute | solution.py:801
  250.5 133.6 %reduce-scatter.10.cloned.1.call-start = ((), (), s32[]{:S(2)}) async-start(), calls=%async_computation.10 | async-start | bytes 2359296 | tf_op jit(solution)/shard_map/reduce_scatter | solution.py:828
  253.8 41.8 %collective-permute-start.12 = (bf16[512,1024]{1,0:T(8,128)(2,1)S(1)}, bf16[512,1024]{1,0:T(8,128)(2,1)}, u32[]{:S(2)}, u32[]{:S(2)}) collective-permute-start(bf16[512,1024]{1,0:T(8,128)(2,1)S(1)} %constant_dynamic-slice_fusion.2), channel_id=1, source_target_pairs={{0,1},{1,0},{2,3},{3,2},{4,5},{5,4},{6,7},{7,6},{8,9},{9,8},{10,11... | collective-permute-start | bytes 3145736 | tf_op jit(solution)/shard_map/ppermute | solution.py:805
  254.9 47.1 %collective-permute-start.11 = (bf16[512,1024]{1,0:T(8,128)(2,1)S(1)}, bf16[512,1024]{1,0:T(8,128)(2,1)}, u32[]{:S(2)}, u32[]{:S(2)}) collective-permute-start(bf16[512,1024]{1,0:T(8,128)(2,1)S(1)} %constant_dynamic-slice_fusion.3), channel_id=1, source_target_pairs={{0,1},{1,0},{2,3},{3,2},{4,5},{5,4},{6,7},{7,6},{8,9},{9,8},{10,11... | collective-permute-start | bytes 3145736 | tf_op jit(solution)/shard_map/ppermute | solution.py:805
  306.8 12.5 %collective-permute-start.13 = (bf16[1024,1024]{1,0:T(8,128)(2,1)S(1)}, bf16[1024,1024]{1,0:T(8,128)(2,1)S(1)}, u32[]{:S(2)}, u32[]{:S(2)}) collective-permute-start(bf16[1024,1024]{1,0:T(8,128)(2,1)S(1)} %fusion.26), channel_id=1, source_target_pairs={{0,2},{2,0},{4,6},{6,4},{8,10},{10,8},{12,14},{14,12},{16,18},{18,... | collective-permute-start | bytes 6291464 | tf_op jit(solution)/shard_map/ppermute | solution.py:801
  323.1 118.3 %reduce-scatter.12.cloned.1.call-start = ((), (), s32[]{:S(2)}) async-start(), calls=%async_computation.11 | async-start | bytes 1363968 | tf_op jit(solution)/shard_map/reduce_scatter | solution.py:828
  382.8 7.6 %collective-permute-start.14 = (f32[1024,295]{0,1:T(8,128)}, f32[1024,295]{0,1:T(8,128)}, u32[]{:S(2)}, u32[]{:S(2)}) collective-permute-start(f32[1024,295]{0,1:T(8,128)} %pad_maximum_fusion), channel_id=1, source_target_pairs={{0,2},{2,0},{4,6},{6,4},{8,10},{10,8},{12,14},{14,12},{16,18},{18,... | collective-permute-start | bytes 3624968 | tf_op jit(solution)/shard_map/ppermute | solution.py:801
  389.6 11.9 %collective-permute-start.15 = (bf16[1024,1024]{1,0:T(8,128)(2,1)}, bf16[1024,1024]{1,0:T(8,128)(2,1)}, u32[]{:S(2)}, u32[]{:S(2)}) collective-permute-start(bf16[1024,1024]{1,0:T(8,128)(2,1)} %convolution_convert_fusion.2), channel_id=1, source_target_pairs={{0,2},{2,0},{4,6},{6,4},{8,10},{10,8},{12,14},{14,12},{16,18},{18,... | collective-permute-start | bytes 6291464 | tf_op jit(solution)/shard_map/ppermute | solution.py:801
  393.0 70.5 %reduce-scatter.14.cloned.1.call-start = ((), (), s32[]{:S(2)}) async-start(), calls=%async_computation.12 | async-start | bytes 2359296 | tf_op jit(solution)/shard_map/reduce_scatter | solution.py:828
  410.3 25.9 %collective-permute-start.16 = (bf16[512,1024]{1,0:T(8,128)(2,1)}, bf16[512,1024]{1,0:T(8,128)(2,1)}, u32[]{:S(2)}, u32[]{:S(2)}) collective-permute-start(bf16[512,1024]{1,0:T(8,128)(2,1)} %constant_dynamic-slice_fusion.1), channel_id=1, source_target_pairs={{0,1},{1,0},{2,3},{3,2},{4,5},{5,4},{6,7},{7,6},{8,9},{9,8},{10,11... | collective-permute-start | bytes 3145736 | tf_op jit(solution)/shard_map/ppermute | solution.py:805
  438.4 25.1 %collective-permute-start.17 = (bf16[512,1024]{1,0:T(8,128)(2,1)}, bf16[512,1024]{1,0:T(8,128)(2,1)}, u32[]{:S(2)}, u32[]{:S(2)}) collective-permute-start(bf16[512,1024]{1,0:T(8,128)(2,1)} %constant_dynamic-slice_fusion), channel_id=1, source_target_pairs={{0,1},{1,0},{2,3},{3,2},{4,5},{5,4},{6,7},{7,6},{8,9},{9,8},{10,11... | collective-permute-start | bytes 3145736 | tf_op jit(solution)/shard_map/ppermute | solution.py:805
  466.6 11.0 %collective-permute-start.18 = (f32[32960]{0:T(1024)S(1)}, f32[32960]{0:T(1024)S(1)}, u32[]{:S(2)}, u32[]{:S(2)}) collective-permute-start(f32[32960]{0:T(1024)S(1)} %concatenate.55), channel_id=1, source_target_pairs={{0,1},{1,0},{2,3},{3,2},{4,5},{5,4},{6,7},{7,6},{8,9},{9,8},{10,11... | collective-permute-start | bytes 395528 | tf_op jit(solution)/shard_map/ppermute | solution.py:805
  (53 other events, 478.0 us)
Sparse Core Ops, SparseCore 0:
  10.4 58.4 all-gather.3
  70.4 47.9 all-gather.5
  127.2 47.4 all-gather.7
  184.8 48.1 reduce-scatter.5
  250.6 48.2 reduce-scatter.7
  323.2 32.9 reduce-scatter.9
  393.2 29.7 reduce-scatter.11
  425.8 32.0 reduce-scatter.13

commit v2 on v1

--- a/solution.py
+++ b/solution.py
@@ -151,7 +151,7 @@
 def forward_kernel(
     heads, first, prefix_ref, x_ref, taps_ref, skip_ref, cols_ref, rows_ref, act_ref, *refs
 ):
-    out_ref, xd_ref, kept_ref, back_ref, state_ref = refs[-5:]
+    out_ref, states_ref, xd_ref, kept_ref, back_ref, state_ref = refs[-6:]
     length, width = x_ref.shape
     chunks = length // Q
     anti = min(MAX_PREFIX // Q, chunks)
@@ -193,7 +193,9 @@
         part = cols_ref[rows_of(c), :]
         within, beyond = growths(part, heads)
         entering = split_dot(within, by_cum)
-        total = kept_ref[rows_of(c), :] + dot(c_mat, low(state_ref[...])) * entering
+        state_low = low(state_ref[...])
+        states_ref[c] = state_low
+        total = kept_ref[rows_of(c), :] + dot(c_mat, state_low) * entering
         if two_way:
             leaving = split_dot(beyond, by_ecum)
             total = total + dot(c_mat, back_ref[c]) * leaving
@@ -252,8 +254,14 @@
         functools.partial(forward_kernel, channels // P_SIZE, group * HG),
         grid=(1,),
         in_specs=in_specs,
-        out_specs=pl.BlockSpec((length, CG), lambda g: (0, group)),
-        out_shape=jax.ShapeDtypeStruct((length, channels), BF16),
+        out_specs=[
+            pl.BlockSpec((length, CG), lambda g: (0, group)),
+            pl.BlockSpec((length // Q, N, CG), lambda g: (0, 0, 0)),
+        ],
+        out_shape=(
+            jax.ShapeDtypeStruct((length, channels), BF16),
+            jax.ShapeDtypeStruct((length // Q, N, CG), BF16),
+        ),
         input_output_aliases=aliases,
         scratch_shapes=[
             pltpu.VMEM((length, CG), BF16),
@@ -279,6 +287,7 @@
     cols_ref,
     rows_ref,
     act_ref,
+    states_scr,
     *refs,
 ):
     (
@@ -289,12 +298,11 @@
         gsum_ref,
         x_scr,
         slope_scr,
-        states_scr,
         dback_scr,
         state_ref,
         dstate_ref,
         next_scr,
-    ) = refs[-12:]
+    ) = refs[-11:]
     length, width = x_ref.shape
     chunks = length // Q
     anti = min(MAX_PREFIX // Q, chunks)
@@ -318,18 +326,13 @@
         slope_scr[rows_of(c), :] = s + x * (1.0 - s)
         dy = dy_scr[rows_of(c), :].astype(F32)
         gsum_ref[4:5, :] += jnp.sum(dy * x, axis=0, keepdims=True)
-        part = cols_ref[rows_of(c), :]
-        within, beyond = growths(part, heads)
-        states_scr[c] = low(state_ref[...])
-        entering = split_dot(within[Q - 8 :], by_cum)
-        x_low = low(x * split_dot(part, by_step) * split_dot(beyond, by_cum))
-        b_mat = act_ref[rows_of(c), 0:N]
-        c_mat = act_ref[rows_of(c), N : 2 * N]
-        state_ref[...] = state_ref[...] * entering[7:8] + dot(b_mat, x_low, TN)
         if two_way:
+            within, beyond = growths(cols_ref[rows_of(c), :], heads)
+            grow = split_dot(within[Q - 8 :], by_cum)[7:8]
             leaving = split_dot(beyond, by_ecum)
+            c_mat = act_ref[rows_of(c), N : 2 * N]
             dback_scr[c + 1] = low(
-                dback_scr[c].astype(F32) * entering[7:8] + dot(c_mat, low(dy * leaving), TN)
+                dback_scr[c].astype(F32) * grow + dot(c_mat, low(dy * leaving), TN)
             )
         return 0
 
@@ -475,12 +478,12 @@
     lax.fori_loop(0, anti, lambda i, _: chunk_body(anti - 1 - i, True), 0, unroll=4)
 
 
-def scan_backward(prefix, x_pre, grad_ssd, taps, skip, cols, rows, act, group, place, places, gx, before):
+def scan_backward(prefix, x_pre, grad_ssd, taps, skip, cols, rows, act, states, group, place, places, gx, before):
     length, channels = x_pre.shape
     chunks = length // Q
     anti = min(MAX_PREFIX // Q, chunks)
     wide = pl.BlockSpec((length, CG), lambda i: (0, group))
-    given = [prefix, x_pre, grad_ssd, taps, skip, cols, rows, act]
+    given = [prefix, x_pre, grad_ssd, taps, skip, cols, rows, act, states]
     in_specs = [
         pl.BlockSpec(memory_space=pltpu.SMEM),
         wide,
@@ -490,6 +493,7 @@
         pl.BlockSpec((length, 128), lambda i: (0, 0)),
         pl.BlockSpec((128, length), lambda i: (0, 0)),
         pl.BlockSpec((length, 2 * N), lambda i: (0, 0)),
+        pl.BlockSpec((chunks, N, CG), lambda i: (0, 0, 0)),
     ]
     aliases = {}
     if before is not None:
@@ -525,7 +529,6 @@
         scratch_shapes=[
             pltpu.VMEM((length, CG), F32),
             pltpu.VMEM((length, CG), F32),
-            pltpu.VMEM((chunks, N, CG), BF16),
             pltpu.VMEM((anti + 1, N, CG), BF16),
             pltpu.VMEM((N, CG), F32),
             pltpu.VMEM((N, CG), F32),
@@ -709,8 +712,7 @@
     )(rest_pre, bc_taps, log_decay[None], dt_bias[None], grad_act, gcols, *grows)
 
 
-def gate_kernel(a_ref, own_ref, other_ref, ssd_ref, gain_ref, gate_ref, out_ref, square_ref):
-    depth = own_ref.shape[0]
+def gate_kernel(a_ref, other_ref, part_ref, ssd_ref, gain_ref, gate_ref, out_ref, square_ref):
     gain = gain_ref[...]
 
     @pl.when(pl.program_id(0) == 0)
@@ -719,7 +721,7 @@
 
     for m in range(0, a_ref.shape[0], 256):
         here = slice(m, m + 256)
-        z = dot(a_ref[here, :depth], own_ref[...]) + dot(a_ref[here, depth:], other_ref[...])
+        z = part_ref[here, :] + dot(a_ref[here, :], other_ref[...])
         gated = ssd_ref[here, :].astype(F32) * (z * sig(z))
         gate_ref[here, :] = low(z)
         out_ref[here, :] = low(gated * gain)
@@ -727,7 +729,7 @@
         square_ref[here, :] += sum(square[:, k : k + 128] for k in range(0, CG, 128))
 
 
-def gate_product(normed, own, other, ssd_out, gain):
+def gate_product(normed, other, part, ssd_out, gain):
     tokens, width = normed.shape
     channels = ssd_out.shape[1]
     tall = pl.BlockSpec((tokens, CG), lambda j: (0, j))
@@ -736,7 +738,7 @@
         gate_kernel,
         grid=(channels // CG,),
         in_specs=[
-            pl.BlockSpec((tokens, width), lambda j: (0, 0)), deep, deep, tall, pl.BlockSpec((1, CG), lambda j: (0, j)),
+            pl.BlockSpec((tokens, width // 2), lambda j: (0, 1)), deep, tall, tall, pl.BlockSpec((1, CG), lambda j: (0, j)),
         ],
         out_specs=[tall, tall, pl.BlockSpec((tokens, 128), lambda j: (0, 0))],
         out_shape=(
@@ -747,7 +749,7 @@
         compiler_params=pltpu.CompilerParams(vmem_limit_bytes=40 * MIB),
         cost_estimate=NO_COST,
         name="gate_product",
-    )(normed, own, other, ssd_out, gain)
+    )(normed, other, part, ssd_out, gain)
 
 
 def gating_kernel(a_ref, own_ref, other_ref, gate_ref, ssd_ref, coef_ref, gain_ref, ggate_ref, dy_ref):
@@ -921,6 +923,9 @@
         hidden_parts[-1], (norm_gain, x_taps, bc_taps, gain, skip)
     )
 
+    def over_tp(v):
+        return v + other_half(v) if tp == 2 else lax.psum(v, "tp")
+
     x_own = gather(payload, fsdp)
     z_own = gather(z_weight, fsdp)
     out_own = gather(out_weight.T, fsdp)
@@ -936,14 +941,16 @@
     rest_own, rest_other = x_own[:, rest], x_other[:, rest]
     act, cols, head_rows = prep(rest_pre, bc_taps, log_decay, dt_bias)
     x_pre = low(dot(na, x_own[:, :channels]) + dot(nb, x_other[:, :channels]))
-    ssd_out = None
+    ssd_out, states = None, []
     for g in range(groups):
-        ssd_out = scan_forward(prefix, x_pre, x_taps, skip, cols, head_rows, act, g, ssd_out)
+        ssd_out, kept = scan_forward(prefix, x_pre, x_taps, skip, cols, head_rows, act, g, ssd_out)
+        states.append(kept)
     (z_own, cot_parts[-1]), ssd_out = tie((z_own, cot_parts[-1]), ssd_out)
     z_other = other_core(z_own, fsdp)
 
-    gate_low, scaled_out, square = gate_product(normed, z_own, z_other, ssd_out, gain)
-    square_sum = lax.psum(jnp.sum(square, axis=-1), "tp")
+    part = lax.optimization_barrier(dot(na, z_own))
+    gate_low, scaled_out, square = gate_product(normed, z_other, part, ssd_out, gain)
+    square_sum = over_tp(jnp.sum(square, axis=-1))
 
     inv_gate = lax.rsqrt(square_sum / all_channels + EPSILON)[:, None]
     cot_rel = place_tokens(lanes, slots, cot_parts, inv_gate, False)
@@ -960,7 +967,7 @@
         v = dot(scaled_out, out_half, NT)
         along = along + jnp.sum(v * cot_half.astype(F32), axis=-1)
         branch.append(low(v * inv_gate))
-    along = lax.psum(along, "tp")
+    along = over_tp(along)
     coef = inv_gate * inv_gate * (along / all_channels)[:, None]
     coef, branch = tie(coef, branch)
 
@@ -984,14 +991,14 @@
     grad_z = scatter(gz_sum, fsdp)
 
     grows, gsums = [], []
-    first = groups // 2
+    first = groups * 3 // 4
     before = None
 
     def back_through(start, stop, dy, before):
         gx = None
         for g in range(start, stop):
             gx, gact, gcol, grow, gsum = scan_backward(
-                prefix, x_pre, dy, x_taps, skip, cols, head_rows, act, g, g - start, stop - start, gx, before
+                prefix, x_pre, dy, x_taps, skip, cols, head_rows, act, states[g], g, g - start, stop - start, gx, before
             )
             before = (gact, gcol)
             grows.append(grow)
@@ -1012,10 +1019,10 @@
         dy, total = tie(dy, total)
         grad_x.append(scatter(total, fsdp))
     gx, before = back_through(first, groups, dy, before)
-    gx, (grad_z, *grad_x) = tie(gx, (grad_z, *grad_x))
+    if not first:
+        gx, grad_z = tie(gx, grad_z)
     g_gain = jnp.sum(out_weight.T.astype(F32) * grad_out.astype(F32), axis=0) / gain[0]
     g_gain = jnp.transpose(g_gain.reshape(heads, fsdp, -1), (1, 0, 2))
-    grad_x = list(grad_x)
     late = slice(first * CG, channels)
     grest, gbc_taps, ghead = post(rest_pre, bc_taps, log_decay, dt_bias, before[0], before[1], grows)
 
@@ -1045,7 +1052,7 @@
     came = other_core(gx_other, fsdp)
     (grest, gx), gx_other = tie((grest, gx), gx_other)
     rest_sum = jnp.concatenate([dot(na, grest, TN), lines_own], axis=1) + rest_came
-    (grest, gx), rest_sum = tie((grest, gx), rest_sum)
+    (grest, gx), (rest_sum, grad_x) = tie((grest, gx), (rest_sum, grad_x))
     mine_rest = scatter(rest_sum, fsdp)
 
     def first_part(v, x_half):
@@ -1068,12 +1075,11 @@
     )
     grad_z, grad_out = grad_z.astype(F32), grad_out.astype(F32).T
     arrived = [v for v, _ in part_sums[0]]
-    second, (arrived, mixed, grad_out, grad_z) = tie(second, (arrived, mixed, grad_out, grad_z))
+    second, (arrived, mixed, grad_out, grad_z, mine_rest) = tie(
+        second, (arrived, mixed, grad_out, grad_z, mine_rest)
+    )
     part_sums[0] = list(zip(arrived, kinds_part))
     part_sums.append(to_own_tokens(low(second + dot(grest, rest_other, NT))))
-
-    def over_tp(v):
-        return v + other_half(v) if tp == 2 else lax.psum(v, "tp")
 
     grad_bc, grad_dt = mine_rest[:, : 2 * N], mine_rest[:, 2 * N : 2 * N + heads]
     lines = mine_rest[:, 2 * N + heads :].reshape(-1)

time: 497 us -> 487 us (0.980)
  matrix products: 119 us -> 134 us
  blocking collectives: 9.88 us -> 0 us
  Pallas kernels: 156 us -> 147 us
  waiting for transfers between devices: 85.6 us -> 77 us
    ppermute x7 -> x9, waiting for transfers between devices: 55.7 us -> 38.5 us  [other_half(): return lax.ppermute(v, 'tp', [(0, 1), (1, 0)])]
    dot_general x24 -> x25, matrix products: 119 us -> 134 us  [dot(): return lax.dot_general(a, b, (dims, ((), ())), preferred_element_type=F32)]
    reduce_scatter x5, waiting for transfers between devices: 0.01 us -> 14.8 us  [scatter(): lax.psum_scatter(v, 'fsdp', scatter_dimension=0, tiled=True, axis_index_g...]
    psum x2 -> x0, blocking collectives: 9.88 us -> none  [the longest x1 4.95 us: on_device(): square_sum = lax.psum(jnp.sum(square, axis=-1), 'tp')]
    ppermute x8, waiting for transfers between devices: 13.4 us -> 7.16 us  [other_core(): return lax.ppermute(v, 'fsdp', [(i, i ^ 1) for i in range(devices)])]
    unnamed x128 -> x144, local copies, waits for them, and re-layouts: 34.9 us -> 38.9 us
    ppermute x7 -> x9, starting transfers between devices: 9.75 us -> 12.4 us  [other_half(): return lax.ppermute(v, 'tp', [(0, 1), (1, 0)])]
  transfers between devices with their start and end apart: 27 -> 29, of which waited for: 11 -> 11; matrix products, arithmetic and copies ran while one was open for 32% -> 35% of each run, Pallas kernels for 32% -> 31%
where the time goes in v2:
time: 487 us; the launch traced here: 478 us
  Pallas kernels  147 us (30%)
  matrix products  134 us (28%)
  waiting for transfers between devices  77 us (16%)
  local copies, waits for them, and re-layouts  62.1 us (13%)
  starting transfers between devices  21.2 us (4%)
  other arithmetic  21 us (4%)
  between operations  16.1 us (3%)
    dot_general x25, matrix products, dot(): return lax.dot_general(a, b, (dims, ((), ())), preferred_element_type=F32)  134 us
    pallas_call x4, Pallas kernels, scan_backward(): pl.pallas_call(functools.partial(backward_kernel, channels // P_SIZE, gro...  66 us
    unnamed x144, local copies, waits for them, and re-layouts  38.9 us
    ppermute x9, waiting for transfers between devices, other_half(): return lax.ppermute(v, 'tp', [(0, 1), (1, 0)])  38.5 us
    pallas_call x4, Pallas kernels, scan_forward(): pl.pallas_call(functools.partial(forward_kernel, channels // P_SIZE, grou...  27.2 us
    pallas_call x1, Pallas kernels, gating_product(): pl.pallas_call(gating_kernel, grid=(channels // CG,), in_specs=[pl.BlockS...  15.8 us
    reduce_scatter x5, waiting for transfers between devices, scatter(): lax.psum_scatter(v, 'fsdp', scatter_dimension=0, tiled=True, axis_index_g...  14.8 us
    pallas_call x2, Pallas kernels, own_rows(): pl.pallas_call(kernel, grid_spec=pltpu.PrefetchScalarGridSpec(num_scalar_...  14.4 us
  transfers between devices with their start and end apart: 29, of which 11 were waited for; matrix products, arithmetic and copies ran while one was open for 35% of the time, Pallas kernels for 31%

profile of v2, /device:TPU:0, one launch (start us, length us, event | category | flops | bytes accessed | tf_op | source)
XLA Modules:
  0.0 478.3 jit_solution(21737054068788179)
XLA Ops:
  32.9 26.4 %collective-permute-done.refs_1_ = bf16[512,2048]{1,0:T(8,128)(2,1)} collective-permute-done((bf16[512,2048]{1,0:T(8,128)(2,1)}, bf16[512,2048]{1,0:T(8,128)(2,1)}, u32[]{:S(2)}, u32[]{:S(2)}) %collective-permute-start) | collective-permute-done | bytes 2097184 | tf_op jit(solution)/shard_map/ppermute | solution.py:807
  59.3 9.6 %all-gather.4.cloned.1.call-done = bf16[1024,2432]{1,0:T(8,128)(2,1)} async-done(((bf16[128,2432]{1,0:T(8,128)(2,1)}), bf16[1024,2432]{1,0:T(8,128)(2,1)}) %all-gather.4.cloned.1.call-update) | async-done | bytes 4980752 | tf_op jit(solution)/shard_map/all_gather | solution.py:815
  71.2 5.6 %place_tokens.2.a_ref = bf16[1024,2048]{1,0:T(8,128)(2,1)S(1)} custom-call(s32[16]{0:T(128)S(1)} %pad_add_fusion.lanes_ref, s32[2]{0:T(128)S(1)} %pad_add_fusion.1.slots_ref, bf16[512,2048]{1,0:T(8,128)(2,1)S(1)} %copy-done.6, bf16[512,2048]{1,0:T(8,128)(2,1)} %collective-permute-done.refs_1_, f32[1,2048]{1,0:T(1,128)S(1)} %bitcast.61), custom_call_target="tpu_custom_call" | custom-call | tf_op jit(solution)/shard_map/place_tokens/pallas_call | solution.py:581
  76.8 6.7 %fusion.2 = f32[1024,2048]{1,0:T(8,128)} fusion(bf16[1024,2432]{1,0:T(8,128)(2,1)S(1)} %copy-done.59, bf16[1024,2048]{1,0:T(8,128)(2,1)S(1)} %place_tokens.2.a_ref), kind=kOutput, calls=%fused_computation.12 | convolution fusion | flops 4294967296 | bytes 14680064 | tf_op jit(solution)/shard_map/dot_general | solution.py:28
  89.1 8.3 %add_convert_fusion.2.x_ref = bf16[1024,2048]{1,0:T(8,128)(2,1)S(1)} fusion(f32[1024,2048]{1,0:T(8,128)} %fusion.2, bf16[1024,2432]{1,0:T(8,128)(2,1)} %collective-permute-done.6, bf16[1024,2048]{1,0:T(8,128)(2,1)S(1)} %place_tokens.2.a_ref), kind=kOutput, calls=%fused_computation.2 | convolution fusion | flops 4299161600 | bytes 18874368 | tf_op jit(solution)/shard_map/dot_general | solution.py:28
  97.4 7.1 %scan_forward.4 = (bf16[1024,2048]{1,0:T(8,128)(2,1)S(1)}, bf16[8,128,512]{2,1,0:T(8,128)(2,1)S(1)}) custom-call(s32[1]{0:T(128)S(6)} %copy.173.prefix_ref, bf16[1024,2048]{1,0:T(8,128)(2,1)S(1)} %add_convert_fusion.2.x_ref, f32[4,2048]{1,0:T(4,128)S(1)} %reshape.148.taps_ref, f32[1,2048]{1,0:T(1,128)S(1)} %broadcast_in_dim_reshape.3.skip_ref, ...), custom_call_target="tpu_custom_call" | custom-call | tf_op jit(solution)/shard_map/scan_forward/pallas_call | solution.py:253
  105.5 6.6 %scan_forward.5 = (bf16[1024,2048]{1,0:T(8,128)(2,1)S(1)}, bf16[8,128,512]{2,1,0:T(8,128)(2,1)S(1)}) custom-call(s32[1]{0:T(128)S(6)} %copy.173.prefix_ref, bf16[1024,2048]{1,0:T(8,128)(2,1)S(1)} %add_convert_fusion.2.x_ref, f32[4,2048]{1,0:T(4,128)S(1)} %reshape.148.taps_ref, ...), custom_call_target="tpu_custom_call", output_to_operand_aliasing={{0}: (7, {})} | custom-call | tf_op jit(solution)/shard_map/scan_forward/pallas_call | solution.py:253
  113.0 6.9 %scan_forward.6 = (bf16[1024,2048]{1,0:T(8,128)(2,1)S(1)}, bf16[8,128,512]{2,1,0:T(8,128)(2,1)S(1)}) custom-call(s32[1]{0:T(128)S(6)} %copy.173.prefix_ref, bf16[1024,2048]{1,0:T(8,128)(2,1)S(1)} %add_convert_fusion.2.x_ref, f32[4,2048]{1,0:T(4,128)S(1)} %reshape.148.taps_ref, ...), custom_call_target="tpu_custom_call", output_to_operand_aliasing={{0}: (7, {})} | custom-call | tf_op jit(solution)/shard_map/scan_forward/pallas_call | solution.py:253
  120.9 6.7 %scan_forward.7 = (bf16[1024,2048]{1,0:T(8,128)(2,1)S(1)}, bf16[8,128,512]{2,1,0:T(8,128)(2,1)S(1)}) custom-call(s32[1]{0:T(128)S(6)} %copy.173.prefix_ref, bf16[1024,2048]{1,0:T(8,128)(2,1)S(1)} %add_convert_fusion.2.x_ref, f32[4,2048]{1,0:T(4,128)S(1)} %reshape.148.taps_ref, ...), custom_call_target="tpu_custom_call", output_to_operand_aliasing={{0}: (7, {})} | custom-call | tf_op jit(solution)/shard_map/scan_forward/pallas_call | solution.py:253
  133.8 10.8 %fusion.28.part_ref = f32[1024,2048]{1,0:T(8,128)} fusion(bf16[1024,2048]{1,0:T(8,128)(2,1)} %all-gather.6.cloned.1.call-done, bf16[1024,2048]{1,0:T(8,128)(2,1)} %copy-done.11), kind=kOutput, calls=%fused_computation.37 | convolution fusion | flops 4294967296 | bytes 14680064 | tf_op jit(solution)/shard_map/dot_general | solution.py:28
  144.6 10.8 %gate_product.1 = (bf16[1024,2048]{1,0:T(8,128)(2,1)S(1)}, bf16[1024,2048]{1,0:T(8,128)(2,1)S(1)}, f32[1024,128]{1,0:T(8,128)S(1)}) custom-call(bf16[1024,2048]{1,0:T(8,128)(2,1)S(1)} %copy-done.12, bf16[1024,2048]{1,0:T(8,128)(2,1)} %collective-permute-done.7.other_ref, f32[1024,2048]{1,0:T(8,128)} %fusion.28.part_ref, bf16[1024,2048]{1,0:T(8,128)(2,1)} %copy-done.3, ...), custom_call_target="tpu_custom_call" | custom-call | tf_op jit(solution)/shard_map/gate_product/pallas_call | solution.py:737
  169.6 5.0 %convolution_convert_fusion.2 = bf16[1024,2048]{1,0:T(8,128)(2,1)S(1)} fusion(bf16[1024,2048]{1,0:T(8,128)(2,1)S(1)} %copy-done.48, bf16[1024,2048]{1,0:T(8,128)(2,1)S(1)} %place_tokens.3.a_ref), kind=kOutput, calls=%fused_computation.16 | convolution fusion | flops 4297064448 | bytes 10485760 | tf_op jit(solution)/shard_map/dot_general | solution.py:28
  174.7 7.1 %collective-permute-done.9 = bf16[1024,2048]{1,0:T(8,128)(2,1)S(1)} collective-permute-done((bf16[1024,2048]{1,0:T(8,128)(2,1)S(1)}, bf16[1024,2048]{1,0:T(8,128)(2,1)S(1)}, u32[]{:S(2)}, u32[]{:S(2)}) %collective-permute-start.9) | collective-permute-done | bytes 4194336 | tf_op jit(solution)/shard_map/ppermute | solution.py:803
  181.9 6.5 %add_convert_fusion.1 = bf16[1024,2048]{1,0:T(8,128)(2,1)} fusion(bf16[1024,2048]{1,0:T(8,128)(2,1)S(1)} %collective-permute-done.9, bf16[1024,2048]{1,0:T(8,128)(2,1)S(1)} %copy-done.48, bf16[1024,2048]{1,0:T(8,128)(2,1)S(1)} %place_tokens.3.a_ref), kind=kOutput, calls=%fused_computation.1 | convolution fusion | flops 4301258752 | bytes 14680064 | tf_op jit(solution)/shard_map/dot_general | solution.py:28
  188.7 7.7 %fusion.69 = f32[1024,1024]{1,0:T(8,128)S(1)} fusion(bf16[1024,2048]{1,0:T(8,128)(2,1)} %copy-done.47, bf16[1024,2048]{1,0:T(8,128)(2,1)} %all-gather.8.cloned.1.call-done.own_ref), kind=kOutput, calls=%fused_computation.126 | convolution fusion | flops 4294967296 | bytes 12582912 | tf_op jit(solution)/shard_map/dot_general | solution.py:28
  196.5 9.0 %multiply_reduce_fusion = (f32[1024]{0:T(1024)S(1)}, f32[1024]{0:T(1024)S(1)}, bf16[1024,1024]{1,0:T(8,128)(2,1)}, bf16[1024,1024]{1,0:T(8,128)(2,1)}) fusion(bf16[1024,2048]{1,0:T(8,128)(2,1)S(1)} %copy-done.18, f32[1024,1024]{1,0:T(8,128)S(1)} %fusion.69, f32[1024]{0:T(1024)S(1)} %add_rsqrt_fusion, bf16[1024,2048]{1,0:T(8,128)(2,1)S(1)} %copy-done.49, ...), kind=kOutput, calls=%fused_computation.10 | convolution fusion | flops 4305451008 | bytes 20983808 | tf_op jit(solution)/shard_map/dot_general | solution.py:28
  211.6 15.8 %gating_product.1 = (bf16[1024,2048]{1,0:T(8,128)(2,1)S(1)}, bf16[1024,2048]{1,0:T(8,128)(2,1)S(1)}) custom-call(bf16[1024,2048]{1,0:T(8,128)(2,1)S(1)} %copy-done.19, bf16[1024,2048]{1,0:T(8,128)(2,1)} %all-gather.8.cloned.1.call-done.own_ref, bf16[1024,2048]{1,0:T(8,128)(2,1)} %collective-permute-done.10.other_ref, bf16[1024,2048]{1,0:T(8,128)(2,1)} %copy-done.25, ...), custom_call_target="tpu_custom_call" | custom-call | tf_op jit(solution)/shard_map/gating_product/pallas_call | solution.py:775
  232.4 6.1 %fusion.70 = f32[1024,1024]{1,0:T(8,128)} fusion(bf16[1024,2048]{1,0:T(8,128)(2,1)S(1)} %get-tuple-element.143, bf16[1024,2048]{1,0:T(8,128)(2,1)S(1)} %copy-done.63), kind=kOutput, calls=%fused_computation.127 | convolution fusion | flops 4294967296 | bytes 12582912 | tf_op jit(solution)/shard_map/dot_general | solution.py:28
  238.5 8.2 %fusion.71 = f32[1024,1024]{1,0:T(8,128)} fusion(bf16[1024,2048]{1,0:T(8,128)(2,1)S(1)} %get-tuple-element.143, bf16[1024,2048]{1,0:T(8,128)(2,1)} %collective-permute-done.7.other_ref), kind=kOutput, calls=%fused_computation.128 | convolution fusion | flops 4294967296 | bytes 12582912 | tf_op jit(solution)/shard_map/dot_general | solution.py:28
  246.7 6.1 %add_convert_fusion = bf16[1024,2048]{1,0:T(8,128)(2,1)} fusion(bf16[1024,2048]{1,0:T(8,128)(2,1)S(1)} %collective-permute-done.12, bf16[1024,2048]{1,0:T(8,128)(2,1)S(1)} %get-tuple-element.143, bf16[1024,2048]{1,0:T(8,128)(2,1)S(1)} %copy-done.13), kind=kOutput, calls=%fused_computation | convolution fusion | flops 4301258752 | bytes 14680064 | tf_op jit(solution)/shard_map/dot_general | solution.py:28
  259.6 16.5 %scan_backward.4 = (bf16[1024,1536]{1,0:T(8,128)(2,1)S(1)}, f32[1024,256]{1,0:T(8,128)S(1)}, f32[1024,256]{1,0:T(8,128)S(1)}, f32[1,8,1024]{2,1,0:T(8,128)S(1)}, f32[8,512]{1,0:T(8,128)S(1)}) custom-call(s32[1]{0:T(128)S(6)} %copy.173.prefix_ref, bf16[1024,2048]{1,0:T(8,128)(2,1)S(1)} %copy-done.1, bf16[1024,2048]{1,0:T(8,128)(2,1)} %copy-done.4, ...), custom_call_target="tpu_custom_call" | custom-call | tf_op jit(solution)/shard_map/scan_backward/pallas_call | solution.py:510
  276.2 17.0 %scan_backward.5 = (bf16[1024,1536]{1,0:T(8,128)(2,1)S(1)}, f32[1024,256]{1,0:T(8,128)S(1)}, f32[1024,256]{1,0:T(8,128)S(1)}, f32[1,8,1024]{2,1,0:T(8,128)S(1)}, f32[8,512]{1,0:T(8,128)S(1)}) custom-call(s32[1]{0:T(128)S(6)} %copy.173.prefix_ref, bf16[1024,2048]{1,0:T(8,128)(2,1)S(1)} %copy-done.1, ...), custom_call_target="tpu_custom_call", output_to_operand_aliasing={{1}: (9, {}), {2}: (10, {}), {0}: (11, {})} | custom-call | tf_op jit(solution)/shard_map/scan_backward/pallas_call | solution.py:510
  293.2 16.7 %scan_backward.6 = (bf16[1024,1536]{1,0:T(8,128)(2,1)S(1)}, f32[1024,256]{1,0:T(8,128)S(1)}, f32[1024,256]{1,0:T(8,128)S(1)}, f32[1,8,1024]{2,1,0:T(8,128)S(1)}, f32[8,512]{1,0:T(8,128)S(1)}) custom-call(s32[1]{0:T(128)S(6)} %copy.173.prefix_ref, bf16[1024,2048]{1,0:T(8,128)(2,1)S(1)} %copy-done.1, ...), custom_call_target="tpu_custom_call", output_to_operand_aliasing={{1}: (9, {}), {2}: (10, {}), {0}: (11, {})} | custom-call | tf_op jit(solution)/shard_map/scan_backward/pallas_call | solution.py:510
  312.5 6.1 %convolution_convert_fusion = bf16[1024,1536]{1,0:T(8,128)(2,1)S(1)} fusion(bf16[1024,1536]{1,0:T(8,128)(2,1)} %copy-done.20, bf16[1024,2048]{1,0:T(8,128)(2,1)} %copy-done.11), kind=kOutput, calls=%fused_computation.14 | convolution fusion | flops 3222798336 | bytes 8388608 | tf_op jit(solution)/shard_map/dot_general | solution.py:28
  318.8 7.1 %fusion.12 = f32[1024,1024]{1,0:T(8,128)} fusion(f32[1024,1024]{1,0:T(8,128)S(1)} %copy-done.64, bf16[1024,1536]{1,0:T(8,128)(2,1)S(1)} %copy-done.21, bf16[1024,2432]{1,0:T(8,128)(2,1)} %all-gather.4.cloned.1.call-done), kind=kOutput, calls=%fused_computation.25 | convolution fusion | flops 3222274048 | bytes 14680064 | tf_op jit(solution)/shard_map/dot_general | solution.py:28
  325.9 7.1 %fusion.15 = f32[1024,1024]{1,0:T(8,128)} fusion(f32[1024,1024]{1,0:T(8,128)S(1)} %copy-done.65, bf16[1024,1536]{1,0:T(8,128)(2,1)S(1)} %copy-done.21, bf16[1024,2432]{1,0:T(8,128)(2,1)} %collective-permute-done.6), kind=kOutput, calls=%fused_computation.26 | convolution fusion | flops 3222274048 | bytes 14680064 | tf_op jit(solution)/shard_map/dot_general | solution.py:28
  333.1 5.0 %add_convert_fusion.3 = bf16[1024,1536]{1,0:T(8,128)(2,1)} fusion(bf16[1024,1536]{1,0:T(8,128)(2,1)S(1)} %collective-permute-done.15, bf16[1024,1536]{1,0:T(8,128)(2,1)S(1)} %copy-done.21, bf16[1024,2048]{1,0:T(8,128)(2,1)S(1)} %copy-done.14), kind=kOutput, calls=%fused_computation.3 | convolution fusion | flops 3225944064 | bytes 11534336 | tf_op jit(solution)/shard_map/dot_general | solution.py:28
  350.5 15.8 %scan_backward.7 = (bf16[1024,512]{1,0:T(8,128)(2,1)S(1)}, f32[1024,256]{1,0:T(8,128)S(1)}, f32[1024,256]{1,0:T(8,128)S(1)}, f32[1,8,1024]{2,1,0:T(8,128)S(1)}, f32[8,512]{1,0:T(8,128)S(1)}) custom-call(s32[1]{0:T(128)S(6)} %copy.173.prefix_ref, bf16[1024,2048]{1,0:T(8,128)(2,1)S(1)} %copy-done.2, ...), custom_call_target="tpu_custom_call", output_to_operand_aliasing={{1}: (9, {}), {2}: (10, {})} | custom-call | tf_op jit(solution)/shard_map/scan_backward/pallas_call | solution.py:510
  402.9 6.4 %add_branch.1 = f32[512,2048]{1,0:T(8,128)} custom-call(s32[16]{0:T(128)} %copy-done.42, s32[2]{0:T(128)} %copy-done.41, bf16[512,2048]{1,0:T(8,128)(2,1)} %hidden_ref.3, bf16[1024,1024]{1,0:T(8,128)(2,1)} %get-tuple-element.199.refs_0_, bf16[512,1024]{1,0:T(8,128)(2,1)} %collective-permute-done.13.refs_1_, bf16[1024,1024]{1,0:T(8,128)(2,1)} %get-tuple-element.201.refs_2_, ...), custom_call_target="tpu_custom_call" | custom-call | tf_op jit(solution)/shard_map/add_branch/pallas_call | solution.py:644
  418.6 6.8 %collective-permute-done.18.refs_1_ = bf16[512,1024]{1,0:T(8,128)(2,1)} collective-permute-done((bf16[512,1024]{1,0:T(8,128)(2,1)}, bf16[512,1024]{1,0:T(8,128)(2,1)}, u32[]{:S(2)}, u32[]{:S(2)}) %collective-permute-start.18) | collective-permute-done | bytes 1048608 | tf_op jit(solution)/shard_map/ppermute | solution.py:807
  432.0 14.8 %reduce-scatter.14.cloned.1.call-done = bf16[128,512]{1,0:T(8,128)(2,1)} async-done(((bf16[1024,512]{1,0:T(8,128)(2,1)}), bf16[128,512]{1,0:T(8,128)(2,1)}) %reduce-scatter.14.cloned.1.call-update) | async-done | bytes 131088 | tf_op jit(solution)/shard_map/reduce_scatter | solution.py:830
  461.3 8.0 %finish.1 = f32[512,2048]{1,0:T(8,128)} custom-call(s32[16]{0:T(128)} %copy-done.42, s32[2]{0:T(128)} %copy-done.41, bf16[512,2048]{1,0:T(8,128)(2,1)} %hidden_ref.3, bf16[512,2048]{1,0:T(8,128)(2,1)} %cot_ref.1, f32[1,2048]{1,0:T(1,128)} %bitcast.62, bf16[1024,1024]{1,0:T(8,128)(2,1)} %add_convert_fusion.5.refs_0_, ...), custom_call_target="tpu_custom_call" | custom-call | tf_op jit(solution)/shard_map/finish/pallas_call | solution.py:644
  (322 shorter events, 157.8 us)
Async XLA Ops:
  7.2 64.0 %copy-start.6 = (bf16[512,2048]{1,0:T(8,128)(2,1)S(1)}, bf16[512,2048]{1,0:T(8,128)(2,1)}, u32[]{:S(2)}) copy-start(bf16[512,2048]{1,0:T(8,128)(2,1)} %hidden_ref.3) | copy-start | bytes 6291460
  7.2 61.7 %all-gather.4.cloned.1.call-start = ((), (), s32[]{:S(2)}) async-start(), calls=%async_computation.5 | async-start | bytes 5603328 | tf_op jit(solution)/shard_map/all_gather | solution.py:815
  10.3 121.7 %all-gather.6.cloned.1.call-start = ((), (), s32[]{:S(2)}) async-start(), calls=%async_computation.6 | async-start | bytes 4718592 | tf_op jit(solution)/shard_map/all_gather | solution.py:815
  10.3 49.0 %collective-permute-start = (bf16[512,2048]{1,0:T(8,128)(2,1)}, bf16[512,2048]{1,0:T(8,128)(2,1)}, u32[]{:S(2)}, u32[]{:S(2)}) collective-permute-start(bf16[512,2048]{1,0:T(8,128)(2,1)} %hidden_ref.3), channel_id=1, source_target_pairs={{0,1},{1,0},{2,3},{3,2},{4,5},{5,4},{6,7},{7,6},{8,9},{9,8},{10,11... | collective-permute-start | bytes 6291464 | tf_op jit(solution)/shard_map/ppermute | solution.py:807
  16.7 1.2 collective-permute-start.1
  17.9 3.7 collective-permute-start.2
  21.6 3.8 collective-permute-start.3
  23.3 165.0 %all-gather.8.cloned.1.call-start = ((), (), s32[]{:S(2)}) async-start(), calls=%async_computation.7 | async-start | bytes 4718592 | tf_op jit(solution)/shard_map/all_gather | solution.py:815
  25.5 5.0 %collective-permute-start.4 = (bf16[8,896]{1,0:T(8,128)(2,1)S(1)}, bf16[8,896]{1,0:T(8,128)(2,1)S(1)}, u32[]{:S(2)}, u32[]{:S(2)}) collective-permute-start(bf16[8,896]{1,0:T(8,128)(2,1)S(1)} %pad_maximum_fusion.1), channel_id=1, source_target_pairs={{0,16},{2,18},{4,20},{6,22},{8,24},{10,26},{12,28},{14,30},{16,0},... | collective-permute-start | bytes 43016 | tf_op jit(solution)/shard_map/ppermute | solution.py:822
  68.9 15.9 %collective-permute-start.6 = (bf16[1024,2432]{1,0:T(8,128)(2,1)}, bf16[1024,2432]{1,0:T(8,128)(2,1)}, u32[]{:S(2)}, u32[]{:S(2)}) collective-permute-start(bf16[1024,2432]{1,0:T(8,128)(2,1)} %all-gather.4.cloned.1.call-done), channel_id=1, source_target_pairs={{0,2},{2,0},{4,6},{6,4},{8,10},{10,8},{12,14},{14,12},{16,18},{18,... | collective-permute-start | bytes 14942216 | tf_op jit(solution)/shard_map/ppermute | solution.py:803
  69.6 94.0 %copy-start.41 = (s32[2]{0:T(128)}, s32[2]{0:T(128)S(1)}, u32[]{:S(2)}) copy-start(s32[2]{0:T(128)S(1)} %pad_add_fusion.1.slots_ref) | copy-start | bytes 28
  69.7 94.0 %copy-start.42 = (s32[16]{0:T(128)}, s32[16]{0:T(128)S(1)}, u32[]{:S(2)}) copy-start(s32[16]{0:T(128)S(1)} %pad_add_fusion.lanes_ref) | copy-start | bytes 196
  69.7 61.0 %collective-permute-start.5 = (bf16[512,2048]{1,0:T(8,128)(2,1)}, bf16[512,2048]{1,0:T(8,128)(2,1)S(1)}, u32[]{:S(2)}, u32[]{:S(2)}) collective-permute-start(bf16[512,2048]{1,0:T(8,128)(2,1)} %cot_ref.1), channel_id=1, source_target_pairs={{0,1},{1,0},{2,3},{3,2},{4,5},{5,4},{6,7},{7,6},{8,9},{9,8},{10,11... | collective-permute-start | bytes 6291464 | tf_op jit(solution)/shard_map/ppermute | solution.py:807
  132.0 12.6 %collective-permute-start.7 = (bf16[1024,2048]{1,0:T(8,128)(2,1)}, bf16[1024,2048]{1,0:T(8,128)(2,1)}, u32[]{:S(2)}, u32[]{:S(2)}) collective-permute-start(bf16[1024,2048]{1,0:T(8,128)(2,1)} %all-gather.6.cloned.1.call-done), channel_id=1, source_target_pairs={{0,2},{2,0},{4,6},{6,4},{8,10},{10,8},{12,14},{14,12},{16,18},{18,... | collective-permute-start | bytes 12582920 | tf_op jit(solution)/shard_map/ppermute | solution.py:803
  133.3 179.2 %reduce-scatter.6.cloned.1.call-start = ((), (), s32[]{:S(2)}) async-start(), calls=%async_computation.8 | async-start | bytes 4718592 | tf_op jit(solution)/shard_map/reduce_scatter | solution.py:830
  159.7 3.7 collective-permute-start.8
  174.6 7.2 %collective-permute-start.9 = (bf16[1024,2048]{1,0:T(8,128)(2,1)S(1)}, bf16[1024,2048]{1,0:T(8,128)(2,1)S(1)}, u32[]{:S(2)}, u32[]{:S(2)}) collective-permute-start(bf16[1024,2048]{1,0:T(8,128)(2,1)S(1)} %convolution_convert_fusion.2), channel_id=1, source_target_pairs={{0,2},{2,0},{4,6},{6,4},{8,10},{10,8},{12,14},{14,12},{16,18},{18,... | collective-permute-start | bytes 12582920 | tf_op jit(solution)/shard_map/ppermute | solution.py:803
  188.3 8.2 %collective-permute-start.10 = (bf16[1024,2048]{1,0:T(8,128)(2,1)}, bf16[1024,2048]{1,0:T(8,128)(2,1)}, u32[]{:S(2)}, u32[]{:S(2)}) collective-permute-start(bf16[1024,2048]{1,0:T(8,128)(2,1)} %all-gather.8.cloned.1.call-done.own_ref), channel_id=1, source_target_pairs={{0,2},{2,0},{4,6},{6,4},{8,10},{10,8},{12,14},{14,12},{16,18},{18,... | collective-permute-start | bytes 12582920 | tf_op jit(solution)/shard_map/ppermute | solution.py:803
  188.5 124.0 %reduce-scatter.8.cloned.1.call-start = ((), (), s32[]{:S(2)}) async-start(), calls=%async_computation.9 | async-start | bytes 4718592 | tf_op jit(solution)/shard_map/reduce_scatter | solution.py:830
  205.5 3.6 collective-permute-start.11
  232.3 14.4 %collective-permute-start.12 = (bf16[1024,2048]{1,0:T(8,128)(2,1)S(1)}, bf16[1024,2048]{1,0:T(8,128)(2,1)S(1)}, u32[]{:S(2)}, u32[]{:S(2)}) collective-permute-start(bf16[1024,2048]{1,0:T(8,128)(2,1)S(1)} %convolution_convert_fusion.1), channel_id=1, source_target_pairs={{0,2},{2,0},{4,6},{6,4},{8,10},{10,8},{12,14},{14,12},{16,18},{18,... | collective-permute-start | bytes 12582920 | tf_op jit(solution)/shard_map/ppermute | solution.py:803
  252.9 133.1 %reduce-scatter.10.cloned.1.call-start = ((), (), s32[]{:S(2)}) async-start(), calls=%async_computation.10 | async-start | bytes 3538944 | tf_op jit(solution)/shard_map/reduce_scatter | solution.py:830
  256.2 56.3 %collective-permute-start.14 = (bf16[512,1024]{1,0:T(8,128)(2,1)S(1)}, bf16[512,1024]{1,0:T(8,128)(2,1)}, u32[]{:S(2)}, u32[]{:S(2)}) collective-permute-start(bf16[512,1024]{1,0:T(8,128)(2,1)S(1)} %constant_dynamic-slice_fusion.2), channel_id=1, source_target_pairs={{0,1},{1,0},{2,3},{3,2},{4,5},{5,4},{6,7},{7,6},{8,9},{9,8},{10,11... | collective-permute-start | bytes 3145736 | tf_op jit(solution)/shard_map/ppermute | solution.py:807
  257.2 55.3 %collective-permute-start.13 = (bf16[512,1024]{1,0:T(8,128)(2,1)S(1)}, bf16[512,1024]{1,0:T(8,128)(2,1)}, u32[]{:S(2)}, u32[]{:S(2)}) collective-permute-start(bf16[512,1024]{1,0:T(8,128)(2,1)S(1)} %constant_dynamic-slice_fusion.3), channel_id=1, source_target_pairs={{0,1},{1,0},{2,3},{3,2},{4,5},{5,4},{6,7},{7,6},{8,9},{9,8},{10,11... | collective-permute-start | bytes 3145736 | tf_op jit(solution)/shard_map/ppermute | solution.py:807
  318.7 14.3 %collective-permute-start.15 = (bf16[1024,1536]{1,0:T(8,128)(2,1)S(1)}, bf16[1024,1536]{1,0:T(8,128)(2,1)S(1)}, u32[]{:S(2)}, u32[]{:S(2)}) collective-permute-start(bf16[1024,1536]{1,0:T(8,128)(2,1)S(1)} %convolution_convert_fusion), channel_id=1, source_target_pairs={{0,2},{2,0},{4,6},{6,4},{8,10},{10,8},{12,14},{14,12},{16,18},{18,... | collective-permute-start | bytes 9437192 | tf_op jit(solution)/shard_map/ppermute | solution.py:803
  338.1 87.3 %reduce-scatter.12.cloned.1.call-start = ((), (), s32[]{:S(2)}) async-start(), calls=%async_computation.11 | async-start | bytes 1363968 | tf_op jit(solution)/shard_map/reduce_scatter | solution.py:830
  378.4 5.0 %collective-permute-start.16 = (f32[1024,295]{0,1:T(8,128)}, f32[1024,295]{0,1:T(8,128)}, u32[]{:S(2)}, u32[]{:S(2)}) collective-permute-start(f32[1024,295]{0,1:T(8,128)} %pad_maximum_fusion), channel_id=1, source_target_pairs={{0,2},{2,0},{4,6},{6,4},{8,10},{10,8},{12,14},{14,12},{16,18},{18,... | collective-permute-start | bytes 3624968 | tf_op jit(solution)/shard_map/ppermute | solution.py:803
  386.0 60.8 %reduce-scatter.14.cloned.1.call-start = ((), (), s32[]{:S(2)}) async-start(), calls=%async_computation.12 | async-start | bytes 1179648 | tf_op jit(solution)/shard_map/reduce_scatter | solution.py:830
  386.2 7.5 %collective-permute-start.17 = (bf16[1024,512]{1,0:T(8,128)(2,1)S(1)}, bf16[1024,512]{1,0:T(8,128)(2,1)}, u32[]{:S(2)}, u32[]{:S(2)}) collective-permute-start(bf16[1024,512]{1,0:T(8,128)(2,1)S(1)} %fusion.41), channel_id=1, source_target_pairs={{0,2},{2,0},{4,6},{6,4},{8,10},{10,8},{12,14},{14,12},{16,18},{18,... | collective-permute-start | bytes 3145736 | tf_op jit(solution)/shard_map/ppermute | solution.py:803
  399.6 25.9 %collective-permute-start.18 = (bf16[512,1024]{1,0:T(8,128)(2,1)}, bf16[512,1024]{1,0:T(8,128)(2,1)}, u32[]{:S(2)}, u32[]{:S(2)}) collective-permute-start(bf16[512,1024]{1,0:T(8,128)(2,1)} %constant_dynamic-slice_fusion.1), channel_id=1, source_target_pairs={{0,1},{1,0},{2,3},{3,2},{4,5},{5,4},{6,7},{7,6},{8,9},{9,8},{10,11... | collective-permute-start | bytes 3145736 | tf_op jit(solution)/shard_map/ppermute | solution.py:807
  430.8 25.1 %collective-permute-start.19 = (bf16[512,1024]{1,0:T(8,128)(2,1)}, bf16[512,1024]{1,0:T(8,128)(2,1)}, u32[]{:S(2)}, u32[]{:S(2)}) collective-permute-start(bf16[512,1024]{1,0:T(8,128)(2,1)} %constant_dynamic-slice_fusion), channel_id=1, source_target_pairs={{0,1},{1,0},{2,3},{3,2},{4,5},{5,4},{6,7},{7,6},{8,9},{9,8},{10,11... | collective-permute-start | bytes 3145736 | tf_op jit(solution)/shard_map/ppermute | solution.py:807
  456.7 12.6 %collective-permute-start.20 = (f32[32960]{0:T(1024)S(1)}, f32[32960]{0:T(1024)S(1)}, u32[]{:S(2)}, u32[]{:S(2)}) collective-permute-start(f32[32960]{0:T(1024)S(1)} %concatenate.55), channel_id=1, source_target_pairs={{0,1},{1,0},{2,3},{3,2},{4,5},{5,4},{6,7},{7,6},{8,9},{9,8},{10,11... | collective-permute-start | bytes 395528 | tf_op jit(solution)/shard_map/ppermute | solution.py:807
  (64 other events, 721.9 us)
Sparse Core Ops, SparseCore 0:
  10.4 58.4 all-gather.3
  70.4 47.9 all-gather.5
  133.4 47.4 all-gather.7
  188.6 48.0 reduce-scatter.5
  253.0 48.0 reduce-scatter.7
  338.2 38.7 reduce-scatter.9
  386.1 29.4 reduce-scatter.11
  418.4 28.2 reduce-scatter.13

commit v3 on v2

--- a/solution.py
+++ b/solution.py
@@ -476,13 +476,15 @@
     if chunks > anti:
         lax.fori_loop(0, chunks - anti, lambda i, _: chunk_body(chunks - 1 - i, False), 0, unroll=4)
     lax.fori_loop(0, anti, lambda i, _: chunk_body(anti - 1 - i, True), 0, unroll=4)
-
-
-def scan_backward(prefix, x_pre, grad_ssd, taps, skip, cols, rows, act, states, group, place, places, gx, before):
-    length, channels = x_pre.shape
+    by_head = low_pair_dot(jnp.broadcast_to(gsum_ref[4:5, :], (8, width)), collect)
+    gsum_ref[5:6, 0:128] = by_head[0:1]
+
+
+def scan_backward(prefix, x_pre, grad_ssd, taps, skip, cols, rows, act, states, group, column, place, places, gx, before):
+    length, heads = x_pre.shape[0], taps.shape[1] // P_SIZE
     chunks = length // Q
     anti = min(MAX_PREFIX // Q, chunks)
-    wide = pl.BlockSpec((length, CG), lambda i: (0, group))
+    wide = pl.BlockSpec((length, CG), lambda i: (0, column))
     given = [prefix, x_pre, grad_ssd, taps, skip, cols, rows, act, states]
     in_specs = [
         pl.BlockSpec(memory_space=pltpu.SMEM),
@@ -508,7 +510,7 @@
         given.append(gx)
         in_specs.append(pl.BlockSpec(memory_space=pl.ANY))
     return pl.pallas_call(
-        functools.partial(backward_kernel, channels // P_SIZE, group * HG, before is not None),
+        functools.partial(backward_kernel, heads, group * HG, before is not None),
         grid=(1,),
         in_specs=in_specs,
         out_specs=[
@@ -540,7 +542,7 @@
     )(*given)
 
 
-TILE = 128
+TILE = 256
 
 
 def block_of(lanes_ref, j):
@@ -569,22 +571,23 @@
 
 def place_tokens(lanes, slots, sources, by, normalize):
     tokens, width = sources[0].shape
-    count, tiles = len(sources), tokens // TILE
+    size = min(TILE, tokens)
+    count, tiles = len(sources), tokens // size
 
     def source(k):
-        return pl.BlockSpec((TILE, width), lambda i, a, s: (jnp.clip(i - k * tiles, 0, tiles - 1), 0))
+        return pl.BlockSpec((size, width), lambda i, a, s: (jnp.clip(i - k * tiles, 0, tiles - 1), 0))
 
     def placed(i, a, s):
         return (s[i // tiles] * tiles + i % tiles, 0)
 
-    by_spec = pl.BlockSpec((1, width), lambda i, a, s: (0, 0)) if normalize else pl.BlockSpec((TILE, 1), placed)
+    by_spec = pl.BlockSpec((1, width), lambda i, a, s: (0, 0)) if normalize else pl.BlockSpec((size, 1), placed)
     return pl.pallas_call(
         functools.partial(place_kernel, normalize, count, tiles),
         grid_spec=pltpu.PrefetchScalarGridSpec(
             num_scalar_prefetch=2,
             grid=(count * tiles,),
             in_specs=[source(k) for k in range(count)] + [by_spec],
-            out_specs=pl.BlockSpec((TILE, width), placed),
+            out_specs=pl.BlockSpec((size, width), placed),
         ),
         out_shape=jax.ShapeDtypeStruct((tokens * count, width), BF16),
         compiler_params=pltpu.CompilerParams(vmem_limit_bytes=32 * MIB),
@@ -616,7 +619,7 @@
     blocks = width // 128
     wide = hidden_ref[...].astype(F32)
     inv = lax.rsqrt(jnp.sum(wide * wide, axis=-1, keepdims=True) / width + EPSILON)
-    total = jnp.zeros((TILE, 128), F32)
+    total = jnp.zeros((hidden_ref.shape[0], 128), F32)
     for j in range(blocks):
         there = block_of(lanes_ref, j)
         scaled = half_sum(refs[:-1], j, blocks // 2) * gain_ref[:, there]
@@ -628,8 +631,9 @@
 
 def own_rows(kernel, name, lanes, slots, hidden, more, gain, halves):
     tokens, width = hidden.shape
-    tiles = tokens // TILE
-    tile = pl.BlockSpec((TILE, width), lambda i, a, s: (i, 0))
+    size = min(TILE, tokens)
+    tiles = tokens // size
+    tile = pl.BlockSpec((size, width), lambda i, a, s: (i, 0))
     given, specs = [hidden, *more], [tile] * (1 + len(more))
     if gain is not None:
         given.append(gain)
@@ -638,9 +642,9 @@
         for array, whole in half:
             given.append(array)
             if whole:
-                specs.append(pl.BlockSpec((TILE, width // 2), lambda i, a, s: (s[0] * tiles + i, 0)))
+                specs.append(pl.BlockSpec((size, width // 2), lambda i, a, s: (s[0] * tiles + i, 0)))
             else:
-                specs.append(pl.BlockSpec((TILE, width // 2), lambda i, a, s: (i, 0)))
+                specs.append(pl.BlockSpec((size, width // 2), lambda i, a, s: (i, 0)))
     return pl.pallas_call(
         kernel,
         grid_spec=pltpu.PrefetchScalarGridSpec(
@@ -651,6 +655,25 @@
         cost_estimate=NO_COST,
         name=name,
     )(lanes, slots, *given)
+
+
+def turn_kernel(v_ref, out_ref):
+    for j in range(out_ref.shape[0] // 128):
+        here = slice(j * 128, j * 128 + 128)
+        out_ref[here, :] = v_ref[:, here].astype(F32).T
+
+
+def turned(v):
+    rows, columns = v.shape
+    if rows % 128:
+        return v.astype(F32).T
+    return pl.pallas_call(
+        turn_kernel,
+        out_shape=jax.ShapeDtypeStruct((columns, rows), F32),
+        compiler_params=pltpu.CompilerParams(vmem_limit_bytes=32 * MIB),
+        cost_estimate=NO_COST,
+        name="turned",
+    )(v)
 
 
 def post_kernel(rest_ref, taps_ref, decay_ref, bias_ref, *refs):
@@ -996,9 +1019,11 @@
 
     def back_through(start, stop, dy, before):
         gx = None
+        dy = dy[:, start * CG : stop * CG] if start else dy
         for g in range(start, stop):
             gx, gact, gcol, grow, gsum = scan_backward(
-                prefix, x_pre, dy, x_taps, skip, cols, head_rows, act, states[g], g, g - start, stop - start, gx, before
+                prefix, x_pre[:, start * CG : stop * CG] if start else x_pre, dy, x_taps, skip, cols, head_rows, act, states[g],
+                g, g - start, g - start, stop - start, gx, before
             )
             before = (gact, gcol)
             grows.append(grow)
@@ -1029,7 +1054,7 @@
     gsum = jnp.concatenate(gsums, axis=1)
     gx_taps = jnp.transpose(gsum[0:4].reshape(4, heads, fsdp, taps_own), (2, 1, 0, 3))
     g_taps = jnp.transpose(gbc_taps[0:4].reshape(4, fsdp, -1), (1, 0, 2))
-    g_skip = jnp.sum(gsum[4].reshape(heads, P_SIZE), axis=-1)
+    g_skip = sum(v[5, :heads] for v in gsums)
     per_head = jnp.concatenate([ghead[0, :heads], ghead[1, :heads], g_skip])
     slices = jnp.concatenate(
         [
@@ -1073,7 +1098,7 @@
             [list(zip(half, kind)) for half, kind in zip(branch_parts, kinds)],
         )
     )
-    grad_z, grad_out = grad_z.astype(F32), grad_out.astype(F32).T
+    grad_z, grad_out = grad_z.astype(F32), turned(grad_out)
     arrived = [v for v, _ in part_sums[0]]
     second, (arrived, mixed, grad_out, grad_z, mine_rest) = tie(
         second, (arrived, mixed, grad_out, grad_z, mine_rest)

time: 487 us -> 487 us (level)
    unnamed x144 -> x136, local copies, waits for them, and re-layouts: 38.9 us -> 32.5 us
    pallas_call x4 -> x5, Pallas kernels: 66 us -> 67.3 us  [the longest x4 66.1 us: scan_backward(): pl.pallas_call(functools.partial(backward_kernel, heads, group * HG, befo...]
  transfers between devices with their start and end apart: 29 -> 29, of which waited for: 11 -> 11; matrix products, arithmetic and copies ran while one was open for 35% -> 36% of each run, Pallas kernels for 31% -> 31%
where the time goes in v3:
time: 487 us; the launch traced here: 477 us
  Pallas kernels  146 us (30%)
  matrix products  134 us (28%)
  waiting for transfers between devices  77 us (16%)
  local copies, waits for them, and re-layouts  63.1 us (13%)
  starting transfers between devices  21.2 us (4%)
  other arithmetic  20.5 us (4%)
  between operations  16.1 us (3%)
    dot_general x25, matrix products, dot(): return lax.dot_general(a, b, (dims, ((), ())), preferred_element_type=F32)  134 us
    pallas_call x4, Pallas kernels, scan_backward(): pl.pallas_call(functools.partial(backward_kernel, heads, group * HG, befo...  66.1 us
    ppermute x9, waiting for transfers between devices, other_half(): return lax.ppermute(v, 'tp', [(0, 1), (1, 0)])  37 us
    unnamed x136, local copies, waits for them, and re-layouts  32.5 us
    pallas_call x4, Pallas kernels, scan_forward(): pl.pallas_call(functools.partial(forward_kernel, channels // P_SIZE, grou...  27 us
    reduce_scatter x5, waiting for transfers between devices, scatter(): lax.psum_scatter(v, 'fsdp', scatter_dimension=0, tiled=True, axis_index_g...  16.2 us
    pallas_call x1, Pallas kernels, gating_product(): pl.pallas_call(gating_kernel, grid=(channels // CG,), in_specs=[pl.BlockS...  15.8 us
    pallas_call x2, Pallas kernels, own_rows(): pl.pallas_call(kernel, grid_spec=pltpu.PrefetchScalarGridSpec(num_scalar_...  13.3 us
  transfers between devices with their start and end apart: 29, of which 11 were waited for; matrix products, arithmetic and copies ran while one was open for 36% of the time, Pallas kernels for 31%

profile of v3, /device:TPU:0, one launch (start us, length us, event | category | flops | bytes accessed | tf_op | source)
XLA Modules:
  0.0 477.4 jit_solution(2297807601332283117)
XLA Ops:
  35.1 24.2 %collective-permute-done.refs_1_ = bf16[512,2048]{1,0:T(8,128)(2,1)} collective-permute-done((bf16[512,2048]{1,0:T(8,128)(2,1)}, bf16[512,2048]{1,0:T(8,128)(2,1)}, u32[]{:S(2)}, u32[]{:S(2)}) %collective-permute-start) | collective-permute-done | bytes 2097184 | tf_op jit(solution)/shard_map/ppermute | solution.py:830
  59.3 9.6 %all-gather.4.cloned.1.call-done = bf16[1024,2432]{1,0:T(8,128)(2,1)} async-done(((bf16[128,2432]{1,0:T(8,128)(2,1)}), bf16[1024,2432]{1,0:T(8,128)(2,1)}) %all-gather.4.cloned.1.call-update) | async-done | bytes 4980752 | tf_op jit(solution)/shard_map/all_gather | solution.py:838
  71.2 5.1 %place_tokens.2.a_ref = bf16[1024,2048]{1,0:T(8,128)(2,1)S(1)} custom-call(s32[16]{0:T(128)S(1)} %pad_add_fusion.lanes_ref, s32[2]{0:T(128)S(1)} %pad_add_fusion.1.slots_ref, bf16[512,2048]{1,0:T(8,128)(2,1)S(1)} %copy-done.4, bf16[512,2048]{1,0:T(8,128)(2,1)} %collective-permute-done.refs_1_, f32[1,2048]{1,0:T(1,128)S(1)} %bitcast.61), custom_call_target="tpu_custom_call" | custom-call | tf_op jit(solution)/shard_map/place_tokens/pallas_call | solution.py:584
  76.4 6.7 %fusion.2 = f32[1024,2048]{1,0:T(8,128)} fusion(bf16[1024,2432]{1,0:T(8,128)(2,1)S(1)} %copy-done.57, bf16[1024,2048]{1,0:T(8,128)(2,1)S(1)} %place_tokens.2.a_ref), kind=kOutput, calls=%fused_computation.12 | convolution fusion | flops 4294967296 | bytes 14680064 | tf_op jit(solution)/shard_map/dot_general | solution.py:28
  88.6 8.3 %add_convert_fusion.2.x_ref = bf16[1024,2048]{1,0:T(8,128)(2,1)S(1)} fusion(f32[1024,2048]{1,0:T(8,128)} %fusion.2, bf16[1024,2432]{1,0:T(8,128)(2,1)} %collective-permute-done.6, bf16[1024,2048]{1,0:T(8,128)(2,1)S(1)} %place_tokens.2.a_ref), kind=kOutput, calls=%fused_computation.2 | convolution fusion | flops 4299161600 | bytes 18874368 | tf_op jit(solution)/shard_map/dot_general | solution.py:28
  97.0 6.8 %scan_forward.4 = (bf16[1024,2048]{1,0:T(8,128)(2,1)S(1)}, bf16[8,128,512]{2,1,0:T(8,128)(2,1)S(1)}) custom-call(s32[1]{0:T(128)S(6)} %copy.166.prefix_ref, bf16[1024,2048]{1,0:T(8,128)(2,1)S(1)} %add_convert_fusion.2.x_ref, f32[4,2048]{1,0:T(4,128)S(1)} %reshape.151.taps_ref, f32[1,2048]{1,0:T(1,128)S(1)} %broadcast_in_dim_reshape.3.skip_ref, ...), custom_call_target="tpu_custom_call" | custom-call | tf_op jit(solution)/shard_map/scan_forward/pallas_call | solution.py:253
  104.8 6.6 %scan_forward.5 = (bf16[1024,2048]{1,0:T(8,128)(2,1)S(1)}, bf16[8,128,512]{2,1,0:T(8,128)(2,1)S(1)}) custom-call(s32[1]{0:T(128)S(6)} %copy.166.prefix_ref, bf16[1024,2048]{1,0:T(8,128)(2,1)S(1)} %add_convert_fusion.2.x_ref, f32[4,2048]{1,0:T(4,128)S(1)} %reshape.151.taps_ref, ...), custom_call_target="tpu_custom_call", output_to_operand_aliasing={{0}: (7, {})} | custom-call | tf_op jit(solution)/shard_map/scan_forward/pallas_call | solution.py:253
  112.3 6.9 %scan_forward.6 = (bf16[1024,2048]{1,0:T(8,128)(2,1)S(1)}, bf16[8,128,512]{2,1,0:T(8,128)(2,1)S(1)}) custom-call(s32[1]{0:T(128)S(6)} %copy.166.prefix_ref, bf16[1024,2048]{1,0:T(8,128)(2,1)S(1)} %add_convert_fusion.2.x_ref, f32[4,2048]{1,0:T(4,128)S(1)} %reshape.151.taps_ref, ...), custom_call_target="tpu_custom_call", output_to_operand_aliasing={{0}: (7, {})} | custom-call | tf_op jit(solution)/shard_map/scan_forward/pallas_call | solution.py:253
  119.3 6.7 %scan_forward.7 = (bf16[1024,2048]{1,0:T(8,128)(2,1)S(1)}, bf16[8,128,512]{2,1,0:T(8,128)(2,1)S(1)}) custom-call(s32[1]{0:T(128)S(6)} %copy.166.prefix_ref, bf16[1024,2048]{1,0:T(8,128)(2,1)S(1)} %add_convert_fusion.2.x_ref, f32[4,2048]{1,0:T(4,128)S(1)} %reshape.151.taps_ref, ...), custom_call_target="tpu_custom_call", output_to_operand_aliasing={{0}: (7, {})} | custom-call | tf_op jit(solution)/shard_map/scan_forward/pallas_call | solution.py:253
  132.2 10.8 %fusion.28.part_ref = f32[1024,2048]{1,0:T(8,128)} fusion(bf16[1024,2048]{1,0:T(8,128)(2,1)} %all-gather.6.cloned.1.call-done, bf16[1024,2048]{1,0:T(8,128)(2,1)} %copy-done.5), kind=kOutput, calls=%fused_computation.37 | convolution fusion | flops 4294967296 | bytes 14680064 | tf_op jit(solution)/shard_map/dot_general | solution.py:28
  143.0 10.8 %gate_product.1 = (bf16[1024,2048]{1,0:T(8,128)(2,1)S(1)}, bf16[1024,2048]{1,0:T(8,128)(2,1)S(1)}, f32[1024,128]{1,0:T(8,128)S(1)}) custom-call(bf16[1024,2048]{1,0:T(8,128)(2,1)S(1)} %copy-done.6, bf16[1024,2048]{1,0:T(8,128)(2,1)} %collective-permute-done.7.other_ref, f32[1024,2048]{1,0:T(8,128)} %fusion.28.part_ref, bf16[1024,2048]{1,0:T(8,128)(2,1)} %copy-done.2, ...), custom_call_target="tpu_custom_call" | custom-call | tf_op jit(solution)/shard_map/gate_product/pallas_call | solution.py:760
  167.5 5.0 %convolution_convert_fusion.2 = bf16[1024,2048]{1,0:T(8,128)(2,1)S(1)} fusion(bf16[1024,2048]{1,0:T(8,128)(2,1)S(1)} %copy-done.48, bf16[1024,2048]{1,0:T(8,128)(2,1)S(1)} %place_tokens.3.a_ref), kind=kOutput, calls=%fused_computation.16 | convolution fusion | flops 4297064448 | bytes 10485760 | tf_op jit(solution)/shard_map/dot_general | solution.py:28
  172.5 7.1 %collective-permute-done.9 = bf16[1024,2048]{1,0:T(8,128)(2,1)S(1)} collective-permute-done((bf16[1024,2048]{1,0:T(8,128)(2,1)S(1)}, bf16[1024,2048]{1,0:T(8,128)(2,1)S(1)}, u32[]{:S(2)}, u32[]{:S(2)}) %collective-permute-start.9) | collective-permute-done | bytes 4194336 | tf_op jit(solution)/shard_map/ppermute | solution.py:826
  179.7 6.4 %add_convert_fusion.1 = bf16[1024,2048]{1,0:T(8,128)(2,1)} fusion(bf16[1024,2048]{1,0:T(8,128)(2,1)S(1)} %collective-permute-done.9, bf16[1024,2048]{1,0:T(8,128)(2,1)S(1)} %copy-done.48, bf16[1024,2048]{1,0:T(8,128)(2,1)S(1)} %place_tokens.3.a_ref), kind=kOutput, calls=%fused_computation.1 | convolution fusion | flops 4301258752 | bytes 14680064 | tf_op jit(solution)/shard_map/dot_general | solution.py:28
  186.5 7.7 %fusion.69 = f32[1024,1024]{1,0:T(8,128)S(1)} fusion(bf16[1024,2048]{1,0:T(8,128)(2,1)} %copy-done.47, bf16[1024,2048]{1,0:T(8,128)(2,1)} %all-gather.8.cloned.1.call-done.own_ref), kind=kOutput, calls=%fused_computation.124 | convolution fusion | flops 4294967296 | bytes 12582912 | tf_op jit(solution)/shard_map/dot_general | solution.py:28
  194.3 9.0 %multiply_reduce_fusion = (f32[1024]{0:T(1024)S(1)}, f32[1024]{0:T(1024)S(1)}, bf16[1024,1024]{1,0:T(8,128)(2,1)}, bf16[1024,1024]{1,0:T(8,128)(2,1)}) fusion(bf16[1024,2048]{1,0:T(8,128)(2,1)S(1)} %copy-done.12, f32[1024,1024]{1,0:T(8,128)S(1)} %fusion.69, f32[1024]{0:T(1024)S(1)} %add_rsqrt_fusion, bf16[1024,2048]{1,0:T(8,128)(2,1)S(1)} %copy-done.49, ...), kind=kOutput, calls=%fused_computation.10 | convolution fusion | flops 4305451008 | bytes 20983808 | tf_op jit(solution)/shard_map/dot_general | solution.py:28
  209.4 15.8 %gating_product.1 = (bf16[1024,2048]{1,0:T(8,128)(2,1)S(1)}, bf16[1024,2048]{1,0:T(8,128)(2,1)S(1)}) custom-call(bf16[1024,2048]{1,0:T(8,128)(2,1)S(1)} %copy-done.13, bf16[1024,2048]{1,0:T(8,128)(2,1)} %all-gather.8.cloned.1.call-done.own_ref, bf16[1024,2048]{1,0:T(8,128)(2,1)} %collective-permute-done.10.other_ref, bf16[1024,2048]{1,0:T(8,128)(2,1)} %copy-done.23, ...), custom_call_target="tpu_custom_call" | custom-call | tf_op jit(solution)/shard_map/gating_product/pallas_call | solution.py:798
  230.2 6.1 %fusion.70 = f32[1024,1024]{1,0:T(8,128)} fusion(bf16[1024,2048]{1,0:T(8,128)(2,1)S(1)} %get-tuple-element.143, bf16[1024,2048]{1,0:T(8,128)(2,1)S(1)} %copy-done.61), kind=kOutput, calls=%fused_computation.125 | convolution fusion | flops 4294967296 | bytes 12582912 | tf_op jit(solution)/shard_map/dot_general | solution.py:28
  236.3 8.2 %fusion.71 = f32[1024,1024]{1,0:T(8,128)} fusion(bf16[1024,2048]{1,0:T(8,128)(2,1)S(1)} %get-tuple-element.143, bf16[1024,2048]{1,0:T(8,128)(2,1)} %collective-permute-done.7.other_ref), kind=kOutput, calls=%fused_computation.126 | convolution fusion | flops 4294967296 | bytes 12582912 | tf_op jit(solution)/shard_map/dot_general | solution.py:28
  244.5 6.1 %add_convert_fusion = bf16[1024,2048]{1,0:T(8,128)(2,1)} fusion(bf16[1024,2048]{1,0:T(8,128)(2,1)S(1)} %collective-permute-done.12, bf16[1024,2048]{1,0:T(8,128)(2,1)S(1)} %get-tuple-element.143, bf16[1024,2048]{1,0:T(8,128)(2,1)S(1)} %copy-done.7), kind=kOutput, calls=%fused_computation | convolution fusion | flops 4301258752 | bytes 14680064 | tf_op jit(solution)/shard_map/dot_general | solution.py:28
  257.4 16.5 %scan_backward.4 = (bf16[1024,1536]{1,0:T(8,128)(2,1)S(1)}, f32[1024,256]{1,0:T(8,128)S(1)}, f32[1024,256]{1,0:T(8,128)S(1)}, f32[1,8,1024]{2,1,0:T(8,128)S(1)}, f32[8,512]{1,0:T(8,128)S(1)}) custom-call(s32[1]{0:T(128)S(6)} %copy.166.prefix_ref, bf16[1024,2048]{1,0:T(8,128)(2,1)S(1)} %copy-done.1, bf16[1024,2048]{1,0:T(8,128)(2,1)} %copy-done.3, ...), custom_call_target="tpu_custom_call" | custom-call | tf_op jit(solution)/shard_map/scan_backward/pallas_call | solution.py:512
  273.9 17.0 %scan_backward.5 = (bf16[1024,1536]{1,0:T(8,128)(2,1)S(1)}, f32[1024,256]{1,0:T(8,128)S(1)}, f32[1024,256]{1,0:T(8,128)S(1)}, f32[1,8,1024]{2,1,0:T(8,128)S(1)}, f32[8,512]{1,0:T(8,128)S(1)}) custom-call(s32[1]{0:T(128)S(6)} %copy.166.prefix_ref, bf16[1024,2048]{1,0:T(8,128)(2,1)S(1)} %copy-done.1, ...), custom_call_target="tpu_custom_call", output_to_operand_aliasing={{1}: (9, {}), {2}: (10, {}), {0}: (11, {})} | custom-call | tf_op jit(solution)/shard_map/scan_backward/pallas_call | solution.py:512
  290.9 16.6 %scan_backward.6 = (bf16[1024,1536]{1,0:T(8,128)(2,1)S(1)}, f32[1024,256]{1,0:T(8,128)S(1)}, f32[1024,256]{1,0:T(8,128)S(1)}, f32[1,8,1024]{2,1,0:T(8,128)S(1)}, f32[8,512]{1,0:T(8,128)S(1)}) custom-call(s32[1]{0:T(128)S(6)} %copy.166.prefix_ref, bf16[1024,2048]{1,0:T(8,128)(2,1)S(1)} %copy-done.1, ...), custom_call_target="tpu_custom_call", output_to_operand_aliasing={{1}: (9, {}), {2}: (10, {}), {0}: (11, {})} | custom-call | tf_op jit(solution)/shard_map/scan_backward/pallas_call | solution.py:512
  310.2 6.1 %convolution_convert_fusion = bf16[1024,1536]{1,0:T(8,128)(2,1)S(1)} fusion(bf16[1024,1536]{1,0:T(8,128)(2,1)} %copy-done.18, bf16[1024,2048]{1,0:T(8,128)(2,1)} %copy-done.5), kind=kOutput, calls=%fused_computation.14 | convolution fusion | flops 3222798336 | bytes 8388608 | tf_op jit(solution)/shard_map/dot_general | solution.py:28
  316.5 7.1 %fusion.12 = f32[1024,1024]{1,0:T(8,128)} fusion(f32[1024,1024]{1,0:T(8,128)S(1)} %copy-done.62, bf16[1024,1536]{1,0:T(8,128)(2,1)S(1)} %copy-done.19, bf16[1024,2432]{1,0:T(8,128)(2,1)} %all-gather.4.cloned.1.call-done), kind=kOutput, calls=%fused_computation.25 | convolution fusion | flops 3222274048 | bytes 14680064 | tf_op jit(solution)/shard_map/dot_general | solution.py:28
  323.6 7.1 %fusion.15 = f32[1024,1024]{1,0:T(8,128)} fusion(f32[1024,1024]{1,0:T(8,128)S(1)} %copy-done.63, bf16[1024,1536]{1,0:T(8,128)(2,1)S(1)} %copy-done.19, bf16[1024,2432]{1,0:T(8,128)(2,1)} %collective-permute-done.6), kind=kOutput, calls=%fused_computation.26 | convolution fusion | flops 3222274048 | bytes 14680064 | tf_op jit(solution)/shard_map/dot_general | solution.py:28
  330.7 5.0 %add_convert_fusion.3 = bf16[1024,1536]{1,0:T(8,128)(2,1)} fusion(bf16[1024,1536]{1,0:T(8,128)(2,1)S(1)} %collective-permute-done.15, bf16[1024,1536]{1,0:T(8,128)(2,1)S(1)} %copy-done.19, bf16[1024,2048]{1,0:T(8,128)(2,1)S(1)} %copy-done.8), kind=kOutput, calls=%fused_computation.3 | convolution fusion | flops 3225944064 | bytes 11534336 | tf_op jit(solution)/shard_map/dot_general | solution.py:28
  351.0 16.0 %scan_backward.7 = (bf16[1024,512]{1,0:T(8,128)(2,1)S(1)}, f32[1024,256]{1,0:T(8,128)S(1)}, f32[1024,256]{1,0:T(8,128)S(1)}, f32[1,8,1024]{2,1,0:T(8,128)S(1)}, f32[8,512]{1,0:T(8,128)S(1)}) custom-call(s32[1]{0:T(128)S(6)} %copy.166.prefix_ref, bf16[1024,512]{1,0:T(8,128)(2,1)S(1)} %copy-done.24, ...), custom_call_target="tpu_custom_call", output_to_operand_aliasing={{1}: (9, {}), {2}: (10, {})} | custom-call | tf_op jit(solution)/shard_map/scan_backward/pallas_call | solution.py:512
  403.7 5.3 %add_branch.1 = f32[512,2048]{1,0:T(8,128)} custom-call(s32[16]{0:T(128)} %copy-done.42, s32[2]{0:T(128)} %copy-done.41, bf16[512,2048]{1,0:T(8,128)(2,1)} %hidden_ref.3, bf16[1024,1024]{1,0:T(8,128)(2,1)} %get-tuple-element.199.refs_0_, bf16[512,1024]{1,0:T(8,128)(2,1)} %collective-permute-done.13.refs_1_, bf16[1024,1024]{1,0:T(8,128)(2,1)} %get-tuple-element.201.refs_2_, ...), custom_call_target="tpu_custom_call" | custom-call | tf_op jit(solution)/shard_map/add_branch/pallas_call | solution.py:648
  418.3 7.5 %collective-permute-done.18.refs_1_ = bf16[512,1024]{1,0:T(8,128)(2,1)} collective-permute-done((bf16[512,1024]{1,0:T(8,128)(2,1)}, bf16[512,1024]{1,0:T(8,128)(2,1)}, u32[]{:S(2)}, u32[]{:S(2)}) %collective-permute-start.18) | collective-permute-done | bytes 1048608 | tf_op jit(solution)/shard_map/ppermute | solution.py:830
  432.1 16.2 %reduce-scatter.14.cloned.1.call-done = bf16[128,512]{1,0:T(8,128)(2,1)} async-done(((bf16[1024,512]{1,0:T(8,128)(2,1)}), bf16[128,512]{1,0:T(8,128)(2,1)}) %reduce-scatter.14.cloned.1.call-update) | async-done | bytes 131088 | tf_op jit(solution)/shard_map/reduce_scatter | solution.py:853
  460.3 8.0 %finish.1 = f32[512,2048]{1,0:T(8,128)} custom-call(s32[16]{0:T(128)} %copy-done.42, s32[2]{0:T(128)} %copy-done.41, bf16[512,2048]{1,0:T(8,128)(2,1)} %hidden_ref.3, bf16[512,2048]{1,0:T(8,128)(2,1)} %cot_ref.1, f32[1,2048]{1,0:T(1,128)} %bitcast.62, bf16[1024,1024]{1,0:T(8,128)(2,1)} %add_convert_fusion.5.refs_0_, ...), custom_call_target="tpu_custom_call" | custom-call | tf_op jit(solution)/shard_map/finish/pallas_call | solution.py:648
  (313 shorter events, 158.7 us)
Async XLA Ops:
  7.2 64.0 %copy-start.4 = (bf16[512,2048]{1,0:T(8,128)(2,1)S(1)}, bf16[512,2048]{1,0:T(8,128)(2,1)}, u32[]{:S(2)}) copy-start(bf16[512,2048]{1,0:T(8,128)(2,1)} %hidden_ref.3) | copy-start | bytes 6291460
  7.2 61.7 %all-gather.4.cloned.1.call-start = ((), (), s32[]{:S(2)}) async-start(), calls=%async_computation.5 | async-start | bytes 5603328 | tf_op jit(solution)/shard_map/all_gather | solution.py:838
  10.3 120.1 %all-gather.6.cloned.1.call-start = ((), (), s32[]{:S(2)}) async-start(), calls=%async_computation.6 | async-start | bytes 4718592 | tf_op jit(solution)/shard_map/all_gather | solution.py:838
  10.3 49.0 %collective-permute-start = (bf16[512,2048]{1,0:T(8,128)(2,1)}, bf16[512,2048]{1,0:T(8,128)(2,1)}, u32[]{:S(2)}, u32[]{:S(2)}) collective-permute-start(bf16[512,2048]{1,0:T(8,128)(2,1)} %hidden_ref.3), channel_id=1, source_target_pairs={{0,1},{1,0},{2,3},{3,2},{4,5},{5,4},{6,7},{7,6},{8,9},{9,8},{10,11... | collective-permute-start | bytes 6291464 | tf_op jit(solution)/shard_map/ppermute | solution.py:830
  16.7 1.2 collective-permute-start.1
  17.9 3.7 collective-permute-start.2
  21.6 3.8 collective-permute-start.3
  23.3 162.8 %all-gather.8.cloned.1.call-start = ((), (), s32[]{:S(2)}) async-start(), calls=%async_computation.7 | async-start | bytes 4718592 | tf_op jit(solution)/shard_map/all_gather | solution.py:838
  25.5 5.0 %collective-permute-start.4 = (bf16[8,896]{1,0:T(8,128)(2,1)S(1)}, bf16[8,896]{1,0:T(8,128)(2,1)S(1)}, u32[]{:S(2)}, u32[]{:S(2)}) collective-permute-start(bf16[8,896]{1,0:T(8,128)(2,1)S(1)} %pad_maximum_fusion.4), channel_id=1, source_target_pairs={{0,16},{2,18},{4,20},{6,22},{8,24},{10,26},{12,28},{14,30},{16,0},... | collective-permute-start | bytes 43016 | tf_op jit(solution)/shard_map/ppermute | solution.py:845
  68.9 15.5 %collective-permute-start.6 = (bf16[1024,2432]{1,0:T(8,128)(2,1)}, bf16[1024,2432]{1,0:T(8,128)(2,1)}, u32[]{:S(2)}, u32[]{:S(2)}) collective-permute-start(bf16[1024,2432]{1,0:T(8,128)(2,1)} %all-gather.4.cloned.1.call-done), channel_id=1, source_target_pairs={{0,2},{2,0},{4,6},{6,4},{8,10},{10,8},{12,14},{14,12},{16,18},{18,... | collective-permute-start | bytes 14942216 | tf_op jit(solution)/shard_map/ppermute | solution.py:826
  69.6 92.4 %copy-start.41 = (s32[2]{0:T(128)}, s32[2]{0:T(128)S(1)}, u32[]{:S(2)}) copy-start(s32[2]{0:T(128)S(1)} %pad_add_fusion.1.slots_ref) | copy-start | bytes 28
  69.7 92.3 %copy-start.42 = (s32[16]{0:T(128)}, s32[16]{0:T(128)S(1)}, u32[]{:S(2)}) copy-start(s32[16]{0:T(128)S(1)} %pad_add_fusion.lanes_ref) | copy-start | bytes 196
  69.7 59.3 %collective-permute-start.5 = (bf16[512,2048]{1,0:T(8,128)(2,1)}, bf16[512,2048]{1,0:T(8,128)(2,1)S(1)}, u32[]{:S(2)}, u32[]{:S(2)}) collective-permute-start(bf16[512,2048]{1,0:T(8,128)(2,1)} %cot_ref.1), channel_id=1, source_target_pairs={{0,1},{1,0},{2,3},{3,2},{4,5},{5,4},{6,7},{7,6},{8,9},{9,8},{10,11... | collective-permute-start | bytes 6291464 | tf_op jit(solution)/shard_map/ppermute | solution.py:830
  130.4 12.6 %collective-permute-start.7 = (bf16[1024,2048]{1,0:T(8,128)(2,1)}, bf16[1024,2048]{1,0:T(8,128)(2,1)}, u32[]{:S(2)}, u32[]{:S(2)}) collective-permute-start(bf16[1024,2048]{1,0:T(8,128)(2,1)} %all-gather.6.cloned.1.call-done), channel_id=1, source_target_pairs={{0,2},{2,0},{4,6},{6,4},{8,10},{10,8},{12,14},{14,12},{16,18},{18,... | collective-permute-start | bytes 12582920 | tf_op jit(solution)/shard_map/ppermute | solution.py:826
  131.7 178.5 %reduce-scatter.6.cloned.1.call-start = ((), (), s32[]{:S(2)}) async-start(), calls=%async_computation.8 | async-start | bytes 4718592 | tf_op jit(solution)/shard_map/reduce_scatter | solution.py:853
  158.1 3.7 collective-permute-start.8
  172.4 7.2 %collective-permute-start.9 = (bf16[1024,2048]{1,0:T(8,128)(2,1)S(1)}, bf16[1024,2048]{1,0:T(8,128)(2,1)S(1)}, u32[]{:S(2)}, u32[]{:S(2)}) collective-permute-start(bf16[1024,2048]{1,0:T(8,128)(2,1)S(1)} %convolution_convert_fusion.2), channel_id=1, source_target_pairs={{0,2},{2,0},{4,6},{6,4},{8,10},{10,8},{12,14},{14,12},{16,18},{18,... | collective-permute-start | bytes 12582920 | tf_op jit(solution)/shard_map/ppermute | solution.py:826
  186.1 8.1 %collective-permute-start.10 = (bf16[1024,2048]{1,0:T(8,128)(2,1)}, bf16[1024,2048]{1,0:T(8,128)(2,1)}, u32[]{:S(2)}, u32[]{:S(2)}) collective-permute-start(bf16[1024,2048]{1,0:T(8,128)(2,1)} %all-gather.8.cloned.1.call-done.own_ref), channel_id=1, source_target_pairs={{0,2},{2,0},{4,6},{6,4},{8,10},{10,8},{12,14},{14,12},{16,18},{18,... | collective-permute-start | bytes 12582920 | tf_op jit(solution)/shard_map/ppermute | solution.py:826
  186.3 124.0 %reduce-scatter.8.cloned.1.call-start = ((), (), s32[]{:S(2)}) async-start(), calls=%async_computation.9 | async-start | bytes 4718592 | tf_op jit(solution)/shard_map/reduce_scatter | solution.py:853
  203.2 3.6 collective-permute-start.11
  230.1 14.4 %collective-permute-start.12 = (bf16[1024,2048]{1,0:T(8,128)(2,1)S(1)}, bf16[1024,2048]{1,0:T(8,128)(2,1)S(1)}, u32[]{:S(2)}, u32[]{:S(2)}) collective-permute-start(bf16[1024,2048]{1,0:T(8,128)(2,1)S(1)} %convolution_convert_fusion.1), channel_id=1, source_target_pairs={{0,2},{2,0},{4,6},{6,4},{8,10},{10,8},{12,14},{14,12},{16,18},{18,... | collective-permute-start | bytes 12582920 | tf_op jit(solution)/shard_map/ppermute | solution.py:826
  250.7 137.4 %reduce-scatter.10.cloned.1.call-start = ((), (), s32[]{:S(2)}) async-start(), calls=%async_computation.10 | async-start | bytes 3538944 | tf_op jit(solution)/shard_map/reduce_scatter | solution.py:853
  254.0 56.2 %collective-permute-start.14 = (bf16[512,1024]{1,0:T(8,128)(2,1)S(1)}, bf16[512,1024]{1,0:T(8,128)(2,1)}, u32[]{:S(2)}, u32[]{:S(2)}) collective-permute-start(bf16[512,1024]{1,0:T(8,128)(2,1)S(1)} %constant_dynamic-slice_fusion.2), channel_id=1, source_target_pairs={{0,1},{1,0},{2,3},{3,2},{4,5},{5,4},{6,7},{7,6},{8,9},{9,8},{10,11... | collective-permute-start | bytes 3145736 | tf_op jit(solution)/shard_map/ppermute | solution.py:830
  254.9 55.2 %collective-permute-start.13 = (bf16[512,1024]{1,0:T(8,128)(2,1)S(1)}, bf16[512,1024]{1,0:T(8,128)(2,1)}, u32[]{:S(2)}, u32[]{:S(2)}) collective-permute-start(bf16[512,1024]{1,0:T(8,128)(2,1)S(1)} %constant_dynamic-slice_fusion.3), channel_id=1, source_target_pairs={{0,1},{1,0},{2,3},{3,2},{4,5},{5,4},{6,7},{7,6},{8,9},{9,8},{10,11... | collective-permute-start | bytes 3145736 | tf_op jit(solution)/shard_map/ppermute | solution.py:830
  316.4 14.3 %collective-permute-start.15 = (bf16[1024,1536]{1,0:T(8,128)(2,1)S(1)}, bf16[1024,1536]{1,0:T(8,128)(2,1)S(1)}, u32[]{:S(2)}, u32[]{:S(2)}) collective-permute-start(bf16[1024,1536]{1,0:T(8,128)(2,1)S(1)} %convolution_convert_fusion), channel_id=1, source_target_pairs={{0,2},{2,0},{4,6},{6,4},{8,10},{10,8},{12,14},{14,12},{16,18},{18,... | collective-permute-start | bytes 9437192 | tf_op jit(solution)/shard_map/ppermute | solution.py:826
  335.8 90.0 %reduce-scatter.12.cloned.1.call-start = ((), (), s32[]{:S(2)}) async-start(), calls=%async_computation.11 | async-start | bytes 1363968 | tf_op jit(solution)/shard_map/reduce_scatter | solution.py:853
  379.5 6.0 %collective-permute-start.16 = (f32[1024,295]{0,1:T(8,128)}, f32[1024,295]{0,1:T(8,128)}, u32[]{:S(2)}, u32[]{:S(2)}) collective-permute-start(f32[1024,295]{0,1:T(8,128)} %pad_maximum_fusion), channel_id=1, source_target_pairs={{0,2},{2,0},{4,6},{6,4},{8,10},{10,8},{12,14},{14,12},{16,18},{18,... | collective-permute-start | bytes 3624968 | tf_op jit(solution)/shard_map/ppermute | solution.py:826
  388.1 60.2 %reduce-scatter.14.cloned.1.call-start = ((), (), s32[]{:S(2)}) async-start(), calls=%async_computation.12 | async-start | bytes 1179648 | tf_op jit(solution)/shard_map/reduce_scatter | solution.py:853
  388.4 6.8 %collective-permute-start.17 = (bf16[1024,512]{1,0:T(8,128)(2,1)}, bf16[1024,512]{1,0:T(8,128)(2,1)S(1)}, u32[]{:S(2)}, u32[]{:S(2)}) collective-permute-start(bf16[1024,512]{1,0:T(8,128)(2,1)} %fusion.41), channel_id=1, source_target_pairs={{0,2},{2,0},{4,6},{6,4},{8,10},{10,8},{12,14},{14,12},{16,18},{18,... | collective-permute-start | bytes 3145736 | tf_op jit(solution)/shard_map/ppermute | solution.py:826
  399.7 26.0 %collective-permute-start.18 = (bf16[512,1024]{1,0:T(8,128)(2,1)}, bf16[512,1024]{1,0:T(8,128)(2,1)}, u32[]{:S(2)}, u32[]{:S(2)}) collective-permute-start(bf16[512,1024]{1,0:T(8,128)(2,1)} %constant_dynamic-slice_fusion.1), channel_id=1, source_target_pairs={{0,1},{1,0},{2,3},{3,2},{4,5},{5,4},{6,7},{7,6},{8,9},{9,8},{10,11... | collective-permute-start | bytes 3145736 | tf_op jit(solution)/shard_map/ppermute | solution.py:830
  431.1 26.4 %collective-permute-start.19 = (bf16[512,1024]{1,0:T(8,128)(2,1)}, bf16[512,1024]{1,0:T(8,128)(2,1)}, u32[]{:S(2)}, u32[]{:S(2)}) collective-permute-start(bf16[512,1024]{1,0:T(8,128)(2,1)} %constant_dynamic-slice_fusion), channel_id=1, source_target_pairs={{0,1},{1,0},{2,3},{3,2},{4,5},{5,4},{6,7},{7,6},{8,9},{9,8},{10,11... | collective-permute-start | bytes 3145736 | tf_op jit(solution)/shard_map/ppermute | solution.py:830
  458.2 10.1 %collective-permute-start.20 = (f32[32960]{0:T(1024)S(1)}, f32[32960]{0:T(1024)S(1)}, u32[]{:S(2)}, u32[]{:S(2)}) collective-permute-start(f32[32960]{0:T(1024)S(1)} %concatenate.55), channel_id=1, source_target_pairs={{0,1},{1,0},{2,3},{3,2},{4,5},{5,4},{6,7},{7,6},{8,9},{9,8},{10,11... | collective-permute-start | bytes 395528 | tf_op jit(solution)/shard_map/ppermute | solution.py:830
  (62 other events, 741.2 us)
Sparse Core Ops, SparseCore 0:
  10.4 58.4 all-gather.3
  70.4 47.9 all-gather.5
  131.8 47.3 all-gather.7
  186.4 47.9 reduce-scatter.5
  250.8 48.0 reduce-scatter.7
  335.9 38.7 reduce-scatter.9
  388.2 29.4 reduce-scatter.11
  420.0 28.2 reduce-scatter.13
